TPU v7x, 512 devices: a whole 4x8x8 slice. The times are simulated.
512 devices in a mesh: grp: 16 (over y_hi, x, core), hist: 32 (over z, y_lo).
Axes of the slice: x: 4, y: 8 (y_hi: 2, y_lo: 4; y = y_hi * 4 + y_lo), z: 8, core: 2. Of those that a mesh axis runs over, the one named last changes fastest.
Arguments:
- cand_x: bfloat16 [512, 32, 1024], P('grp', 'hist'), may hold values from -10 to 10
- hist_kv: bfloat16 [32, 16384, 2048], P(None, 'hist', 'grp'), may hold values from -12 to 12
- hist_len: int32 [32], P('hist'), may hold values from 2048 to 16384, as said below
- cand_count: int32 [32], P('hist'), may hold values from 256 to 512, as said below
- block_mask: int32 [32, 128], P('hist'), may hold values 0 or 1
- w_proj: bfloat16 [1024, 2048], P(None, 'grp'), may hold values from -0.1875 to 0.1875
- w_out: bfloat16 [1024, 1024], P('grp'), may hold values from -0.1875 to 0.1875
Outputs:
- mixed: bfloat16 [512, 32, 1024], P('grp', 'hist')
Inputs may be any that keep to these rules, and one draw needn't show every extreme that they name: `hist_len`: the number of live positions of each user's history; positions at or past it are padding. In every draw one user has all 16384 and one has 2048. `cand_count`: the number of real candidates of each user; slots at or past it are padding. In every draw one user has 512 and one has 256. `block_mask`: 1 keeps a block of 128 history positions, 0 drops it.
All inputs are finite; a program needn't handle non-finite values.
Results may differ from a plain program's by a relative error of at most 0.015.
Values may be sent and summed in bfloat16 or wider, within the bound.
No kernel may reach another device: no remote copies, remote signals or barrier semaphores. Data moves between devices by JAX's collectives and lax.ppermute only.
A program may use at most 64 MiB of HBM per device.

v0:
```python
import math

import jax
import jax.numpy as jnp
from jax import lax
from jax.sharding import PartitionSpec as P

D = 1024
HEADS = 16
BLK = 128


def layer_norm(values):
    average = jnp.mean(values, axis=-1, keepdims=True)
    centred = values - average
    spread = jnp.mean(centred * centred, axis=-1, keepdims=True)
    return centred * lax.rsqrt(spread + 1e-05)


def project_rows(normed, weights):
    product = jnp.einsum("cud,dk->cuk", normed, weights, preferred_element_type=jnp.float32)
    return jax.nn.silu(product).astype(jnp.bfloat16)


def attend_user(queries, user_kv, length, mask_row, heads_here, head_dim):
    hist_rows = user_kv.shape[0]
    key_block = math.gcd(hist_rows, 512)
    blocks = hist_rows // key_block
    kv_blocks = user_kv.reshape(blocks, key_block, heads_here, 2, head_dim)
    positions = jnp.arange(hist_rows, dtype=jnp.int32).reshape(blocks, key_block)
    live_keys = (positions < length) & (jnp.repeat(mask_row, BLK).reshape(blocks, key_block) == 1)
    score_scale = head_dim ** (-0.5)

    def add_block(running, operand_pair):
        kv_block, live_block = operand_pair
        scores = (
            jnp.einsum(
                "chd,khd->hck", queries, kv_block[:, :, 0, :], preferred_element_type=jnp.float32
            )
            * score_scale
        )
        weights = jnp.where(live_block[None, None, :], jax.nn.silu(scores), 0.0).astype(
            jnp.bfloat16
        )
        running = running + jnp.einsum(
            "hck,khd->chd", weights, kv_block[:, :, 1, :], preferred_element_type=jnp.float32
        )
        return (running, None)

    start_value = jnp.zeros((queries.shape[0], heads_here, head_dim), jnp.float32)
    running, _ = lax.scan(add_block, start_value, (kv_blocks, live_keys))
    return running


def per_device(cand_x, hist_kv, hist_len, cand_count, block_mask, w_proj, w_out):
    head_dim = D // HEADS
    heads_here = w_out.shape[0] // head_dim
    own_rows = cand_x.shape[0]
    local_users = cand_x.shape[1]
    inputs = cand_x.astype(jnp.float32)
    normed = layer_norm(inputs).astype(jnp.bfloat16)
    head_cols = project_rows(lax.all_gather(normed, "grp", axis=0, tiled=True), w_proj)
    all_rows = head_cols.shape[0]
    head_cols = head_cols.reshape(all_rows, local_users, heads_here, 2, head_dim)
    queries = head_cols[:, :, :, 0, :]
    gate_part = head_cols[:, :, :, 1, :].reshape(all_rows, local_users, heads_here * head_dim)
    histories = lax.all_to_all(hist_kv, "hist", split_axis=0, concat_axis=1, tiled=True)
    attended = jnp.stack(
        [
            attend_user(
                queries[:, 0], histories[0], hist_len[0], block_mask[0], heads_here, head_dim
            )
        ],
        axis=1,
    )
    attended = attended.reshape(all_rows, local_users, heads_here * head_dim)
    row_sum = jnp.sum(attended, axis=-1)
    row_square = jnp.sum(attended * attended, axis=-1)
    total_sum, total_square = lax.psum((row_sum, row_square), "grp")
    average = total_sum / D
    spread = total_square / D - average * average
    centred = (attended - average[..., None]) * lax.rsqrt(spread + 1e-05)[..., None]
    gated = (centred * gate_part.astype(jnp.float32)).astype(jnp.bfloat16)
    branch = lax.psum_scatter(
        jnp.einsum("cuk,ke->cue", gated, w_out, preferred_element_type=jnp.float32).astype(
            jnp.bfloat16
        ),
        "grp",
        scatter_dimension=0,
        tiled=True,
    ).astype(jnp.float32)
    mixed_out = inputs + branch
    row_index = lax.axis_index("grp") * own_rows + jnp.arange(own_rows, dtype=jnp.int32)
    keep_rows = row_index[:, None] < cand_count[None, :]
    return jnp.where(keep_rows[:, :, None], mixed_out, 0.0).astype(jnp.bfloat16)


def solution(mesh):
    in_specs = (
        P("grp", "hist", None),
        P(None, "hist", "grp"),
        P("hist"),
        P("hist"),
        P("hist", None),
        P(None, "grp"),
        P("grp", None),
    )
    out_specs = P("grp", "hist", None)
    return jax.shard_map(
        per_device, mesh=mesh, in_specs=in_specs, out_specs=out_specs, check_vma=False
    )
```

profile of v0, /device:TPU:2, one launch (start us, length us, event | category | flops | bytes accessed | tf_op | source)
XLA Modules:
  0.0 344.5 jit_solution(11277703794724817701)
XLA Ops:
  6.5 6.6 %copy.9 = bf16[32,512,128]{1,2,0:T(8,128)(2,1)} copy(bf16[32,512,128]{2,1,0:T(8,128)(2,1)} %param.10) | data formatting | bytes 8388608 | tf_op args[1]
  13.1 14.0 %all-to-all-start = ((bf16[32,512,128]{1,2,0:T(8,128)(2,1)}), bf16[32,512,128]{1,2,0:T(8,128)(2,1)}, u32[]{:S(2)}, u32[]{:S(2)}) async-start(bf16[32,512,128]{1,2,0:T(8,128)(2,1)} %copy.9), calls=%async_computation | async-start | bytes 8388608 | tf_op jit(solution)/shard_map/all_to_all | solution.py:67
  27.5 0.7 fusion.19
  29.3 64.4 %all-gather.2.cloned.1.call-done = bf16[512,1,1024]{2,0,1:T(8,128)(2,1)} async-done(((bf16[32,1,1024]{2,0,1:T(8,128)(2,1)}), bf16[512,1,1024]{2,0,1:T(8,128)(2,1)}) %all-gather.2.cloned.1.call-update) | async-done | bytes 1048592 | tf_op jit(solution)/shard_map/all_gather | solution.py:62
  93.7 1.7 multiply_convert_fusion
  95.4 50.8 %all-to-all-done = bf16[32,512,128]{1,2,0:T(8,128)(2,1)} async-done(((bf16[32,512,128]{1,2,0:T(8,128)(2,1)}), bf16[32,512,128]{1,2,0:T(8,128)(2,1)}, u32[]{:S(2)}, u32[]{:S(2)}) %all-to-all-start) | async-done | bytes 4194336 | tf_op jit(solution)/shard_map/all_to_all | solution.py:67
  146.3 52.0 %while.11 = (s32[]{:T(128)}, f32[512,1,64]{0,2,1:T(8,128)S(1)}, bf16[32,512,1,2,64]{1,4,3,2,0:T(8,128)(2,1)}, pred[32,512]{1,0:T(8,128)(4,1)S(1)}, bf16[512,1,64]{0,2,1:T(8,128)(2,1)S(1)}, /*index=5*/s32[]{:T(128)}, s32[]{:T(128)}) while((s32[]{:T(128)}, f32[512,1,64]{0,2,1:T(8,128)S(1)}, bf16[32,512,1,2,64]{1,4,3,2,0:T(8,128)(2,1)}, ...), condition=%wide.region_3.4_spmd.clone, body=%wide.region_2.3_spmd.clone.sunk | while | flops 69009408 | bytes 722535 | solution.py:51
  146.3 0.9 dynamic-slice_bitcast_fusion.2
  148.0 0.9 dynamic-slice_bitcast_fusion.2
  149.6 0.9 dynamic-slice_bitcast_fusion.2
  151.2 0.9 dynamic-slice_bitcast_fusion.2
  152.8 0.9 dynamic-slice_bitcast_fusion.2
  154.5 0.9 dynamic-slice_bitcast_fusion.2
  156.1 0.9 dynamic-slice_bitcast_fusion.2
  157.0 0.7 fusion.34
  157.7 0.9 dynamic-slice_bitcast_fusion.2
  158.6 0.7 fusion.34
  159.3 0.9 dynamic-slice_bitcast_fusion.2
  161.0 0.9 dynamic-slice_bitcast_fusion.2
  162.6 0.9 dynamic-slice_bitcast_fusion.2
  164.2 0.9 dynamic-slice_bitcast_fusion.2
  165.8 0.9 dynamic-slice_bitcast_fusion.2
  166.8 0.7 fusion.34
  167.5 0.9 dynamic-slice_bitcast_fusion.2
  168.4 0.7 fusion.34
  169.1 0.9 dynamic-slice_bitcast_fusion.2
  170.7 0.9 dynamic-slice_bitcast_fusion.2
  172.3 0.9 dynamic-slice_bitcast_fusion.2
  174.0 0.9 dynamic-slice_bitcast_fusion.2
  175.6 0.9 dynamic-slice_bitcast_fusion.2
  176.5 0.7 fusion.34
  177.2 0.9 dynamic-slice_bitcast_fusion.2
  178.8 0.9 dynamic-slice_bitcast_fusion.2
  180.5 0.9 dynamic-slice_bitcast_fusion.2
  182.1 0.9 dynamic-slice_bitcast_fusion.2
  183.7 0.9 dynamic-slice_bitcast_fusion.2
  185.3 0.9 dynamic-slice_bitcast_fusion.2
  187.0 0.9 dynamic-slice_bitcast_fusion.2
  188.6 0.9 dynamic-slice_bitcast_fusion.2
  190.2 0.9 dynamic-slice_bitcast_fusion.2
  191.8 0.9 dynamic-slice_bitcast_fusion.2
  193.5 0.9 dynamic-slice_bitcast_fusion.2
  195.1 0.9 dynamic-slice_bitcast_fusion.2
  196.7 0.9 dynamic-slice_bitcast_fusion.2
  198.4 34.6 %all-reduce = (f32[512,1]{0,1:T(1,128)S(1)}, f32[512,1]{0,1:T(1,128)S(1)}) all-reduce(f32[512,1]{0,1:T(1,128)S(1)} %bitcast.76, f32[512,1]{0,1:T(1,128)S(1)} %bitcast.75), channel_id=1, replica_groups=mesh['grp'=16,'hist'=32] {'grp'}, use_global_device_ids=true, to_apply=%region_7.8 | all-reduce | flops 1024 | bytes 8192 | tf_op jit(solution)/shard_map/psum | solution.py:79
  233.0 1.5 fusion.11
  235.1 101.0 %reduce-scatter.2.cloned.1.call-done = bf16[32,1,1024]{2,0,1:T(8,128)(2,1)} async-done(((bf16[512,1,1024]{2,0,1:T(8,128)(2,1)}), bf16[32,1,1024]{2,0,1:T(8,128)(2,1)}) %reduce-scatter.2.cloned.1.call-update) | async-done | bytes 65552 | tf_op jit(solution)/shard_map/reduce_scatter | solution.py:84
  336.1 1.5 fusion.21
  (84 shorter events, 19.2 us)
Async XLA Ops:
  6.5 87.1 %copy-start = (bf16[1024,128]{1,0:T(8,128)(2,1)S(1)}, bf16[1024,128]{1,0:T(8,128)(2,1)}, u32[]{:S(2)}) copy-start(bf16[1024,128]{1,0:T(8,128)(2,1)} %param.14) | copy-start | bytes 786436
  13.1 14.1 %copy-start.1 = (bf16[32,1,1024]{2,0,1:T(8,128)(2,1)S(1)}, bf16[32,1,1024]{2,0,1:T(8,128)(2,1)}, u32[]{:S(2)}) copy-start(bf16[32,1,1024]{2,0,1:T(8,128)(2,1)} %param.9) | copy-start | bytes 196612
  13.1 15.2 %copy-start.3 = (s32[1,128]{1,0:T(1,128)S(1)}, s32[1,128]{1,0:T(1,128)}, u32[]{:S(2)}) copy-start(s32[1,128]{1,0:T(1,128)} %param.13) | copy-start | bytes 1540
  13.1 133.2 %all-to-all-start = ((bf16[32,512,128]{1,2,0:T(8,128)(2,1)}), bf16[32,512,128]{1,2,0:T(8,128)(2,1)}, u32[]{:S(2)}, u32[]{:S(2)}) async-start(bf16[32,512,128]{1,2,0:T(8,128)(2,1)} %copy.9), calls=%async_computation | async-start | bytes 8388608 | tf_op jit(solution)/shard_map/all_to_all | solution.py:67
  27.1 66.5 %all-gather.2.cloned.1.call-start = ((), (), s32[]{:S(2)}) async-start(), calls=%async_computation.2 | async-start | bytes 1114112 | tf_op jit(solution)/shard_map/all_gather | solution.py:62
  28.3 307.8 %reduce-scatter.2.cloned.1.call-start = ((), (), s32[]{:S(2)}) async-start(), calls=%async_computation.3 | async-start | bytes 1114112 | tf_op jit(solution)/shard_map/reduce_scatter | solution.py:84
  146.3 86.7 %copy-start.2 = (bf16[64,1024]{1,0:T(8,128)(2,1)S(1)}, bf16[64,1024]{1,0:T(8,128)(2,1)}, u32[]{:S(2)}) copy-start(bf16[64,1024]{1,0:T(8,128)(2,1)} %param.15) | copy-start | bytes 393220
Sparse Core Ops, SparseCore 0:
  31.3 62.3 all-gather.1
  234.6 101.4 reduce-scatter.1
where the time goes:
time: 345 us; the launch traced here: 344 us
  waiting for transfers between devices  216 us (63%)
  local copies, waits for them, and re-layouts  37 us (11%)
  blocking collectives  34.6 us (10%)
  matrix products  24 us (7%)
  between operations  14.8 us (4%)
  starting transfers between devices  14.1 us (4%)
    reduce_scatter x1, waiting for transfers between devices, per_device(): lax.psum_scatter(jnp.einsum('cuk,ke->cue', gated, w_out, preferred_elemen...  101 us
    all_gather x1, waiting for transfers between devices, per_device(): lax.all_gather(normed, 'grp', axis=0, tiled=True)  64.4 us
    all_to_all x1, waiting for transfers between devices, per_device(): lax.all_to_all(hist_kv, 'hist', split_axis=0, concat_axis=1, tiled=True)  50.8 us
    psum x1, blocking collectives, per_device(): total_sum, total_square = lax.psum((row_sum, row_square), 'grp')  34.6 us
    squeeze x32, local copies, waits for them, and re-layouts, attend_user(): running, _ = lax.scan(add_block, start_value, (kv_blocks, live_keys))  29.3 us
    dot_general x32, matrix products, add_block(): jnp.einsum('hck,khd->chd', weights, kv_block[:, :, 1, :], preferred_eleme...  20.8 us
    all_to_all x1, starting transfers between devices, per_device(): lax.all_to_all(hist_kv, 'hist', split_axis=0, concat_axis=1, tiled=True)  14 us
  transfers between devices with their start and end apart: 3, of which 3 were waited for; matrix products, arithmetic and copies ran while one was open for 1% of the time, Pallas kernels for 0%

commit v1 on v0

v1 whole, which is shorter than its diff:
```python
import functools

import jax
import jax.numpy as jnp
from jax import lax
from jax.experimental import pallas as pl
from jax.experimental.pallas import tpu as pltpu
from jax.sharding import PartitionSpec as P

D = 1024
BLK = 128
TILE = 256
HALF = 64
VMEM_LIMIT = 48 * 1024 * 1024


def layer_norm(values):
    average = jnp.mean(values, axis=-1, keepdims=True)
    centred = values - average
    spread = jnp.mean(centred * centred, axis=-1, keepdims=True)
    return centred * lax.rsqrt(spread + 1e-05)


def low_lanes(shape):
    return lax.broadcasted_iota(jnp.int32, shape, len(shape) - 1) < HALF


def project_kernel(rows_ref, w_ref, query_ref, gate_ref):
    product = jnp.dot(rows_ref[...], w_ref[...], preferred_element_type=jnp.float32)
    values = (product / (1.0 + jnp.exp(-product))).astype(jnp.bfloat16).astype(jnp.float32)
    query_ref[...] = jnp.where(low_lanes(values.shape), values * (0.5 * HALF ** (-0.5)), 0.0).astype(jnp.bfloat16)
    slices = values.reshape(values.shape[0] // 32, 2, 16, 128)
    first, second = slices[:, 0], slices[:, 1]
    turned = pltpu.roll(first.reshape(-1, 128), HALF, 1).reshape(first.shape)
    gate_ref[...] = jnp.where(low_lanes(first.shape), turned, second).astype(jnp.bfloat16)


def project(rows, w_proj):
    count = rows.shape[0]
    return pl.pallas_call(
        project_kernel,
        out_shape=(
            jax.ShapeDtypeStruct((count, 128), jnp.bfloat16),
            jax.ShapeDtypeStruct((count // 32, 16, 128), jnp.bfloat16),
        ),
        compiler_params=pltpu.CompilerParams(vmem_limit_bytes=VMEM_LIMIT),
        cost_estimate=pl.CostEstimate(flops=2 * count * D * 128, bytes_accessed=1 << 20, transcendentals=0),
    )(rows, w_proj)


def attend_tile(query, kv, live_first, live_second):
    scores = lax.dot_general(query, kv, (((1,), (1,)), ((), ())), preferred_element_type=jnp.float32)
    weights = (scores + scores * jnp.tanh(scores)).astype(jnp.bfloat16)
    row = lax.broadcasted_iota(jnp.int32, kv.shape, 0)
    live = row < jnp.where(row < BLK, live_first, live_second + BLK)
    values = jnp.where(live, kv, jnp.zeros_like(kv))
    return jnp.dot(weights, values, preferred_element_type=jnp.float32)


def attend_kernel(tiles, live_ref, query_ref, gate_ref, kv_ref, out_ref, total):
    step = pl.program_id(0)

    @pl.when(step == 0)
    def _():
        total[...] = jnp.zeros_like(total)

    for tile in range(tiles):
        block = (step * tiles + tile) * 2
        live_first, live_second = live_ref[block], live_ref[block + 1]

        @pl.when(live_first + live_second > 0)
        def _():
            kv = kv_ref[pl.ds(tile * TILE, TILE), :]
            total[...] += attend_tile(query_ref[...], kv, live_first, live_second)

    @pl.when(step == pl.num_programs(0) - 1)
    def _():
        slices = total[...].reshape(out_ref.shape[0], 2, 16, 128)
        first, second = slices[:, 0], slices[:, 1]
        turned = pltpu.roll(first.reshape(-1, 128), HALF, 1).reshape(first.shape)
        out_ref[:, 0:16, :] = jnp.where(low_lanes(first.shape), turned, second).astype(jnp.bfloat16)
        out_ref[:, 16:32, :] = gate_ref[...]


def attend(live, query, gate, kv):
    count = query.shape[0]
    positions = kv.shape[0]
    tiles = 4
    steps = positions // (tiles * TILE)
    return pl.pallas_call(
        functools.partial(attend_kernel, tiles),
        out_shape=jax.ShapeDtypeStruct((count // 32, 32, 128), jnp.bfloat16),
        grid=(steps,),
        in_specs=[
            pl.BlockSpec(memory_space=pltpu.SMEM),
            pl.BlockSpec((count, 128), lambda i: (0, 0)),
            pl.BlockSpec((count // 32, 16, 128), lambda i: (0, 0, 0)),
            pl.BlockSpec((tiles * TILE, 128), lambda i: (i, 0)),
        ],
        out_specs=pl.BlockSpec((count // 32, 32, 128), lambda i: (0, 0, 0)),
        scratch_shapes=[pltpu.VMEM((count, 128), jnp.float32)],
        compiler_params=pltpu.CompilerParams(vmem_limit_bytes=VMEM_LIMIT),
        cost_estimate=pl.CostEstimate(flops=4 * count * positions * 128, bytes_accessed=4 << 20, transcendentals=count * positions),
    )(live, query, gate, kv)


def spread_heads(packed):
    columns = []
    for pair in range(packed.shape[0] // 2):
        even, odd = packed[2 * pair], packed[2 * pair + 1]
        low = low_lanes(even.shape)
        top = jnp.where(low, even, pltpu.roll(odd, HALF, 1))
        bottom = jnp.where(low, pltpu.roll(even, HALF, 1), odd)
        columns.append(jnp.concatenate([top, bottom], axis=0))
    return jnp.concatenate(columns, axis=1)


def output_kernel(count_ref, parts_ref, w_ref, x_ref, out_ref):
    attended = spread_heads(parts_ref[:, 0:16, :].astype(jnp.float32))
    gate = spread_heads(parts_ref[:, 16:32, :].astype(jnp.float32))
    gated = (layer_norm(attended) * gate).astype(jnp.bfloat16)
    branch = jnp.dot(gated, w_ref[...], preferred_element_type=jnp.float32)
    mixed = x_ref[...].astype(jnp.float32) + branch
    row = lax.broadcasted_iota(jnp.int32, mixed.shape, 0)
    out_ref[...] = jnp.where(row < count_ref[0], mixed, 0.0).astype(jnp.bfloat16)


def output(keep, parts, w_out, rows):
    return pl.pallas_call(
        output_kernel,
        out_shape=jax.ShapeDtypeStruct(rows.shape, jnp.bfloat16),
        in_specs=[
            pl.BlockSpec(memory_space=pltpu.SMEM),
            pl.BlockSpec(memory_space=pltpu.VMEM),
            pl.BlockSpec(memory_space=pltpu.VMEM),
            pl.BlockSpec(memory_space=pltpu.VMEM),
        ],
        out_specs=pl.BlockSpec(memory_space=pltpu.VMEM),
        compiler_params=pltpu.CompilerParams(vmem_limit_bytes=VMEM_LIMIT),
        cost_estimate=pl.CostEstimate(flops=2 * 32 * D * D, bytes_accessed=3 << 20, transcendentals=0),
    )(keep, parts, w_out, rows)


def per_device(cand_x, hist_kv, hist_len, cand_count, block_mask, w_proj, w_out):
    own_rows = cand_x.shape[0]
    rows = cand_x.reshape(own_rows, D)
    histories = lax.all_to_all(hist_kv, "hist", split_axis=0, concat_axis=0, tiled=True)
    normed = layer_norm(rows.astype(jnp.float32)).astype(jnp.bfloat16)
    all_rows = lax.all_gather(normed, "grp", axis=0, tiled=True)
    w_out, all_rows = lax.optimization_barrier((w_out, all_rows))
    w_full = lax.all_gather(w_out, "grp", axis=0, tiled=True)
    query, gate = project(all_rows, w_proj)
    starts = jnp.arange(block_mask.shape[1], dtype=jnp.int32) * BLK
    live = jnp.clip(hist_len[0] - starts, 0, BLK) * block_mask[0]
    attended = attend(live, query, gate, histories.reshape(-1, 128))
    parts = lax.all_to_all(attended, "grp", split_axis=0, concat_axis=0, tiled=True)
    keep = cand_count - lax.axis_index("grp") * own_rows
    return output(keep, parts, w_full, rows).reshape(cand_x.shape)


def solution(mesh):
    in_specs = (
        P("grp", "hist", None),
        P(None, "hist", "grp"),
        P("hist"),
        P("hist"),
        P("hist", None),
        P(None, "grp"),
        P("grp", None),
    )
    out_specs = P("grp", "hist", None)
    return jax.shard_map(per_device, mesh=mesh, in_specs=in_specs, out_specs=out_specs, check_vma=False)
```

time: 345 us -> 206 us (0.60)
  the two profiles are of different devices: /device:TPU:2 before, /device:TPU:193 now
where the time goes in v1:
time: 206 us; the launch traced here: 205 us
  waiting for transfers between devices  114 us (55%)
  starting transfers between devices  42.5 us (21%)
  Pallas kernels  30.4 us (15%)
  between operations  14.8 us (7%)
  local copies, waits for them, and re-layouts  2.82 us (1%)
    all_gather x1, waiting for transfers between devices, per_device(): all_rows = lax.all_gather(normed, 'grp', axis=0, tiled=True)  65.8 us
    all_to_all x1, waiting for transfers between devices, per_device(): lax.all_to_all(hist_kv, 'hist', split_axis=0, concat_axis=0, tiled=True)  38.7 us
    all_to_all x1, starting transfers between devices, per_device(): lax.all_to_all(attended, 'grp', split_axis=0, concat_axis=0, tiled=True)  31.4 us
    pallas_call x1, Pallas kernels, attend(): pl.pallas_call(functools.partial(attend_kernel, tiles), out_shape=jax.Sha...  28.6 us
    all_to_all x1, starting transfers between devices, per_device(): lax.all_to_all(hist_kv, 'hist', split_axis=0, concat_axis=0, tiled=True)  11 us
    all_to_all x1, waiting for transfers between devices, per_device(): lax.all_to_all(attended, 'grp', split_axis=0, concat_axis=0, tiled=True)  9.37 us
  transfers between devices with their start and end apart: 4, of which 3 were waited for; matrix products, arithmetic and copies ran while one was open for 1% of the time, Pallas kernels for 14%

profile of v1, /device:TPU:193, one launch (start us, length us, event | category | flops | bytes accessed | tf_op | source)
XLA Modules:
  0.0 205.5 jit_solution(1369961113053364532)
XLA Ops:
  6.5 0.0 copy-start.2
  6.5 0.0 copy-start.4
  6.5 0.0 copy-start.3
  6.5 11.0 %all-to-all-start = ((bf16[32,512,128]{2,1,0:T(8,128)(2,1)}), bf16[32,512,128]{2,1,0:T(8,128)(2,1)}, u32[]{:S(2)}, u32[]{:S(2)}) async-start(bf16[32,512,128]{2,1,0:T(8,128)(2,1)} %param.8), calls=%async_computation | async-start | bytes 8388608 | tf_op jit(solution)/shard_map/all_to_all | solution.py:147
  17.5 0.0 all-gather.3.cloned.1.call-start
  17.6 0.0 copy-done.2
  17.6 0.1 convert_reduce_fusion
  17.7 0.2 fusion.2
  17.9 0.7 fusion.3
  18.6 0.0 all-gather.3.cloned.1.call-update
  18.7 0.0 all-gather.5.cloned.1.call-start
  18.7 65.8 %all-gather.3.cloned.1.call-done.rows_ref = bf16[512,1024]{1,0:T(8,128)(2,1)} async-done(((bf16[32,1024]{1,0:T(8,128)(2,1)}), bf16[512,1024]{1,0:T(8,128)(2,1)}) %all-gather.3.cloned.1.call-update) | async-done | bytes 1048592 | tf_op jit(solution)/shard_map/all_gather | solution.py:149
  84.6 0.0 all-gather.5.cloned.1.call-update
  85.2 0.0 copy-done.4
  85.3 0.0 copy-done.3
  85.3 0.0 copy-start.1
  85.3 1.2 copy-done.1
  86.5 0.5 shard_map.73
  87.0 38.7 %all-to-all-done = bf16[32,512,128]{2,1,0:T(8,128)(2,1)} async-done(((bf16[32,512,128]{2,1,0:T(8,128)(2,1)}), bf16[32,512,128]{2,1,0:T(8,128)(2,1)}, u32[]{:S(2)}, u32[]{:S(2)}) %all-to-all-start) | async-done | bytes 4194336 | tf_op jit(solution)/shard_map/all_to_all | solution.py:147
  125.7 28.6 %shard_map.74 = bf16[16,32,128]{2,1,0:T(8,128)(2,1)} custom-call(s32[128]{0:T(128)S(1)} %bitcast_multiply_fusion.live_ref, bf16[512,128]{1,0:T(8,128)(2,1)S(1)} %get-tuple-element.10.query_ref, bf16[16,16,128]{2,1,0:T(8,128)(2,1)S(1)} %get-tuple-element.11.gate_ref, bf16[16384,128]{1,0:T(8,128)(2,1)} %bitcast.4.kv_ref), custom_call_target="tpu_custom_call" | custom-call | flops 4294967296 | bytes 4194304 | tf_op jit(solution)/shard_map/pallas_call | solution.py:90
  154.2 31.4 %all-to-all-start.1 = ((bf16[16,32,128]{2,1,0:T(8,128)(2,1)}), bf16[16,32,128]{2,1,0:T(8,128)(2,1)S(1)}, u32[]{:S(2)}, u32[]{:S(2)}) async-start(bf16[16,32,128]{2,1,0:T(8,128)(2,1)} %shard_map.74), calls=%async_computation.1 | async-start | bytes 262144 | tf_op jit(solution)/shard_map/all_to_all | solution.py:156
  186.3 0.0 all-gather.5.cloned.1.call-done.w_ref
  186.3 9.4 %all-to-all-done.1.parts_ref = bf16[16,32,128]{2,1,0:T(8,128)(2,1)S(1)} async-done(((bf16[16,32,128]{2,1,0:T(8,128)(2,1)}), bf16[16,32,128]{2,1,0:T(8,128)(2,1)S(1)}, u32[]{:S(2)}, u32[]{:S(2)}) %all-to-all-start.1) | async-done | bytes 131104 | tf_op jit(solution)/shard_map/all_to_all | solution.py:156
  195.7 0.0 copy-start
  195.7 1.6 copy-done
  197.3 1.3 shard_map.75
  (3 shorter events, 0.0 us)
Async XLA Ops:
  6.5 11.0 %copy-start.2 = (bf16[32,1,1024]{2,0,1:T(8,128)(2,1)S(1)}, bf16[32,1,1024]{2,0,1:T(8,128)(2,1)}, u32[]{:S(2)}) copy-start(bf16[32,1,1024]{2,0,1:T(8,128)(2,1)} %param.7) | copy-start | bytes 196612
  6.5 78.7 %copy-start.4 = (s32[1,128]{1,0:T(1,128)S(1)}, s32[1,128]{1,0:T(1,128)}, u32[]{:S(2)}) copy-start(s32[1,128]{1,0:T(1,128)} %param.11) | copy-start | bytes 1540
  6.5 78.7 %copy-start.3 = (bf16[1024,128]{1,0:T(8,128)(2,1)S(1)}, bf16[1024,128]{1,0:T(8,128)(2,1)}, u32[]{:S(2)}) copy-start(bf16[1024,128]{1,0:T(8,128)(2,1)} %w_ref.1) | copy-start | bytes 786436
  6.5 119.1 %all-to-all-start = ((bf16[32,512,128]{2,1,0:T(8,128)(2,1)}), bf16[32,512,128]{2,1,0:T(8,128)(2,1)}, u32[]{:S(2)}, u32[]{:S(2)}) async-start(bf16[32,512,128]{2,1,0:T(8,128)(2,1)} %param.8), calls=%async_computation | async-start | bytes 8388608 | tf_op jit(solution)/shard_map/all_to_all | solution.py:147
  17.5 67.0 %all-gather.3.cloned.1.call-start = ((), (), s32[]{:S(2)}) async-start(), calls=%async_computation.2 | async-start | bytes 1114112 | tf_op jit(solution)/shard_map/all_gather | solution.py:149
  18.7 167.7 %all-gather.5.cloned.1.call-start = ((), (), s32[]{:S(2)}) async-start(), calls=%async_computation.3 | async-start | bytes 2228224 | tf_op jit(solution)/shard_map/all_gather | solution.py:151
  85.3 1.2 copy-start.1
  154.2 41.5 %all-to-all-start.1 = ((bf16[16,32,128]{2,1,0:T(8,128)(2,1)}), bf16[16,32,128]{2,1,0:T(8,128)(2,1)S(1)}, u32[]{:S(2)}, u32[]{:S(2)}) async-start(bf16[16,32,128]{2,1,0:T(8,128)(2,1)} %shard_map.74), calls=%async_computation.1 | async-start | bytes 262144 | tf_op jit(solution)/shard_map/all_to_all | solution.py:156
  195.7 1.6 copy-start
Sparse Core Ops, SparseCore 0:
  21.7 62.8 all-gather.2
  87.9 79.6 all-gather.4

commit v2 on v1

v2 whole, which is shorter than its diff:
```python
import functools

import jax
import jax.numpy as jnp
from jax import lax
from jax.experimental import pallas as pl
from jax.experimental.pallas import tpu as pltpu
from jax.sharding import Mesh
from jax.sharding import PartitionSpec as P

D = 1024
BLK = 128
HALF = 64
PIECE = 256
TILE = 4
GRP = ("yh", "x", "c")
VMEM_LIMIT = 48 * 1024 * 1024
PARAMS = pltpu.CompilerParams(vmem_limit_bytes=VMEM_LIMIT)


def layer_norm(values):
    average = jnp.mean(values, axis=-1, keepdims=True)
    centred = values - average
    spread = jnp.mean(centred * centred, axis=-1, keepdims=True)
    return centred * lax.rsqrt(spread + 1e-05)


def low_lanes(shape):
    return lax.broadcasted_iota(jnp.int32, shape, len(shape) - 1) < HALF


def turn(values):
    return pltpu.roll(values, HALF, 1)


def norm_kernel(x_ref, out_ref):
    normed = layer_norm(x_ref[...].astype(jnp.float32)).astype(jnp.bfloat16)
    for copy in range(out_ref.shape[0]):
        out_ref[copy] = normed


def norm(rows, copies):
    return pl.pallas_call(
        norm_kernel,
        out_shape=jax.ShapeDtypeStruct((copies,) + rows.shape, jnp.bfloat16),
        compiler_params=PARAMS,
        cost_estimate=pl.CostEstimate(flops=1 << 20, bytes_accessed=1 << 20, transcendentals=0),
        name="norm",
    )(rows)


def project_kernel(length_ref, rows_ref, w_ref, mask_ref, along_z_ref, along_y_ref, gate_ref):
    slices, own, width = rows_ref.shape
    rows = rows_ref[...].reshape(slices * own, width)
    product = jnp.dot(rows, w_ref[...], preferred_element_type=jnp.float32)
    values = (product / (1.0 + jnp.exp(-product))).astype(jnp.bfloat16).astype(jnp.float32)
    values = values.reshape(slices, 2, own // 2, 128)
    first = values[:, 0].reshape(PIECE, 128)
    second = values[:, 1].reshape(PIECE, 128)
    low = low_lanes(first.shape)
    gate_ref[...] = jnp.where(low, turn(first), second).astype(jnp.bfloat16).reshape(gate_ref.shape)
    queries = (jnp.where(low, first, turn(second)) * (0.5 * HALF ** (-0.5))).astype(jnp.bfloat16)
    block = lax.broadcasted_iota(jnp.int32, mask_ref.shape, 1)
    live = jnp.clip(length_ref[0] - block * BLK, 0, BLK) * mask_ref[...]
    tail = jnp.broadcast_to(live, (16, 128)).astype(jnp.float32).astype(jnp.bfloat16)
    for ref in (along_z_ref, along_y_ref):
        for copy in range(ref.shape[0]):
            ref[copy, 0:PIECE] = queries
            ref[copy, PIECE : PIECE + 16] = tail


def project(length, rows, w_proj, mask, z_size, y_size):
    vmem = pl.BlockSpec(memory_space=pltpu.VMEM)
    return pl.pallas_call(
        project_kernel,
        out_shape=(
            jax.ShapeDtypeStruct((z_size, PIECE + 16, 128), jnp.bfloat16),
            jax.ShapeDtypeStruct((y_size, PIECE + 16, 128), jnp.bfloat16),
            jax.ShapeDtypeStruct((rows.shape[0], 16, 128), jnp.bfloat16),
        ),
        in_specs=[pl.BlockSpec(memory_space=pltpu.SMEM), vmem, vmem, vmem],
        out_specs=(vmem, vmem, vmem),
        compiler_params=PARAMS,
        cost_estimate=pl.CostEstimate(flops=2 * 512 * D * 128, bytes_accessed=2 << 20, transcendentals=0),
        name="project",
    )(length, rows, w_proj, mask)


def attend_kernel(pieces, live_ref, message_ref, *refs):
    kv_refs, (out_ref, query, kv, total) = refs[:pieces], refs[pieces:]
    user = pl.program_id(0)
    packed = message_ref[0, 0:PIECE].astype(jnp.float32)
    low = low_lanes(packed.shape)
    query[0] = jnp.where(low, packed, 0.0).astype(jnp.bfloat16)
    query[1] = jnp.where(low, turn(packed), 0.0).astype(jnp.bfloat16)
    total[...] = jnp.zeros_like(total)
    row = lax.broadcasted_iota(jnp.int32, (PIECE, 128), 0)
    for tile in range(pieces // TILE):
        base = (user * pieces + tile * TILE) * 2
        lives = [live_ref[base + i] for i in range(2 * TILE)]

        @pl.when(functools.reduce(jnp.add, lives) > 0)
        def _():
            for i in range(TILE):
                piece = kv_refs[tile * TILE + i][0]
                keep = row < jnp.where(row < BLK, lives[2 * i], lives[2 * i + 1] + BLK)
                kv[i * PIECE : (i + 1) * PIECE] = jnp.where(keep, piece, jnp.zeros_like(piece))
            for half in range(2):
                scores = lax.dot_general(
                    query[half], kv[...], (((1,), (1,)), ((), ())), preferred_element_type=jnp.float32
                )
                weights = (scores + scores * jnp.tanh(scores)).astype(jnp.bfloat16)
                total[half] += jnp.dot(weights, kv[...], preferred_element_type=jnp.float32)

    result = jnp.where(low, turn(total[0]), total[1]).astype(jnp.bfloat16)
    out_ref[...] = result.reshape(out_ref.shape)


def attend(live, messages, pieces, out_shape, out_block, out_index, name):
    users = messages.shape[0]
    count = len(pieces)
    return pl.pallas_call(
        functools.partial(attend_kernel, count),
        out_shape=jax.ShapeDtypeStruct(out_shape, jnp.bfloat16),
        grid=(users,),
        in_specs=[
            pl.BlockSpec(memory_space=pltpu.SMEM),
            pl.BlockSpec((1, PIECE + 16, 128), lambda u: (u, 0, 0)),
        ]
        + [pl.BlockSpec((1, PIECE, 128), lambda u: (u, 0, 0)) for _ in pieces],
        out_specs=pl.BlockSpec(out_block, out_index),
        scratch_shapes=[
            pltpu.VMEM((2, PIECE, 128), jnp.bfloat16),
            pltpu.VMEM((TILE * PIECE, 128), jnp.bfloat16),
            pltpu.VMEM((2, PIECE, 128), jnp.float32),
        ],
        compiler_params=PARAMS,
        cost_estimate=pl.CostEstimate(
            flops=users * count * PIECE * 512 * 512, bytes_accessed=3 << 20, transcendentals=users * count * PIECE * 512
        ),
        name=name,
    )(live, messages, *pieces)


def spread_heads(packed):
    columns = []
    for pair in range(packed.shape[0] // 2):
        even, odd = packed[2 * pair], packed[2 * pair + 1]
        low = low_lanes(even.shape)
        top = jnp.where(low, even, turn(odd))
        bottom = jnp.where(low, turn(even), odd)
        columns.append(jnp.concatenate([top, bottom], axis=0))
    return jnp.concatenate(columns, axis=1)


def output_kernel(count_ref, parts_ref, gate_ref, w_ref, x_ref, out_ref):
    attended = spread_heads(jnp.sum(parts_ref[...].astype(jnp.float32), axis=1))
    gate = spread_heads(gate_ref[...].astype(jnp.float32))
    gated = (layer_norm(attended) * gate).astype(jnp.bfloat16)
    branch = jnp.dot(gated, w_ref[...], preferred_element_type=jnp.float32)
    mixed = x_ref[...].astype(jnp.float32) + branch
    row = lax.broadcasted_iota(jnp.int32, mixed.shape, 0)
    out_ref[...] = jnp.where(row < count_ref[0], mixed, 0.0).astype(jnp.bfloat16)


def output(keep, parts, gate, w_out, rows):
    vmem = pl.BlockSpec(memory_space=pltpu.VMEM)
    return pl.pallas_call(
        output_kernel,
        out_shape=jax.ShapeDtypeStruct(rows.shape, jnp.bfloat16),
        in_specs=[pl.BlockSpec(memory_space=pltpu.SMEM), vmem, vmem, vmem, vmem],
        out_specs=vmem,
        compiler_params=PARAMS,
        cost_estimate=pl.CostEstimate(flops=2 * 32 * D * D, bytes_accessed=3 << 20, transcendentals=0),
        name="output",
    )(keep, parts, gate, w_out, rows)


def exchange(values, axes):
    return lax.all_to_all(values, axes, split_axis=0, concat_axis=0, tiled=True)


def per_device(sizes, cand_x, hist_kv, hist_len, cand_count, block_mask, w_proj, w_out):
    n_grp, n_z, n_y = sizes
    z, y = lax.axis_index("z"), lax.axis_index("yl")
    own_rows = cand_x.shape[0]
    rows = cand_x.reshape(own_rows, D)
    w_full = lax.all_gather(w_out, GRP, axis=0, tiled=True)
    all_rows = exchange(norm(rows, n_grp), GRP)

    kv = hist_kv.reshape(n_z, n_y, 2, PIECE, 128)
    along_y = [lax.dynamic_index_in_dim(kv[:, :, 0], y, 1, keepdims=False)]
    for step in range(1, n_y):
        piece = lax.dynamic_index_in_dim(kv[:, :, 0], y ^ step, 1, keepdims=False)
        along_y.append(lax.ppermute(piece, "yl", [(i, i ^ step) for i in range(n_y)]))
    along_z = [lax.dynamic_index_in_dim(kv[:, :, 1], z, 0, keepdims=False)]
    for step in range(1, n_z):
        piece = lax.dynamic_index_in_dim(kv[:, :, 1], (z + step) % n_z, 0, keepdims=False)
        along_z.append(lax.ppermute(piece, "z", [(i, (i + step) % n_z) for i in range(n_z)]))

    to_z, to_y, gate = project(hist_len, all_rows, w_proj, block_mask, n_z, n_y)
    from_z = exchange(to_z, "z")
    from_y = exchange(to_y, "yl")
    gates = exchange(gate, GRP)

    live_y = from_y[:, PIECE].astype(jnp.int32).reshape(n_y, n_z, n_y, 4)
    live_y = lax.dynamic_index_in_dim(live_y, y, 2, keepdims=False)[:, :, 2:]
    order_z = (z - jnp.arange(n_z, dtype=jnp.int32)) % n_z
    live_y = jnp.take(live_y, order_z, axis=1).reshape(-1)
    part_z = attend(
        live_y, from_y, along_z, (n_y, n_grp, 16, 128), (1, n_grp, 16, 128), lambda u: (u, 0, 0, 0), "attend_along_z"
    )
    shared = jnp.sum(exchange(part_z, "yl").astype(jnp.float32), axis=0)

    live_z = from_z[:, PIECE].astype(jnp.int32).reshape(n_z, n_z, n_y, 4)
    live_z = lax.dynamic_index_in_dim(live_z, z, 1, keepdims=False)[:, :, :2]
    order_y = y ^ jnp.arange(n_y, dtype=jnp.int32)
    live_z = jnp.take(live_z, order_y, axis=1).reshape(-1)
    part_y = attend(
        live_z, from_z, along_y, (n_grp, n_z, 16, 128), (n_grp, 1, 16, 128), lambda u: (0, u, 0, 0), "attend_along_y"
    )
    mine = (jnp.arange(n_z, dtype=jnp.int32) == z)[None, :, None, None]
    partial = (part_y.astype(jnp.float32) + jnp.where(mine, shared[:, None], 0.0)).astype(jnp.bfloat16)
    parts = exchange(partial.reshape(n_grp * n_z, 16, 128), GRP + ("z",)).reshape(n_grp, n_z, 16, 128)
    keep = cand_count - lax.axis_index(GRP) * own_rows
    return output(keep, parts, gates, w_full, rows).reshape(cand_x.shape)


def solution(mesh):
    split = Mesh(mesh.devices.reshape(2, 4, 2, 8, 4), ("yh", "x", "c", "z", "yl"))
    hist = ("z", "yl")
    in_specs = (
        P(GRP, hist, None),
        P(None, hist, GRP),
        P(hist),
        P(hist),
        P(hist, None),
        P(None, GRP),
        P(GRP, None),
    )
    return jax.shard_map(
        functools.partial(per_device, (16, 8, 4)),
        mesh=split,
        in_specs=in_specs,
        out_specs=P(GRP, hist, None),
        check_vma=False,
    )
```

time: 206 us -> 252 us (1.22)
  the two profiles are of different devices: /device:TPU:193 before, /device:TPU:48 now
where the time goes in v2:
time: 252 us; the launch traced here: 251 us
  waiting for transfers between devices  96.1 us (38%)
  starting transfers between devices  94.6 us (38%)
  Pallas kernels  17.2 us (7%)
  between operations  15 us (6%)
  blocking collectives  14.6 us (6%)
  local copies, waits for them, and re-layouts  12.5 us (5%)
    all_to_all x5, waiting for transfers between devices, exchange(): return lax.all_to_all(values, axes, split_axis=0, concat_axis=0, tiled=True)  45.7 us
    all_to_all x5, starting transfers between devices, exchange(): return lax.all_to_all(values, axes, split_axis=0, concat_axis=0, tiled=True)  43.7 us
    ppermute x7, starting transfers between devices, per_device(): lax.ppermute(piece, 'z', [(i, (i + step) % n_z) for i in range(n_z)])  41.7 us
    ppermute x3, waiting for transfers between devices, per_device(): lax.ppermute(piece, 'yl', [(i, i ^ step) for i in range(n_y)])  28.3 us
    ppermute x7, waiting for transfers between devices, per_device(): lax.ppermute(piece, 'z', [(i, (i + step) % n_z) for i in range(n_z)])  22.1 us
    all_to_all x1, blocking collectives, exchange(): return lax.all_to_all(values, axes, split_axis=0, concat_axis=0, tiled=True)  14.6 us
    pallas_call x2, Pallas kernels, attend(): pl.pallas_call(functools.partial(attend_kernel, count), out_shape=jax.Sha...  13.2 us
    ppermute x3, starting transfers between devices, per_device(): lax.ppermute(piece, 'yl', [(i, i ^ step) for i in range(n_y)])  9.2 us
  transfers between devices with their start and end apart: 16, of which 10 were waited for; matrix products, arithmetic and copies ran while one was open for 5% of the time, Pallas kernels for 5%

profile of v2, /device:TPU:48, one launch (start us, length us, event | category | flops | bytes accessed | tf_op | source)
XLA Modules:
  0.0 251.2 jit_solution(1077367879191178520)
XLA Ops:
  6.5 0.8 copy-done.1
  7.4 1.2 norm.1
  8.6 9.7 %all-to-all-start = ((bf16[16,32,1024]{2,1,0:T(8,128)(2,1)}), bf16[16,32,1024]{2,1,0:T(8,128)(2,1)S(1)}, u32[]{:S(2)}, u32[]{:S(2)}) async-start(bf16[16,32,1024]{2,1,0:T(8,128)(2,1)} %norm.1), calls=%async_computation | async-start | bytes 2097152 | tf_op jit(solution)/shard_map/all_to_all | solution.py:180
  19.0 4.1 %fusion.5 = (bf16[8,4,1,256,128]{4,3,2,1,0:T(8,128)(2,1)S(1)}, bf16[8,4,1,256,128]{4,3,2,1,0:T(8,128)(2,1)}) fusion(bf16[8,4,2,256,128]{4,3,2,1,0:T(8,128)(2,1)} %bitcast.70), kind=kLoop, calls=%fused_computation.42 | loop fusion | bytes 8388608 | tf_op jit(solution)/shard_map/slice | solution.py:196
  23.1 21.7 %all-to-all-done.rows_ref = bf16[16,32,1024]{2,1,0:T(8,128)(2,1)S(1)} async-done(((bf16[16,32,1024]{2,1,0:T(8,128)(2,1)}), bf16[16,32,1024]{2,1,0:T(8,128)(2,1)S(1)}, u32[]{:S(2)}, u32[]{:S(2)}) %all-to-all-start) | async-done | bytes 1048608 | tf_op jit(solution)/shard_map/all_to_all | solution.py:180
  44.8 1.4 project.1
  46.2 4.2 %all-to-all-start.2 = ((bf16[4,272,128]{2,1,0:T(8,128)(2,1)}), bf16[4,272,128]{2,1,0:T(8,128)(2,1)S(1)}, u32[]{:S(2)}, u32[]{:S(2)}) async-start(bf16[4,272,128]{2,1,0:T(8,128)(2,1)} %get-tuple-element.9), calls=%async_computation.2 | async-start | bytes 557056 | tf_op jit(solution)/shard_map/all_to_all | solution.py:180
  50.4 1.1 dynamic-slice_bitcast_fusion.4
  51.5 4.3 %collective-permute-start.3 = (bf16[4,256,128]{2,1,0:T(8,128)(2,1)}, bf16[4,256,128]{2,1,0:T(8,128)(2,1)S(1)}, u32[]{:S(2)}, u32[]{:S(2)}) collective-permute-start(bf16[4,256,128]{2,1,0:T(8,128)(2,1)} %get-tuple-element.19), channel_id=1, source_target_pairs={{0,4},{4,8},{8,12},{12,16},{16,20},{20,24},{24,28},{28,0},{1,5},{5... | collective-permute-start | bytes 786440 | tf_op jit(solution)/shard_map/ppermute | solution.py:199
  55.8 6.1 %collective-permute-start.4 = (bf16[4,256,128]{2,1,0:T(8,128)(2,1)}, bf16[4,256,128]{2,1,0:T(8,128)(2,1)S(1)}, u32[]{:S(2)}, u32[]{:S(2)}) collective-permute-start(bf16[4,256,128]{2,1,0:T(8,128)(2,1)} %get-tuple-element.18), channel_id=1, source_target_pairs={{0,8},{4,12},{8,16},{12,20},{16,24},{20,28},{24,0},{28,4},{1,9},{5... | collective-permute-start | bytes 786440 | tf_op jit(solution)/shard_map/ppermute | solution.py:199
  61.9 7.3 %collective-permute-start.5 = (bf16[4,256,128]{2,1,0:T(8,128)(2,1)}, bf16[4,256,128]{2,1,0:T(8,128)(2,1)S(1)}, u32[]{:S(2)}, u32[]{:S(2)}) collective-permute-start(bf16[4,256,128]{2,1,0:T(8,128)(2,1)} %get-tuple-element.17), channel_id=1, source_target_pairs={{0,12},{4,16},{8,20},{12,24},{16,28},{20,0},{24,4},{28,8},{1,13},{... | collective-permute-start | bytes 786440 | tf_op jit(solution)/shard_map/ppermute | solution.py:199
  69.2 2.8 %collective-permute-start.6 = (bf16[4,256,128]{2,1,0:T(8,128)(2,1)}, bf16[4,256,128]{2,1,0:T(8,128)(2,1)S(1)}, u32[]{:S(2)}, u32[]{:S(2)}) collective-permute-start(bf16[4,256,128]{2,1,0:T(8,128)(2,1)} %get-tuple-element.16), channel_id=1, source_target_pairs={{0,16},{4,20},{8,24},{12,28},{16,0},{20,4},{24,8},{28,12},{1,17},{... | collective-permute-start | bytes 786440 | tf_op jit(solution)/shard_map/ppermute | solution.py:199
  72.1 6.9 %collective-permute-start.7 = (bf16[4,256,128]{2,1,0:T(8,128)(2,1)}, bf16[4,256,128]{2,1,0:T(8,128)(2,1)S(1)}, u32[]{:S(2)}, u32[]{:S(2)}) collective-permute-start(bf16[4,256,128]{2,1,0:T(8,128)(2,1)} %get-tuple-element.15), channel_id=1, source_target_pairs={{0,20},{4,24},{8,28},{12,0},{16,4},{20,8},{24,12},{28,16},{1,21},{... | collective-permute-start | bytes 786440 | tf_op jit(solution)/shard_map/ppermute | solution.py:199
  79.1 0.1 reshape.143
  79.3 3.7 %collective-permute-start.8 = (bf16[4,256,128]{2,1,0:T(8,128)(2,1)S(1)}, bf16[4,256,128]{2,1,0:T(8,128)(2,1)S(1)}, u32[]{:S(2)}, u32[]{:S(2)}) collective-permute-start(bf16[4,256,128]{2,1,0:T(8,128)(2,1)S(1)} %get-tuple-element.14), channel_id=1, source_target_pairs={{0,24},{4,28},{8,0},{12,4},{16,8},{20,12},{24,16},{28,20},{1,25},{... | collective-permute-start | bytes 786440 | tf_op jit(solution)/shard_map/ppermute | solution.py:199
  82.9 1.7 collective-permute-done.4.refs_2_
  84.6 10.6 %collective-permute-start.9 = (bf16[4,256,128]{2,1,0:T(8,128)(2,1)S(1)}, bf16[4,256,128]{2,1,0:T(8,128)(2,1)S(1)}, u32[]{:S(2)}, u32[]{:S(2)}) collective-permute-start(bf16[4,256,128]{2,1,0:T(8,128)(2,1)S(1)} %get-tuple-element.13), channel_id=1, source_target_pairs={{0,28},{4,0},{8,4},{12,8},{16,12},{20,16},{24,20},{28,24},{1,29},{... | collective-permute-start | bytes 786440 | tf_op jit(solution)/shard_map/ppermute | solution.py:199
  95.4 0.1 copy.35
  95.5 0.6 gather_fusion.1
  96.1 0.1 select_bitcast_fusion
  96.2 0.1 copy.26
  96.3 0.1 select_n.156.live_ref
  96.4 5.9 %collective-permute-done.5.refs_3_ = bf16[4,256,128]{2,1,0:T(8,128)(2,1)S(1)} collective-permute-done((bf16[4,256,128]{2,1,0:T(8,128)(2,1)}, bf16[4,256,128]{2,1,0:T(8,128)(2,1)S(1)}, u32[]{:S(2)}, u32[]{:S(2)}) %collective-permute-start.5) | collective-permute-done | bytes 262176 | tf_op jit(solution)/shard_map/ppermute | solution.py:199
  102.4 0.5 collective-permute-done.7.refs_5_
  102.8 10.8 %collective-permute-done.8.refs_6_ = bf16[4,256,128]{2,1,0:T(8,128)(2,1)S(1)} collective-permute-done((bf16[4,256,128]{2,1,0:T(8,128)(2,1)S(1)}, bf16[4,256,128]{2,1,0:T(8,128)(2,1)S(1)}, u32[]{:S(2)}, u32[]{:S(2)}) %collective-permute-start.8) | collective-permute-done | bytes 262176 | tf_op jit(solution)/shard_map/ppermute | solution.py:199
  113.7 3.1 %collective-permute-done.9.refs_7_ = bf16[4,256,128]{2,1,0:T(8,128)(2,1)S(1)} collective-permute-done((bf16[4,256,128]{2,1,0:T(8,128)(2,1)S(1)}, bf16[4,256,128]{2,1,0:T(8,128)(2,1)S(1)}, u32[]{:S(2)}, u32[]{:S(2)}) %collective-permute-start.9) | collective-permute-done | bytes 262176 | tf_op jit(solution)/shard_map/ppermute | solution.py:199
  116.8 5.1 %attend_along_z.1 = bf16[4,16,16,128]{3,2,1,0:T(8,128)(2,1)S(1)} custom-call(s32[64]{0:T(128)S(1)} %select_n.156.live_ref, bf16[4,272,128]{2,1,0:T(8,128)(2,1)S(1)} %all-to-all-done.2.message_ref, bf16[4,256,128]{2,1,0:T(8,128)(2,1)S(1)} %get-tuple-element.20.refs_0_, bf16[4,256,128]{2,1,0:T(8,128)(2,1)S(1)} %collective-permute-done.3.refs_1_, ...), custom_call_target="tpu_custom_call" | custom-call | flops 2147483648 | bytes 3145728 | tf_op jit(solution)/shard_map/attend_along_z/pallas_call | solution.py:122
  121.9 14.6 %all_to_all.30 = bf16[4,16,16,128]{3,2,1,0:T(8,128)(2,1)S(1)} all-to-all(bf16[4,16,16,128]{3,2,1,0:T(8,128)(2,1)S(1)} %attend_along_z.1), channel_id=1, replica_groups=mesh['yh'=2,'x'=4,'c'=2,'z'=8,'yl'=4] {'yl'}, dimensions={0} | all-to-all | bytes 524288 | tf_op jit(solution)/shard_map/all_to_all | solution.py:180
  136.4 7.4 %all-to-all-start.1 = ((bf16[8,272,128]{2,1,0:T(8,128)(2,1)}), bf16[8,272,128]{2,1,0:T(8,128)(2,1)S(1)}, u32[]{:S(2)}, u32[]{:S(2)}) async-start(bf16[8,272,128]{2,1,0:T(8,128)(2,1)} %get-tuple-element.8), calls=%async_computation.1 | async-start | bytes 1114112 | tf_op jit(solution)/shard_map/all_to_all | solution.py:180
  143.9 2.7 %dynamic-slice_bitcast_fusion = (bf16[8,256,128]{2,1,0:T(8,128)(2,1)}, bf16[8,256,128]{2,1,0:T(8,128)(2,1)}, bf16[8,256,128]{2,1,0:T(8,128)(2,1)}, bf16[8,256,128]{2,1,0:T(8,128)(2,1)S(1)}) fusion(bf16[8,4,1,256,128]{4,3,2,1,0:T(8,128)(2,1)} %get-tuple-element.12, s32[]{:T(128)S(6)} %select_n.150, s32[]{:T(128)S(6)} %select_n.149, s32[]{:T(128)S(6)} %select_n.148, ...), kind=kLoop, calls=%fused_computation.4 | loop fusion | bytes 4194320 | tf_op jit(solution)/shard_map/jit(dynamic_index_in_dim)/squeeze | solution.py:194
  146.6 3.8 %collective-permute-start = (bf16[8,256,128]{2,1,0:T(8,128)(2,1)}, bf16[8,256,128]{2,1,0:T(8,128)(2,1)S(1)}, u32[]{:S(2)}, u32[]{:S(2)}) collective-permute-start(bf16[8,256,128]{2,1,0:T(8,128)(2,1)} %get-tuple-element.23), channel_id=1, source_target_pairs={{0,1},{1,0},{2,3},{3,2},{4,5},{5,4},{6,7},{7,6},{8,9},{9,8},{10,11... | collective-permute-start | bytes 1572872 | tf_op jit(solution)/shard_map/ppermute | solution.py:195
  150.4 1.9 collective-permute-start.1
  152.3 3.5 %collective-permute-start.2 = (bf16[8,256,128]{2,1,0:T(8,128)(2,1)}, bf16[8,256,128]{2,1,0:T(8,128)(2,1)S(1)}, u32[]{:S(2)}, u32[]{:S(2)}) collective-permute-start(bf16[8,256,128]{2,1,0:T(8,128)(2,1)} %get-tuple-element.21), channel_id=1, source_target_pairs={{0,3},{1,2},{2,1},{3,0},{4,7},{5,6},{6,5},{7,4},{8,11},{9,10},{10,... | collective-permute-start | bytes 1572872 | tf_op jit(solution)/shard_map/ppermute | solution.py:195
  155.9 6.0 %all-to-all-done.1.message_ref = bf16[8,272,128]{2,1,0:T(8,128)(2,1)S(1)} async-done(((bf16[8,272,128]{2,1,0:T(8,128)(2,1)}), bf16[8,272,128]{2,1,0:T(8,128)(2,1)S(1)}, u32[]{:S(2)}, u32[]{:S(2)}) %all-to-all-start.1) | async-done | bytes 557088 | tf_op jit(solution)/shard_map/all_to_all | solution.py:180
  161.9 9.3 %all-to-all-start.5 = ((bf16[16,16,128]{2,1,0:T(8,128)(2,1)}), bf16[16,16,128]{2,1,0:T(8,128)(2,1)S(1)}, u32[]{:S(2)}, u32[]{:S(2)}) async-start(bf16[16,16,128]{2,1,0:T(8,128)(2,1)} %get-tuple-element.10), calls=%async_computation.5 | async-start | bytes 131072 | tf_op jit(solution)/shard_map/all_to_all | solution.py:180
  171.2 0.1 copy.21
  171.4 0.6 gather_fusion
  171.9 0.1 select_bitcast_fusion.1
  172.0 0.1 copy.22
  172.1 0.1 select_n.146.live_ref
  172.2 16.6 %collective-permute-done.1.refs_2_ = bf16[8,256,128]{2,1,0:T(8,128)(2,1)S(1)} collective-permute-done((bf16[8,256,128]{2,1,0:T(8,128)(2,1)}, bf16[8,256,128]{2,1,0:T(8,128)(2,1)S(1)}, u32[]{:S(2)}, u32[]{:S(2)}) %collective-permute-start.1) | collective-permute-done | bytes 524320 | tf_op jit(solution)/shard_map/ppermute | solution.py:195
  188.9 11.6 %collective-permute-done.2.refs_3_ = bf16[8,256,128]{2,1,0:T(8,128)(2,1)S(1)} collective-permute-done((bf16[8,256,128]{2,1,0:T(8,128)(2,1)}, bf16[8,256,128]{2,1,0:T(8,128)(2,1)S(1)}, u32[]{:S(2)}, u32[]{:S(2)}) %collective-permute-start.2) | collective-permute-done | bytes 524320 | tf_op jit(solution)/shard_map/ppermute | solution.py:195
  200.5 8.1 %attend_along_y.1 = bf16[16,8,16,128]{3,2,1,0:T(8,128)(2,1)S(1)} custom-call(s32[64]{0:T(128)S(1)} %select_n.146.live_ref, bf16[8,272,128]{2,1,0:T(8,128)(2,1)S(1)} %all-to-all-done.1.message_ref, bf16[8,256,128]{2,1,0:T(8,128)(2,1)S(1)} %get-tuple-element.24.refs_0_, bf16[8,256,128]{2,1,0:T(8,128)(2,1)S(1)} %collective-permute-done.refs_1_, ...), custom_call_target="tpu_custom_call" | custom-call | flops 2147483648 | bytes 3145728 | tf_op jit(solution)/shard_map/attend_along_y/pallas_call | solution.py:122
  208.7 1.0 add_convert_fusion
  209.7 13.0 %all-to-all-start.4 = ((bf16[128,16,128]{2,1,0:T(8,128)(2,1)}), bf16[128,16,128]{2,1,0:T(8,128)(2,1)S(1)}, u32[]{:S(2)}, u32[]{:S(2)}) async-start(bf16[128,16,128]{2,1,0:T(8,128)(2,1)} %bitcast.22), calls=%async_computation.4 | async-start | bytes 1048576 | tf_op jit(solution)/shard_map/all_to_all | solution.py:180
  223.4 18.0 %all-to-all-done.4 = bf16[128,16,128]{2,1,0:T(8,128)(2,1)S(1)} async-done(((bf16[128,16,128]{2,1,0:T(8,128)(2,1)}), bf16[128,16,128]{2,1,0:T(8,128)(2,1)S(1)}, u32[]{:S(2)}, u32[]{:S(2)}) %all-to-all-start.4) | async-done | bytes 524320 | tf_op jit(solution)/shard_map/all_to_all | solution.py:180
  241.4 1.6 copy-done
  243.0 1.3 output.1
  (30 shorter events, 0.3 us)
Async XLA Ops:
  6.5 0.8 copy-start.1
  8.6 36.2 %all-to-all-start = ((bf16[16,32,1024]{2,1,0:T(8,128)(2,1)}), bf16[16,32,1024]{2,1,0:T(8,128)(2,1)S(1)}, u32[]{:S(2)}, u32[]{:S(2)}) async-start(bf16[16,32,1024]{2,1,0:T(8,128)(2,1)} %norm.1), calls=%async_computation | async-start | bytes 2097152 | tf_op jit(solution)/shard_map/all_to_all | solution.py:180
  19.0 25.8 %copy-start.3 = (bf16[1024,128]{1,0:T(8,128)(2,1)S(1)}, bf16[1024,128]{1,0:T(8,128)(2,1)}, u32[]{:S(2)}) copy-start(bf16[1024,128]{1,0:T(8,128)(2,1)} %w_ref.1) | copy-start | bytes 786436
  19.0 25.8 %copy-start.4 = (s32[1,128]{1,0:T(1,128)S(1)}, s32[1,128]{1,0:T(1,128)}, u32[]{:S(2)}) copy-start(s32[1,128]{1,0:T(1,128)} %mask_ref.1) | copy-start | bytes 1540
  46.2 32.9 %all-to-all-start.2 = ((bf16[4,272,128]{2,1,0:T(8,128)(2,1)}), bf16[4,272,128]{2,1,0:T(8,128)(2,1)S(1)}, u32[]{:S(2)}, u32[]{:S(2)}) async-start(bf16[4,272,128]{2,1,0:T(8,128)(2,1)} %get-tuple-element.9), calls=%async_computation.2 | async-start | bytes 557056 | tf_op jit(solution)/shard_map/all_to_all | solution.py:180
  50.4 173.0 %all-gather.2.cloned.1.call-start = ((), (), s32[]{:S(2)}) async-start(), calls=%async_computation.6 | async-start | bytes 2228224 | tf_op jit(solution)/shard_map/all_gather | solution.py:188
  51.5 27.7 %collective-permute-start.3 = (bf16[4,256,128]{2,1,0:T(8,128)(2,1)}, bf16[4,256,128]{2,1,0:T(8,128)(2,1)S(1)}, u32[]{:S(2)}, u32[]{:S(2)}) collective-permute-start(bf16[4,256,128]{2,1,0:T(8,128)(2,1)} %get-tuple-element.19), channel_id=1, source_target_pairs={{0,4},{4,8},{8,12},{12,16},{16,20},{20,24},{24,28},{28,0},{1,5},{5... | collective-permute-start | bytes 786440 | tf_op jit(solution)/shard_map/ppermute | solution.py:199
  55.8 28.8 %collective-permute-start.4 = (bf16[4,256,128]{2,1,0:T(8,128)(2,1)}, bf16[4,256,128]{2,1,0:T(8,128)(2,1)S(1)}, u32[]{:S(2)}, u32[]{:S(2)}) collective-permute-start(bf16[4,256,128]{2,1,0:T(8,128)(2,1)} %get-tuple-element.18), channel_id=1, source_target_pairs={{0,8},{4,12},{8,16},{12,20},{16,24},{20,28},{24,0},{28,4},{1,9},{5... | collective-permute-start | bytes 786440 | tf_op jit(solution)/shard_map/ppermute | solution.py:199
  61.9 40.4 %collective-permute-start.5 = (bf16[4,256,128]{2,1,0:T(8,128)(2,1)}, bf16[4,256,128]{2,1,0:T(8,128)(2,1)S(1)}, u32[]{:S(2)}, u32[]{:S(2)}) collective-permute-start(bf16[4,256,128]{2,1,0:T(8,128)(2,1)} %get-tuple-element.17), channel_id=1, source_target_pairs={{0,12},{4,16},{8,20},{12,24},{16,28},{20,0},{24,4},{28,8},{1,13},{... | collective-permute-start | bytes 786440 | tf_op jit(solution)/shard_map/ppermute | solution.py:199
  69.2 33.1 %collective-permute-start.6 = (bf16[4,256,128]{2,1,0:T(8,128)(2,1)}, bf16[4,256,128]{2,1,0:T(8,128)(2,1)S(1)}, u32[]{:S(2)}, u32[]{:S(2)}) collective-permute-start(bf16[4,256,128]{2,1,0:T(8,128)(2,1)} %get-tuple-element.16), channel_id=1, source_target_pairs={{0,16},{4,20},{8,24},{12,28},{16,0},{20,4},{24,8},{28,12},{1,17},{... | collective-permute-start | bytes 786440 | tf_op jit(solution)/shard_map/ppermute | solution.py:199
  72.1 30.8 %collective-permute-start.7 = (bf16[4,256,128]{2,1,0:T(8,128)(2,1)}, bf16[4,256,128]{2,1,0:T(8,128)(2,1)S(1)}, u32[]{:S(2)}, u32[]{:S(2)}) collective-permute-start(bf16[4,256,128]{2,1,0:T(8,128)(2,1)} %get-tuple-element.15), channel_id=1, source_target_pairs={{0,20},{4,24},{8,28},{12,0},{16,4},{20,8},{24,12},{28,16},{1,21},{... | collective-permute-start | bytes 786440 | tf_op jit(solution)/shard_map/ppermute | solution.py:199
  79.3 34.4 %collective-permute-start.8 = (bf16[4,256,128]{2,1,0:T(8,128)(2,1)S(1)}, bf16[4,256,128]{2,1,0:T(8,128)(2,1)S(1)}, u32[]{:S(2)}, u32[]{:S(2)}) collective-permute-start(bf16[4,256,128]{2,1,0:T(8,128)(2,1)S(1)} %get-tuple-element.14), channel_id=1, source_target_pairs={{0,24},{4,28},{8,0},{12,4},{16,8},{20,12},{24,16},{28,20},{1,25},{... | collective-permute-start | bytes 786440 | tf_op jit(solution)/shard_map/ppermute | solution.py:199
  84.6 32.2 %collective-permute-start.9 = (bf16[4,256,128]{2,1,0:T(8,128)(2,1)S(1)}, bf16[4,256,128]{2,1,0:T(8,128)(2,1)S(1)}, u32[]{:S(2)}, u32[]{:S(2)}) collective-permute-start(bf16[4,256,128]{2,1,0:T(8,128)(2,1)S(1)} %get-tuple-element.13), channel_id=1, source_target_pairs={{0,28},{4,0},{8,4},{12,8},{16,12},{20,16},{24,20},{28,24},{1,29},{... | collective-permute-start | bytes 786440 | tf_op jit(solution)/shard_map/ppermute | solution.py:199
  136.4 25.5 %all-to-all-start.1 = ((bf16[8,272,128]{2,1,0:T(8,128)(2,1)}), bf16[8,272,128]{2,1,0:T(8,128)(2,1)S(1)}, u32[]{:S(2)}, u32[]{:S(2)}) async-start(bf16[8,272,128]{2,1,0:T(8,128)(2,1)} %get-tuple-element.8), calls=%async_computation.1 | async-start | bytes 1114112 | tf_op jit(solution)/shard_map/all_to_all | solution.py:180
  146.6 25.6 %collective-permute-start = (bf16[8,256,128]{2,1,0:T(8,128)(2,1)}, bf16[8,256,128]{2,1,0:T(8,128)(2,1)S(1)}, u32[]{:S(2)}, u32[]{:S(2)}) collective-permute-start(bf16[8,256,128]{2,1,0:T(8,128)(2,1)} %get-tuple-element.23), channel_id=1, source_target_pairs={{0,1},{1,0},{2,3},{3,2},{4,5},{5,4},{6,7},{7,6},{8,9},{9,8},{10,11... | collective-permute-start | bytes 1572872 | tf_op jit(solution)/shard_map/ppermute | solution.py:195
  150.4 38.5 %collective-permute-start.1 = (bf16[8,256,128]{2,1,0:T(8,128)(2,1)}, bf16[8,256,128]{2,1,0:T(8,128)(2,1)S(1)}, u32[]{:S(2)}, u32[]{:S(2)}) collective-permute-start(bf16[8,256,128]{2,1,0:T(8,128)(2,1)} %get-tuple-element.22), channel_id=1, source_target_pairs={{0,2},{1,3},{2,0},{3,1},{4,6},{5,7},{6,4},{7,5},{8,10},{9,11},{10,... | collective-permute-start | bytes 1572872 | tf_op jit(solution)/shard_map/ppermute | solution.py:195
  152.3 48.2 %collective-permute-start.2 = (bf16[8,256,128]{2,1,0:T(8,128)(2,1)}, bf16[8,256,128]{2,1,0:T(8,128)(2,1)S(1)}, u32[]{:S(2)}, u32[]{:S(2)}) collective-permute-start(bf16[8,256,128]{2,1,0:T(8,128)(2,1)} %get-tuple-element.21), channel_id=1, source_target_pairs={{0,3},{1,2},{2,1},{3,0},{4,7},{5,6},{6,5},{7,4},{8,11},{9,10},{10,... | collective-permute-start | bytes 1572872 | tf_op jit(solution)/shard_map/ppermute | solution.py:195
  161.9 47.8 %all-to-all-start.5 = ((bf16[16,16,128]{2,1,0:T(8,128)(2,1)}), bf16[16,16,128]{2,1,0:T(8,128)(2,1)S(1)}, u32[]{:S(2)}, u32[]{:S(2)}) async-start(bf16[16,16,128]{2,1,0:T(8,128)(2,1)} %get-tuple-element.10), calls=%async_computation.5 | async-start | bytes 131072 | tf_op jit(solution)/shard_map/all_to_all | solution.py:180
  208.7 32.8 %copy-start.2 = (bf16[32,1,1024]{2,0,1:T(8,128)(2,1)S(1)}, bf16[32,1,1024]{2,0,1:T(8,128)(2,1)}, u32[]{:S(2)}) copy-start(bf16[32,1,1024]{2,0,1:T(8,128)(2,1)} %param.7) | copy-start | bytes 196612
  209.7 31.7 %all-to-all-start.4 = ((bf16[128,16,128]{2,1,0:T(8,128)(2,1)}), bf16[128,16,128]{2,1,0:T(8,128)(2,1)S(1)}, u32[]{:S(2)}, u32[]{:S(2)}) async-start(bf16[128,16,128]{2,1,0:T(8,128)(2,1)} %bitcast.22), calls=%async_computation.4 | async-start | bytes 1048576 | tf_op jit(solution)/shard_map/all_to_all | solution.py:180
  241.4 1.6 copy-start
Sparse Core Ops, SparseCore 0:
  79.2 63.5 all-gather.1

commit v3 on v1

v3 whole, which is shorter than its diff:
```python
import functools

import jax
import jax.numpy as jnp
from jax import lax
from jax.experimental import pallas as pl
from jax.experimental.pallas import tpu as pltpu
from jax.sharding import Mesh
from jax.sharding import PartitionSpec as P

D = 1024
BLK = 128
TILE = 2048
CHUNKS = ((0, 256), (256, 384), (384, 512))
GRP = ("yh", "x", "c")
HALF = 64
PARAMS = pltpu.CompilerParams(vmem_limit_bytes=24 * 1024 * 1024)


def layer_norm(values):
    average = jnp.mean(values, axis=-1, keepdims=True)
    centred = values - average
    spread = jnp.mean(centred * centred, axis=-1, keepdims=True)
    return centred * lax.rsqrt(spread + 1e-05)


def low_lanes(shape):
    return lax.broadcasted_iota(jnp.int32, shape, len(shape) - 1) < HALF


def member(place_ref, turns, core, half):
    yh, x, c = place_ref[0], place_ref[1], place_ref[2]
    return (yh ^ half) * 8 + lax.rem(x - turns + 4, 4) * 2 + (c ^ core)


def project_kernel(place_ref, *refs):
    quads, (w_ref, query_ref, gate_ref) = refs[:4], refs[4:]
    for turns, quad in enumerate(quads):
        _, _, own, width = quad.shape
        rows = quad[...].reshape(4 * own, width).astype(jnp.float32)
        normed = layer_norm(rows).astype(jnp.bfloat16)
        product = jnp.dot(normed, w_ref[...], preferred_element_type=jnp.float32)
        values = (product / (1.0 + jnp.exp(-product))).astype(jnp.bfloat16).astype(jnp.float32)
        query = jnp.where(low_lanes(values.shape), values * (0.5 * HALF ** (-0.5)), 0.0).astype(jnp.bfloat16)
        pairs = values.reshape(4, 2, own // 2, 128)
        first, second = pairs[:, 0], pairs[:, 1]
        turned = pltpu.roll(first.reshape(-1, 128), HALF, 1).reshape(first.shape)
        gate = jnp.where(low_lanes(first.shape), turned, second).astype(jnp.bfloat16)
        for core in range(2):
            for half in range(2):
                at = member(place_ref, turns, core, half)
                block = core * 2 + half
                query_ref[pl.ds(pl.multiple_of(at * own, own), own)] = query[block * own : (block + 1) * own]
                gate_ref[at] = gate[block]


def project(place, quads, w_proj):
    own = quads[0].shape[2]
    vmem = pl.BlockSpec(memory_space=pltpu.VMEM)
    return pl.pallas_call(
        project_kernel,
        out_shape=(
            jax.ShapeDtypeStruct((16 * own, 128), jnp.bfloat16),
            jax.ShapeDtypeStruct((16, own // 2, 128), jnp.bfloat16),
        ),
        in_specs=[pl.BlockSpec(memory_space=pltpu.SMEM)] + [vmem] * 5,
        out_specs=(vmem, vmem),
        compiler_params=PARAMS,
        cost_estimate=pl.CostEstimate(flops=2 * 512 * D * 128, bytes_accessed=2 << 20, transcendentals=0),
        name="project",
    )(place, *quads, w_proj)


def attend_tiles(live_ref, count_ref, query_ref, kv_ref, total, masked):
    step = pl.program_id(0)
    blocks = kv_ref.shape[0] // BLK
    lives = [live_ref[step * blocks + i] for i in range(blocks)]

    @pl.when(functools.reduce(jnp.add, lives) > 0)
    def _():
        row = lax.broadcasted_iota(jnp.int32, (BLK, 128), 0)
        for i in range(blocks):
            block = kv_ref[i * BLK : (i + 1) * BLK]
            masked[i * BLK : (i + 1) * BLK] = jnp.where(row < lives[i], block, jnp.zeros_like(block))
        for start, end in CHUNKS:

            @pl.when(count_ref[0] > start)
            def _():
                scores = lax.dot_general(
                    query_ref[start:end], masked[...], (((1,), (1,)), ((), ())), preferred_element_type=jnp.float32
                )
                weights = (scores + scores * jnp.tanh(scores)).astype(jnp.bfloat16)
                total[start:end] += jnp.dot(weights, masked[...], preferred_element_type=jnp.float32)


def attend_first_kernel(live_ref, count_ref, query_ref, kv_ref, total, masked):
    @pl.when(pl.program_id(0) == 0)
    def _():
        total[...] = jnp.zeros_like(total)

    attend_tiles(live_ref, count_ref, query_ref, kv_ref, total, masked)


def attend_last_kernel(live_ref, count_ref, query_ref, kv_ref, before_ref, gate_ref, out_ref, total, masked):
    @pl.when(pl.program_id(0) == 0)
    def _():
        total[...] = before_ref[...]

    attend_tiles(live_ref, count_ref, query_ref, kv_ref, total, masked)

    @pl.when(pl.program_id(0) == pl.num_programs(0) - 1)
    def _():
        slices = total[...].reshape(out_ref.shape[0], 2, 16, 128)
        first, second = slices[:, 0], slices[:, 1]
        turned = pltpu.roll(first.reshape(-1, 128), HALF, 1).reshape(first.shape)
        out_ref[:, 0:16, :] = jnp.where(low_lanes(first.shape), turned, second).astype(jnp.bfloat16)
        out_ref[:, 16:32, :] = gate_ref[...]


def attend(live, cand_count, query, kv, before=None, gate=None):
    count = query.shape[0]
    positions = kv.shape[0]
    smem = pl.BlockSpec(memory_space=pltpu.SMEM)
    in_specs = [smem, smem, pl.BlockSpec((count, 128), lambda i: (0, 0)), pl.BlockSpec((TILE, 128), lambda i: (i, 0))]
    masked = pltpu.VMEM((TILE, 128), jnp.bfloat16)
    running = pltpu.VMEM((count, 128), jnp.float32)
    common = dict(
        grid=(positions // TILE,),
        compiler_params=PARAMS,
        cost_estimate=pl.CostEstimate(
            flops=4 * count * positions * 128, bytes_accessed=positions * 256, transcendentals=count * positions
        ),
    )
    if before is None:
        return pl.pallas_call(
            attend_first_kernel,
            out_shape=jax.ShapeDtypeStruct((count, 128), jnp.float32),
            in_specs=in_specs,
            out_specs=pl.BlockSpec((count, 128), lambda i: (0, 0)),
            scratch_shapes=[masked],
            name="attend_first",
            **common,
        )(live, cand_count, query, kv)
    return pl.pallas_call(
        attend_last_kernel,
        out_shape=jax.ShapeDtypeStruct((count // 32, 32, 128), jnp.bfloat16),
        in_specs=in_specs
        + [pl.BlockSpec((count, 128), lambda i: (0, 0)), pl.BlockSpec((count // 32, 16, 128), lambda i: (0, 0, 0))],
        out_specs=pl.BlockSpec((count // 32, 32, 128), lambda i: (0, 0, 0)),
        scratch_shapes=[running, masked],
        name="attend_last",
        **common,
    )(live, cand_count, query, kv, before, gate)


def spread_heads(packed):
    columns = []
    for pair in range(len(packed) // 2):
        even, odd = packed[2 * pair], packed[2 * pair + 1]
        low = low_lanes(even.shape)
        top = jnp.where(low, even, pltpu.roll(odd, HALF, 1))
        bottom = jnp.where(low, pltpu.roll(even, HALF, 1), odd)
        columns.append(jnp.concatenate([top, bottom], axis=0))
    return jnp.concatenate(columns, axis=1)


def output_kernel(place_ref, count_ref, parts_ref, *refs):
    quads, (x_ref, out_ref) = refs[:4], refs[4:]
    attended, gate = [], []
    for turns in range(4):
        for core in range(2):
            for half in range(2):
                part = parts_ref[member(place_ref, turns, core, half)].astype(jnp.float32)
                attended.append(part[0:16])
                gate.append(part[16:32])
    gated = (layer_norm(spread_heads(attended)) * spread_heads(gate)).astype(jnp.bfloat16)
    mixed = x_ref[...].astype(jnp.float32)
    for turns, quad in enumerate(quads):
        depth = 4 * quad.shape[2]
        weights = quad[...].reshape(depth, quad.shape[3])
        mixed += jnp.dot(gated[:, turns * depth : (turns + 1) * depth], weights, preferred_element_type=jnp.float32)
    row = lax.broadcasted_iota(jnp.int32, mixed.shape, 0)
    out_ref[...] = jnp.where(row < count_ref[0], mixed, 0.0).astype(jnp.bfloat16)


def output(place, keep, parts, quads, rows):
    smem, vmem = pl.BlockSpec(memory_space=pltpu.SMEM), pl.BlockSpec(memory_space=pltpu.VMEM)
    return pl.pallas_call(
        output_kernel,
        out_shape=jax.ShapeDtypeStruct(rows.shape, jnp.bfloat16),
        in_specs=[smem, smem] + [vmem] * 6,
        out_specs=vmem,
        compiler_params=PARAMS,
        cost_estimate=pl.CostEstimate(flops=2 * 32 * D * D, bytes_accessed=3 << 20, transcendentals=0),
        name="output",
    )(place, keep, parts, *quads, rows)


def exchange(values, axes):
    return lax.all_to_all(values, axes, split_axis=0, concat_axis=0, tiled=True)


def swap(values, axis):
    return lax.ppermute(values, axis, [(0, 1), (1, 0)])


def go_round(pair):
    quad = jnp.stack([pair, swap(pair, "c")])
    return [quad] + [lax.ppermute(quad, "x", [(i, (i + turns) % 4) for i in range(4)]) for turns in (1, 2, 3)]


def per_device(cand_x, hist_kv, hist_len, cand_count, block_mask, w_proj, w_out):
    own_rows = cand_x.shape[0]
    rows = cand_x.reshape(own_rows, D)
    place = jnp.stack([lax.axis_index("yh"), lax.axis_index("x"), lax.axis_index("c")]).astype(jnp.int32)
    other_rows, other_w = swap(rows, "yh"), swap(w_out, "yh")
    hist_kv, other_rows, other_w = lax.optimization_barrier((hist_kv, other_rows, other_w))
    hist = ("z", "yl")
    bulk = exchange(hist_kv[:, 2 * BLK :], hist)
    bulk, hist_kv, other_rows, other_w = lax.optimization_barrier((bulk, hist_kv, other_rows, other_w))
    rest = exchange(hist_kv[:, : 2 * BLK], hist)

    starts = jnp.arange(block_mask.shape[1], dtype=jnp.int32) * BLK
    live = (jnp.clip(hist_len[0] - starts, 0, BLK) * block_mask[0]).reshape(-1, 4)
    query, gate = project(place, go_round(jnp.stack([rows, other_rows])), w_proj)
    total = attend(live[:, 2:].reshape(-1), cand_count, query, bulk.reshape(-1, 128))
    w_quads = go_round(jnp.stack([w_out, other_w]))
    attended = attend(live[:, :2].reshape(-1), cand_count, query, rest.reshape(-1, 128), total, gate)
    attended, *w_quads = lax.optimization_barrier((attended, *w_quads))
    parts = exchange(attended, GRP)
    keep = cand_count - lax.axis_index(GRP) * own_rows
    return output(place, keep, parts, w_quads, rows).reshape(cand_x.shape)


def solution(mesh):
    split = Mesh(mesh.devices.reshape(2, 4, 2, 8, 4), ("yh", "x", "c", "z", "yl"))
    hist = ("z", "yl")
    in_specs = (
        P(GRP, hist, None),
        P(None, hist, GRP),
        P(hist),
        P(hist),
        P(hist, None),
        P(None, GRP),
        P(GRP, None),
    )
    return jax.shard_map(per_device, mesh=split, in_specs=in_specs, out_specs=P(GRP, hist, None), check_vma=False)
```

time: 206 us -> 170 us (0.83)
  the two profiles are of different devices: /device:TPU:193 before, /device:TPU:25 now
where the time goes in v3:
time: 170 us; the launch traced here: 169 us
  blocking collectives  65.6 us (39%)
  starting transfers between devices  49.3 us (29%)
  waiting for transfers between devices  30.6 us (18%)
  Pallas kernels  14.7 us (9%)
  local copies, waits for them, and re-layouts  5.59 us (3%)
  other arithmetic  1.84 us (1%)
    all_to_all x1, blocking collectives, exchange(): return lax.all_to_all(values, axes, split_axis=0, concat_axis=0, tiled=True)  65.6 us
    all_to_all x2, waiting for transfers between devices, exchange(): return lax.all_to_all(values, axes, split_axis=0, concat_axis=0, tiled=True)  25.5 us
    ppermute x6, starting transfers between devices, go_round(): lax.ppermute(quad, 'x', [(i, (i + turns) % 4) for i in range(4)])  19 us
    ppermute x4, starting transfers between devices, swap(): return lax.ppermute(values, axis, [(0, 1), (1, 0)])  15.1 us
    all_to_all x2, starting transfers between devices, exchange(): return lax.all_to_all(values, axes, split_axis=0, concat_axis=0, tiled=True)  15.1 us
    pallas_call x1, Pallas kernels, attend(): pl.pallas_call(attend_last_kernel, out_shape=jax.ShapeDtypeStruct((count...  5.38 us
    ppermute x4, waiting for transfers between devices, swap(): return lax.ppermute(values, axis, [(0, 1), (1, 0)])  5.1 us
    pallas_call x1, Pallas kernels, attend(): pl.pallas_call(attend_first_kernel, out_shape=jax.ShapeDtypeStruct((count...  4.64 us
  transfers between devices with their start and end apart: 12, of which 3 were waited for; matrix products, arithmetic and copies ran while one was open for 2% of the time, Pallas kernels for 7%

profile of v3, /device:TPU:25, one launch (start us, length us, event | category | flops | bytes accessed | tf_op | source)
XLA Modules:
  0.0 169.1 jit_solution(5485473163453784579)
XLA Ops:
  0.0 4.7 %collective-permute-start.1 = (bf16[64,1024]{1,0:T(8,128)(2,1)}, bf16[64,1024]{1,0:T(8,128)(2,1)S(1)}, u32[]{:S(2)}, u32[]{:S(2)}) collective-permute-start(bf16[64,1024]{1,0:T(8,128)(2,1)} %param.13), channel_id=1, source_target_pairs={{0,256},{256,0},{1,257},{257,1},{2,258},{258,2},{3,259},{259,3},{4... | collective-permute-start | bytes 393224 | tf_op jit(solution)/shard_map/ppermute | solution.py:204
  4.8 0.0 slice-start
  4.8 4.6 %collective-permute-start = (bf16[32,1024]{1,0:T(8,128)(2,1)}, bf16[32,1024]{1,0:T(8,128)(2,1)S(1)}, u32[]{:S(2)}, u32[]{:S(2)}) collective-permute-start(bf16[32,1024]{1,0:T(8,128)(2,1)} %bitcast.22), channel_id=1, source_target_pairs={{0,256},{256,0},{1,257},{257,1},{2,258},{258,2},{3,259},{259,3},{4... | collective-permute-start | bytes 196616 | tf_op jit(solution)/shard_map/ppermute | solution.py:204
  9.3 5.1 %collective-permute-done = bf16[32,1024]{1,0:T(8,128)(2,1)S(1)} collective-permute-done((bf16[32,1024]{1,0:T(8,128)(2,1)}, bf16[32,1024]{1,0:T(8,128)(2,1)S(1)}, u32[]{:S(2)}, u32[]{:S(2)}) %collective-permute-start) | collective-permute-done | bytes 65568 | tf_op jit(solution)/shard_map/ppermute | solution.py:204
  14.4 0.0 collective-permute-done.1
  14.4 0.0 slice-done
  14.4 65.6 %all_to_all.15 = bf16[32,256,128]{2,1,0:T(8,128)(2,1)} all-to-all(bf16[32,256,128]{2,1,0:T(8,128)(2,1)S(1)} %slice-done), channel_id=1, replica_groups=mesh['yh'=2,'x'=4,'c'=2,'z'=8,'yl'=4] {'z','yl'}, dimensions={0} | all-to-all | bytes 4194304 | tf_op jit(solution)/shard_map/all_to_all | solution.py:200
  80.0 0.0 copy-done.5
  80.0 1.5 slice.14
  81.5 7.1 %all-to-all-start.1 = ((bf16[32,256,128]{2,1,0:T(8,128)(2,1)}), bf16[32,256,128]{2,1,0:T(8,128)(2,1)S(1)}, u32[]{:S(2)}, u32[]{:S(2)}) async-start(bf16[32,256,128]{2,1,0:T(8,128)(2,1)} %slice.14), calls=%async_computation.1 | async-start | bytes 4194304 | tf_op jit(solution)/shard_map/all_to_all | solution.py:200
  88.6 0.5 broadcast.9
  89.1 0.0 copy-done.8
  89.1 0.7 reduce.3
  89.7 0.1 squeeze.7
  90.5 0.0 copy-done.2
  90.5 3.9 %collective-permute-start.2 = (bf16[2,32,1024]{2,1,0:T(8,128)(2,1)S(1)}, bf16[2,32,1024]{2,1,0:T(8,128)(2,1)S(1)}, u32[]{:S(2)}, u32[]{:S(2)}) collective-permute-start(bf16[2,32,1024]{2,1,0:T(8,128)(2,1)S(1)} %get-tuple-element.36), channel_id=1, source_target_pairs={{0,32},{32,0},{1,33},{33,1},{2,34},{34,2},{3,35},{35,3},{4,36},{36... | collective-permute-start | bytes 393224 | tf_op jit(solution)/shard_map/ppermute | solution.py:204
  94.5 1.9 %collective-permute-start.6 = (bf16[2,64,1024]{2,1,0:T(8,128)(2,1)S(1)}, bf16[2,64,1024]{2,1,0:T(8,128)(2,1)S(1)}, u32[]{:S(2)}, u32[]{:S(2)}) collective-permute-start(bf16[2,64,1024]{2,1,0:T(8,128)(2,1)S(1)} %get-tuple-element.34), channel_id=1, source_target_pairs={{0,32},{32,0},{1,33},{33,1},{2,34},{34,2},{3,35},{35,3},{4,36},{36... | collective-permute-start | bytes 786440 | tf_op jit(solution)/shard_map/ppermute | solution.py:204
  96.5 0.0 collective-permute-done.2
  96.5 3.1 %collective-permute-start.3 = (bf16[2,2,32,1024]{3,2,1,0:T(8,128)(2,1)S(1)}, bf16[2,2,32,1024]{3,2,1,0:T(8,128)(2,1)}, u32[]{:S(2)}, u32[]{:S(2)}) collective-permute-start(bf16[2,2,32,1024]{3,2,1,0:T(8,128)(2,1)S(1)} %pad_maximum_fusion.1.refs_0_), channel_id=1, source_target_pairs={{0,64},{64,128},{128,192},{192,0},{1,65},{65,129},{129,193},{193,1... | collective-permute-start | bytes 786440 | tf_op jit(solution)/shard_map/ppermute | solution.py:209
  99.7 4.4 %collective-permute-start.4 = (bf16[2,2,32,1024]{3,2,1,0:T(8,128)(2,1)S(1)}, bf16[2,2,32,1024]{3,2,1,0:T(8,128)(2,1)}, u32[]{:S(2)}, u32[]{:S(2)}) collective-permute-start(bf16[2,2,32,1024]{3,2,1,0:T(8,128)(2,1)S(1)} %pad_maximum_fusion.1.refs_0_), channel_id=1, source_target_pairs={{0,128},{64,192},{128,0},{192,64},{1,129},{65,193},{129,1},{193,65... | collective-permute-start | bytes 786440 | tf_op jit(solution)/shard_map/ppermute | solution.py:209
  104.0 3.1 %collective-permute-start.5 = (bf16[2,2,32,1024]{3,2,1,0:T(8,128)(2,1)S(1)}, bf16[2,2,32,1024]{3,2,1,0:T(8,128)(2,1)}, u32[]{:S(2)}, u32[]{:S(2)}) collective-permute-start(bf16[2,2,32,1024]{3,2,1,0:T(8,128)(2,1)S(1)} %pad_maximum_fusion.1.refs_0_), channel_id=1, source_target_pairs={{0,192},{64,0},{128,64},{192,128},{1,193},{65,1},{129,65},{193,129... | collective-permute-start | bytes 786440 | tf_op jit(solution)/shard_map/ppermute | solution.py:209
  107.1 0.1 fusion.2
  107.8 0.1 reshape.24.live_ref
  107.9 0.1 reshape.21.live_ref
  108.0 0.0 collective-permute-done.6
  108.0 0.0 copy-start.6
  108.1 0.7 copy-done.6
  108.8 1.0 pad_maximum_fusion.refs_0_
  109.8 2.2 %collective-permute-start.7 = (bf16[2,2,64,1024]{3,2,1,0:T(8,128)(2,1)S(1)}, bf16[2,2,64,1024]{3,2,1,0:T(8,128)(2,1)S(1)}, u32[]{:S(2)}, u32[]{:S(2)}) collective-permute-start(bf16[2,2,64,1024]{3,2,1,0:T(8,128)(2,1)S(1)} %pad_maximum_fusion.refs_0_), channel_id=1, source_target_pairs={{0,64},{64,128},{128,192},{192,0},{1,65},{65,129},{129,193},{193,1... | collective-permute-start | bytes 1572872 | tf_op jit(solution)/shard_map/ppermute | solution.py:209
  112.0 2.8 %collective-permute-start.8 = (bf16[2,2,64,1024]{3,2,1,0:T(8,128)(2,1)S(1)}, bf16[2,2,64,1024]{3,2,1,0:T(8,128)(2,1)}, u32[]{:S(2)}, u32[]{:S(2)}) collective-permute-start(bf16[2,2,64,1024]{3,2,1,0:T(8,128)(2,1)S(1)} %pad_maximum_fusion.refs_0_), channel_id=1, source_target_pairs={{0,128},{64,192},{128,0},{192,64},{1,129},{65,193},{129,1},{193,65... | collective-permute-start | bytes 1572872 | tf_op jit(solution)/shard_map/ppermute | solution.py:209
  114.8 0.0 collective-permute-done.3.refs_1_
  114.8 3.4 %collective-permute-start.9 = (bf16[2,2,64,1024]{3,2,1,0:T(8,128)(2,1)S(1)}, bf16[2,2,64,1024]{3,2,1,0:T(8,128)(2,1)}, u32[]{:S(2)}, u32[]{:S(2)}) collective-permute-start(bf16[2,2,64,1024]{3,2,1,0:T(8,128)(2,1)S(1)} %pad_maximum_fusion.refs_0_), channel_id=1, source_target_pairs={{0,192},{64,0},{128,64},{192,128},{1,193},{65,1},{129,65},{193,129... | collective-permute-start | bytes 1572872 | tf_op jit(solution)/shard_map/ppermute | solution.py:209
  118.2 0.1 pad_add_fusion.place_ref
  118.3 0.0 collective-permute-done.4.refs_2_
  118.3 0.0 collective-permute-done.5.refs_3_
  118.3 0.9 copy-done.1
  119.3 2.2 %project.1 = (bf16[512,128]{1,0:T(8,128)(2,1)S(1)}, bf16[16,16,128]{2,1,0:T(8,128)(2,1)S(1)}) custom-call(s32[3]{0:T(128)S(1)} %pad_add_fusion.place_ref, bf16[2,2,32,1024]{3,2,1,0:T(8,128)(2,1)S(1)} %pad_maximum_fusion.1.refs_0_, bf16[2,2,32,1024]{3,2,1,0:T(8,128)(2,1)} %collective-permute-done.3.refs_1_, ...), custom_call_target="tpu_custom_call" | custom-call | flops 134217728 | bytes 2097152 | tf_op jit(solution)/shard_map/project/pallas_call | solution.py:60
  121.4 4.6 %attend_first.1.before_ref = f32[512,128]{1,0:T(8,128)S(1)} custom-call(s32[64]{0:T(128)S(1)} %reshape.24.live_ref, s32[1]{0:T(128)S(6)} %copy.9.count_ref, bf16[512,128]{1,0:T(8,128)(2,1)S(1)} %get-tuple-element.23.query_ref, bf16[8192,128]{1,0:T(8,128)(2,1)S(1)} %bitcast.21), custom_call_target="tpu_custom_call" | custom-call | flops 2147483648 | bytes 2097152 | tf_op jit(solution)/shard_map/attend_first/pallas_call | solution.py:135
  126.1 0.6 copy-done.3
  126.7 15.5 %all-to-all-done.1 = bf16[32,256,128]{2,1,0:T(8,128)(2,1)S(1)} async-done(((bf16[32,256,128]{2,1,0:T(8,128)(2,1)}), bf16[32,256,128]{2,1,0:T(8,128)(2,1)S(1)}, u32[]{:S(2)}, u32[]{:S(2)}) %all-to-all-start.1) | async-done | bytes 2097184 | tf_op jit(solution)/shard_map/all_to_all | solution.py:200
  142.2 0.9 copy-done.4
  143.1 5.4 %attend_last.1 = bf16[16,32,128]{2,1,0:T(8,128)(2,1)} custom-call(s32[64]{0:T(128)S(1)} %reshape.21.live_ref, s32[1]{0:T(128)S(6)} %copy.9.count_ref, bf16[512,128]{1,0:T(8,128)(2,1)S(1)} %copy-done.4, bf16[8192,128]{1,0:T(8,128)(2,1)S(1)} %bitcast.20, f32[512,128]{1,0:T(8,128)S(1)} %attend_first.1.before_ref, ...), custom_call_target="tpu_custom_call" | custom-call | flops 2147483648 | bytes 2097152 | tf_op jit(solution)/shard_map/attend_last/pallas_call | solution.py:144
  148.5 0.0 collective-permute-done.7.refs_1_
  148.5 0.0 collective-permute-done.8.refs_2_
  148.5 0.0 collective-permute-done.9.refs_3_
  148.5 8.1 %all-to-all-start.2 = ((bf16[16,32,128]{2,1,0:T(8,128)(2,1)}), bf16[16,32,128]{2,1,0:T(8,128)(2,1)S(1)}, u32[]{:S(2)}, u32[]{:S(2)}) async-start(bf16[16,32,128]{2,1,0:T(8,128)(2,1)} %attend_last.1), calls=%async_computation.2 | async-start | bytes 262144 | tf_op jit(solution)/shard_map/all_to_all | solution.py:200
  156.6 10.1 %all-to-all-done.2.parts_ref = bf16[16,32,128]{2,1,0:T(8,128)(2,1)S(1)} async-done(((bf16[16,32,128]{2,1,0:T(8,128)(2,1)}), bf16[16,32,128]{2,1,0:T(8,128)(2,1)S(1)}, u32[]{:S(2)}, u32[]{:S(2)}) %all-to-all-start.2) | async-done | bytes 131104 | tf_op jit(solution)/shard_map/all_to_all | solution.py:200
  166.6 2.5 %output.1 = bf16[32,1024]{1,0:T(8,128)(2,1)} custom-call(s32[3]{0:T(128)S(1)} %pad_add_fusion.place_ref, s32[1]{0:T(128)S(6)} %sub.14.count_ref, bf16[16,32,128]{2,1,0:T(8,128)(2,1)S(1)} %all-to-all-done.2.parts_ref, bf16[2,2,64,1024]{3,2,1,0:T(8,128)(2,1)S(1)} %pad_maximum_fusion.refs_0_, bf16[2,2,64,1024]{3,2,1,0:T(8,128)(2,1)S(1)} %collective-permute-done.7.refs_1_, ...), custom_call_target="tpu_custom_call" | custom-call | flops 67108864 | bytes 3145728 | tf_op jit(solution)/shard_map/output/pallas_call | solution.py:188
  (14 shorter events, 0.1 us)
Async XLA Ops:
  0.0 14.4 %collective-permute-start.1 = (bf16[64,1024]{1,0:T(8,128)(2,1)}, bf16[64,1024]{1,0:T(8,128)(2,1)S(1)}, u32[]{:S(2)}, u32[]{:S(2)}) collective-permute-start(bf16[64,1024]{1,0:T(8,128)(2,1)} %param.13), channel_id=1, source_target_pairs={{0,256},{256,0},{1,257},{257,1},{2,258},{258,2},{3,259},{259,3},{4... | collective-permute-start | bytes 393224 | tf_op jit(solution)/shard_map/ppermute | solution.py:204
  4.8 9.7 %slice-start = ((bf16[32,512,128]{2,1,0:T(8,128)(2,1)}), bf16[32,256,128]{2,1,0:T(8,128)(2,1)S(1)}, s32[]{:S(2)}) async-start(bf16[32,512,128]{2,1,0:T(8,128)(2,1)} %param.8), calls=%async_computation.3 | async-start | bytes 4194304 | tf_op jit(solution)/shard_map/slice | solution.py:219
  4.8 9.7 %collective-permute-start = (bf16[32,1024]{1,0:T(8,128)(2,1)}, bf16[32,1024]{1,0:T(8,128)(2,1)S(1)}, u32[]{:S(2)}, u32[]{:S(2)}) collective-permute-start(bf16[32,1024]{1,0:T(8,128)(2,1)} %bitcast.22), channel_id=1, source_target_pairs={{0,256},{256,0},{1,257},{257,1},{2,258},{258,2},{3,259},{259,3},{4... | collective-permute-start | bytes 196616 | tf_op jit(solution)/shard_map/ppermute | solution.py:204
  14.4 65.6 %copy-start.5 = (bf16[32,512,128]{2,1,0:T(8,128)(2,1)S(1)}, bf16[32,512,128]{2,1,0:T(8,128)(2,1)}, u32[]{:S(2)}) copy-start(bf16[32,512,128]{2,1,0:T(8,128)(2,1)} %param.8) | copy-start | bytes 12582916
  81.5 7.6 %copy-start.8 = (s32[1,128]{1,0:T(1,128)S(1)}, s32[1,128]{1,0:T(1,128)}, u32[]{:S(2)}) copy-start(s32[1,128]{1,0:T(1,128)} %param.11) | copy-start | bytes 1540
  81.5 9.0 %copy-start.2 = (bf16[32,1,1024]{2,0,1:T(8,128)(2,1)S(1)}, bf16[32,1,1024]{2,0,1:T(8,128)(2,1)}, u32[]{:S(2)}) copy-start(bf16[32,1,1024]{2,0,1:T(8,128)(2,1)} %param.7) | copy-start | bytes 196612
  81.5 13.0 %copy-start.7 = (bf16[64,1024]{1,0:T(8,128)(2,1)S(1)}, bf16[64,1024]{1,0:T(8,128)(2,1)}, u32[]{:S(2)}) copy-start(bf16[64,1024]{1,0:T(8,128)(2,1)} %param.13) | copy-start | bytes 393220
  81.5 60.7 %all-to-all-start.1 = ((bf16[32,256,128]{2,1,0:T(8,128)(2,1)}), bf16[32,256,128]{2,1,0:T(8,128)(2,1)S(1)}, u32[]{:S(2)}, u32[]{:S(2)}) async-start(bf16[32,256,128]{2,1,0:T(8,128)(2,1)} %slice.14), calls=%async_computation.1 | async-start | bytes 4194304 | tf_op jit(solution)/shard_map/all_to_all | solution.py:200
  90.5 5.9 %collective-permute-start.2 = (bf16[2,32,1024]{2,1,0:T(8,128)(2,1)S(1)}, bf16[2,32,1024]{2,1,0:T(8,128)(2,1)S(1)}, u32[]{:S(2)}, u32[]{:S(2)}) collective-permute-start(bf16[2,32,1024]{2,1,0:T(8,128)(2,1)S(1)} %get-tuple-element.36), channel_id=1, source_target_pairs={{0,32},{32,0},{1,33},{33,1},{2,34},{34,2},{3,35},{35,3},{4,36},{36... | collective-permute-start | bytes 393224 | tf_op jit(solution)/shard_map/ppermute | solution.py:204
  94.5 13.5 %collective-permute-start.6 = (bf16[2,64,1024]{2,1,0:T(8,128)(2,1)S(1)}, bf16[2,64,1024]{2,1,0:T(8,128)(2,1)S(1)}, u32[]{:S(2)}, u32[]{:S(2)}) collective-permute-start(bf16[2,64,1024]{2,1,0:T(8,128)(2,1)S(1)} %get-tuple-element.34), channel_id=1, source_target_pairs={{0,32},{32,0},{1,33},{33,1},{2,34},{34,2},{3,35},{35,3},{4,36},{36... | collective-permute-start | bytes 786440 | tf_op jit(solution)/shard_map/ppermute | solution.py:204
  96.5 18.3 %collective-permute-start.3 = (bf16[2,2,32,1024]{3,2,1,0:T(8,128)(2,1)S(1)}, bf16[2,2,32,1024]{3,2,1,0:T(8,128)(2,1)}, u32[]{:S(2)}, u32[]{:S(2)}) collective-permute-start(bf16[2,2,32,1024]{3,2,1,0:T(8,128)(2,1)S(1)} %pad_maximum_fusion.1.refs_0_), channel_id=1, source_target_pairs={{0,64},{64,128},{128,192},{192,0},{1,65},{65,129},{129,193},{193,1... | collective-permute-start | bytes 786440 | tf_op jit(solution)/shard_map/ppermute | solution.py:209
  99.7 18.7 %collective-permute-start.4 = (bf16[2,2,32,1024]{3,2,1,0:T(8,128)(2,1)S(1)}, bf16[2,2,32,1024]{3,2,1,0:T(8,128)(2,1)}, u32[]{:S(2)}, u32[]{:S(2)}) collective-permute-start(bf16[2,2,32,1024]{3,2,1,0:T(8,128)(2,1)S(1)} %pad_maximum_fusion.1.refs_0_), channel_id=1, source_target_pairs={{0,128},{64,192},{128,0},{192,64},{1,129},{65,193},{129,1},{193,65... | collective-permute-start | bytes 786440 | tf_op jit(solution)/shard_map/ppermute | solution.py:209
  104.0 14.3 %collective-permute-start.5 = (bf16[2,2,32,1024]{3,2,1,0:T(8,128)(2,1)S(1)}, bf16[2,2,32,1024]{3,2,1,0:T(8,128)(2,1)}, u32[]{:S(2)}, u32[]{:S(2)}) collective-permute-start(bf16[2,2,32,1024]{3,2,1,0:T(8,128)(2,1)S(1)} %pad_maximum_fusion.1.refs_0_), channel_id=1, source_target_pairs={{0,192},{64,0},{128,64},{192,128},{1,193},{65,1},{129,65},{193,129... | collective-permute-start | bytes 786440 | tf_op jit(solution)/shard_map/ppermute | solution.py:209
  108.0 13.4 %copy-start = (bf16[32,256,128]{2,1,0:T(8,128)(2,1)S(1)}, bf16[32,256,128]{2,1,0:T(8,128)(2,1)}, u32[]{:S(2)}) copy-start(bf16[32,256,128]{2,1,0:T(8,128)(2,1)} %all_to_all.15) | copy-start | bytes 6291460
  108.0 0.7 copy-start.6
  109.8 38.7 %collective-permute-start.7 = (bf16[2,2,64,1024]{3,2,1,0:T(8,128)(2,1)S(1)}, bf16[2,2,64,1024]{3,2,1,0:T(8,128)(2,1)S(1)}, u32[]{:S(2)}, u32[]{:S(2)}) collective-permute-start(bf16[2,2,64,1024]{3,2,1,0:T(8,128)(2,1)S(1)} %pad_maximum_fusion.refs_0_), channel_id=1, source_target_pairs={{0,64},{64,128},{128,192},{192,0},{1,65},{65,129},{129,193},{193,1... | collective-permute-start | bytes 1572872 | tf_op jit(solution)/shard_map/ppermute | solution.py:209
  112.0 36.5 %collective-permute-start.8 = (bf16[2,2,64,1024]{3,2,1,0:T(8,128)(2,1)S(1)}, bf16[2,2,64,1024]{3,2,1,0:T(8,128)(2,1)}, u32[]{:S(2)}, u32[]{:S(2)}) collective-permute-start(bf16[2,2,64,1024]{3,2,1,0:T(8,128)(2,1)S(1)} %pad_maximum_fusion.refs_0_), channel_id=1, source_target_pairs={{0,128},{64,192},{128,0},{192,64},{1,129},{65,193},{129,1},{193,65... | collective-permute-start | bytes 1572872 | tf_op jit(solution)/shard_map/ppermute | solution.py:209
  114.8 33.7 %collective-permute-start.9 = (bf16[2,2,64,1024]{3,2,1,0:T(8,128)(2,1)S(1)}, bf16[2,2,64,1024]{3,2,1,0:T(8,128)(2,1)}, u32[]{:S(2)}, u32[]{:S(2)}) collective-permute-start(bf16[2,2,64,1024]{3,2,1,0:T(8,128)(2,1)S(1)} %pad_maximum_fusion.refs_0_), channel_id=1, source_target_pairs={{0,192},{64,0},{128,64},{192,128},{1,193},{65,1},{129,65},{193,129... | collective-permute-start | bytes 1572872 | tf_op jit(solution)/shard_map/ppermute | solution.py:209
  118.3 1.0 copy-start.1
  126.1 0.7 copy-start.3
  142.2 0.9 copy-start.4
  148.5 18.1 %all-to-all-start.2 = ((bf16[16,32,128]{2,1,0:T(8,128)(2,1)}), bf16[16,32,128]{2,1,0:T(8,128)(2,1)S(1)}, u32[]{:S(2)}, u32[]{:S(2)}) async-start(bf16[16,32,128]{2,1,0:T(8,128)(2,1)} %attend_last.1), calls=%async_computation.2 | async-start | bytes 262144 | tf_op jit(solution)/shard_map/all_to_all | solution.py:200

commit v4 on v3

--- a/solution.py
+++ b/solution.py
@@ -10,8 +10,8 @@
 
 D = 1024
 BLK = 128
-TILE = 2048
-CHUNKS = ((0, 256), (256, 384), (384, 512))
+FINE = 128
+FIRST = 256
 GRP = ("yh", "x", "c")
 HALF = 64
 PARAMS = pltpu.CompilerParams(vmem_limit_bytes=24 * 1024 * 1024)
@@ -71,61 +71,86 @@
     )(place, *quads, w_proj)
 
 
-def attend_tiles(live_ref, count_ref, query_ref, kv_ref, total, masked):
+def attend_tiles(offset, length_ref, mask_ref, count_ref, query_ref, kv_ref, total, masked):
     step = pl.program_id(0)
-    blocks = kv_ref.shape[0] // BLK
-    lives = [live_ref[step * blocks + i] for i in range(blocks)]
-
-    @pl.when(functools.reduce(jnp.add, lives) > 0)
-    def _():
-        row = lax.broadcasted_iota(jnp.int32, (BLK, 128), 0)
-        for i in range(blocks):
-            block = kv_ref[i * BLK : (i + 1) * BLK]
-            masked[i * BLK : (i + 1) * BLK] = jnp.where(row < lives[i], block, jnp.zeros_like(block))
-        for start, end in CHUNKS:
-
-            @pl.when(count_ref[0] > start)
-            def _():
-                scores = lax.dot_general(
-                    query_ref[start:end], masked[...], (((1,), (1,)), ((), ())), preferred_element_type=jnp.float32
-                )
-                weights = (scores + scores * jnp.tanh(scores)).astype(jnp.bfloat16)
-                total[start:end] += jnp.dot(weights, masked[...], preferred_element_type=jnp.float32)
-
-
-def attend_first_kernel(live_ref, count_ref, query_ref, kv_ref, total, masked):
+    sources, rows, _ = kv_ref.shape
+    lives = []
+    for source in range(sources):
+        for block in range(rows // FINE):
+            position = (step * sources + source) * 512 + offset + block * FINE
+            count = jnp.clip(length_ref[0] - position, 0, FINE)
+            lives.append(count * mask_ref[0, (step * sources + source) * 4 + (offset + block * FINE) // BLK])
+
+    def attend_rows(chunks):
+        row = lax.broadcasted_iota(jnp.int32, (FINE, 128), 0)
+        for i, live in enumerate(lives):
+            source, block = divmod(i, rows // FINE)
+            piece = kv_ref[source, block * FINE : (block + 1) * FINE]
+            masked[i * FINE : (i + 1) * FINE] = jnp.where(row < live, piece, jnp.zeros_like(piece))
+        for start, end in chunks:
+            scores = lax.dot_general(
+                query_ref[start:end], masked[...], (((1,), (1,)), ((), ())), preferred_element_type=jnp.float32
+            )
+            weights = (scores + scores * jnp.tanh(scores)).astype(jnp.bfloat16)
+            total[start:end] += jnp.dot(weights, masked[...], preferred_element_type=jnp.float32)
+
+    some = functools.reduce(jnp.add, lives) > 0
+    few = count_ref[0] <= 384
+
+    @pl.when(jnp.logical_and(some, few))
+    def _():
+        attend_rows(((0, 256), (256, 384)))
+
+    @pl.when(jnp.logical_and(some, jnp.logical_not(few)))
+    def _():
+        attend_rows(((0, 256), (256, 512)))
+
+
+def attend_first_kernel(offset, length_ref, mask_ref, count_ref, query_ref, kv_ref, total, masked):
     @pl.when(pl.program_id(0) == 0)
     def _():
         total[...] = jnp.zeros_like(total)
 
-    attend_tiles(live_ref, count_ref, query_ref, kv_ref, total, masked)
-
-
-def attend_last_kernel(live_ref, count_ref, query_ref, kv_ref, before_ref, gate_ref, out_ref, total, masked):
+    attend_tiles(offset, length_ref, mask_ref, count_ref, query_ref, kv_ref, total, masked)
+
+
+def attend_last_kernel(
+    offset, length_ref, mask_ref, count_ref, query_ref, kv_ref, before_ref, gate_ref, out_ref, total, masked
+):
     @pl.when(pl.program_id(0) == 0)
     def _():
         total[...] = before_ref[...]
 
-    attend_tiles(live_ref, count_ref, query_ref, kv_ref, total, masked)
+    attend_tiles(offset, length_ref, mask_ref, count_ref, query_ref, kv_ref, total, masked)
 
     @pl.when(pl.program_id(0) == pl.num_programs(0) - 1)
     def _():
         slices = total[...].reshape(out_ref.shape[0], 2, 16, 128)
         first, second = slices[:, 0], slices[:, 1]
         turned = pltpu.roll(first.reshape(-1, 128), HALF, 1).reshape(first.shape)
-        out_ref[:, 0:16, :] = jnp.where(low_lanes(first.shape), turned, second).astype(jnp.bfloat16)
-        out_ref[:, 16:32, :] = gate_ref[...]
-
-
-def attend(live, cand_count, query, kv, before=None, gate=None):
+        packed = jnp.where(low_lanes(first.shape), turned, second)
+        high = packed.astype(jnp.bfloat16)
+        out_ref[:, 0:16, :] = high
+        out_ref[:, 16:32, :] = (packed - high.astype(jnp.float32)).astype(jnp.bfloat16)
+        out_ref[:, 32:48, :] = gate_ref[...]
+
+
+def attend(offset, sources, length, mask, cand_count, query, kv, before=None, gate=None):
     count = query.shape[0]
-    positions = kv.shape[0]
+    devices, rows, _ = kv.shape
     smem = pl.BlockSpec(memory_space=pltpu.SMEM)
-    in_specs = [smem, smem, pl.BlockSpec((count, 128), lambda i: (0, 0)), pl.BlockSpec((TILE, 128), lambda i: (i, 0))]
-    masked = pltpu.VMEM((TILE, 128), jnp.bfloat16)
+    in_specs = [
+        smem,
+        smem,
+        smem,
+        pl.BlockSpec((count, 128), lambda i: (0, 0)),
+        pl.BlockSpec((sources, rows, 128), lambda i: (i, 0, 0)),
+    ]
+    masked = pltpu.VMEM((sources * rows, 128), jnp.bfloat16)
     running = pltpu.VMEM((count, 128), jnp.float32)
+    positions = devices * rows
     common = dict(
-        grid=(positions // TILE,),
+        grid=(devices // sources,),
         compiler_params=PARAMS,
         cost_estimate=pl.CostEstimate(
             flops=4 * count * positions * 128, bytes_accessed=positions * 256, transcendentals=count * positions
@@ -133,24 +158,24 @@
     )
     if before is None:
         return pl.pallas_call(
-            attend_first_kernel,
+            functools.partial(attend_first_kernel, offset),
             out_shape=jax.ShapeDtypeStruct((count, 128), jnp.float32),
             in_specs=in_specs,
             out_specs=pl.BlockSpec((count, 128), lambda i: (0, 0)),
             scratch_shapes=[masked],
             name="attend_first",
             **common,
-        )(live, cand_count, query, kv)
+        )(length, mask, cand_count, query, kv)
     return pl.pallas_call(
-        attend_last_kernel,
-        out_shape=jax.ShapeDtypeStruct((count // 32, 32, 128), jnp.bfloat16),
+        functools.partial(attend_last_kernel, offset),
+        out_shape=jax.ShapeDtypeStruct((count // 32, 48, 128), jnp.bfloat16),
         in_specs=in_specs
         + [pl.BlockSpec((count, 128), lambda i: (0, 0)), pl.BlockSpec((count // 32, 16, 128), lambda i: (0, 0, 0))],
-        out_specs=pl.BlockSpec((count // 32, 32, 128), lambda i: (0, 0, 0)),
+        out_specs=pl.BlockSpec((count // 32, 48, 128), lambda i: (0, 0, 0)),
         scratch_shapes=[running, masked],
         name="attend_last",
         **common,
-    )(live, cand_count, query, kv, before, gate)
+    )(length, mask, cand_count, query, kv, before, gate)
 
 
 def spread_heads(packed):
@@ -171,8 +196,8 @@
         for core in range(2):
             for half in range(2):
                 part = parts_ref[member(place_ref, turns, core, half)].astype(jnp.float32)
-                attended.append(part[0:16])
-                gate.append(part[16:32])
+                attended.append(part[0:16] + part[16:32])
+                gate.append(part[32:48])
     gated = (layer_norm(spread_heads(attended)) * spread_heads(gate)).astype(jnp.bfloat16)
     mixed = x_ref[...].astype(jnp.float32)
     for turns, quad in enumerate(quads):
@@ -214,21 +239,21 @@
     rows = cand_x.reshape(own_rows, D)
     place = jnp.stack([lax.axis_index("yh"), lax.axis_index("x"), lax.axis_index("c")]).astype(jnp.int32)
     other_rows, other_w = swap(rows, "yh"), swap(w_out, "yh")
-    hist_kv, other_rows, other_w = lax.optimization_barrier((hist_kv, other_rows, other_w))
+    first, second, other_rows, other_w = lax.optimization_barrier(
+        (hist_kv[:, :FIRST], hist_kv[:, FIRST:], other_rows, other_w)
+    )
     hist = ("z", "yl")
-    bulk = exchange(hist_kv[:, 2 * BLK :], hist)
-    bulk, hist_kv, other_rows, other_w = lax.optimization_barrier((bulk, hist_kv, other_rows, other_w))
-    rest = exchange(hist_kv[:, : 2 * BLK], hist)
-
-    starts = jnp.arange(block_mask.shape[1], dtype=jnp.int32) * BLK
-    live = (jnp.clip(hist_len[0] - starts, 0, BLK) * block_mask[0]).reshape(-1, 4)
+    bulk = exchange(first, hist)
+    bulk, second, other_rows, other_w = lax.optimization_barrier((bulk, second, other_rows, other_w))
+    rest = exchange(second, hist)
+
+    limits = (hist_len, block_mask, cand_count)
     query, gate = project(place, go_round(jnp.stack([rows, other_rows])), w_proj)
-    total = attend(live[:, 2:].reshape(-1), cand_count, query, bulk.reshape(-1, 128))
+    total = attend(0, 8, *limits, query, bulk)
     w_quads = go_round(jnp.stack([w_out, other_w]))
-    attended = attend(live[:, :2].reshape(-1), cand_count, query, rest.reshape(-1, 128), total, gate)
-    attended, *w_quads = lax.optimization_barrier((attended, *w_quads))
+    attended = attend(FIRST, 8, *limits, query, rest, total, gate)
+    keep = cand_count - lax.axis_index(GRP) * own_rows
     parts = exchange(attended, GRP)
-    keep = cand_count - lax.axis_index(GRP) * own_rows
     return output(place, keep, parts, w_quads, rows).reshape(cand_x.shape)
 
 

time: 170 us -> 168 us (0.988)
  the two profiles are of different devices: /device:TPU:25 before, /device:TPU:80 now
where the time goes in v4:
time: 168 us
  blocking collectives  60.6 us (36%)
  starting transfers between devices  49.6 us (30%)
  waiting for transfers between devices  38.9 us (23%)
  Pallas kernels  9.97 us (6%)
  local copies, waits for them, and re-layouts  6.59 us (4%)
  between operations  1.72 us (1%)
    all_to_all x1, blocking collectives, exchange(): return lax.all_to_all(values, axes, split_axis=0, concat_axis=0, tiled=True)  60.6 us
    all_to_all x2, waiting for transfers between devices, exchange(): return lax.all_to_all(values, axes, split_axis=0, concat_axis=0, tiled=True)  33 us
    ppermute x6, starting transfers between devices, go_round(): lax.ppermute(quad, 'x', [(i, (i + turns) % 4) for i in range(4)])  20.4 us
    all_to_all x2, starting transfers between devices, exchange(): return lax.all_to_all(values, axes, split_axis=0, concat_axis=0, tiled=True)  15.1 us
    ppermute x4, starting transfers between devices, swap(): return lax.ppermute(values, axis, [(0, 1), (1, 0)])  14.1 us
    ppermute x4, waiting for transfers between devices, swap(): return lax.ppermute(values, axis, [(0, 1), (1, 0)])  5.9 us
    slice x1, local copies, waits for them, and re-layouts, per_device(): hist_kv[:, FIRST:]  4.07 us
  transfers between devices with their start and end apart: 12, of which 3 were waited for; matrix products, arithmetic and copies ran while one was open for 3% of the time, Pallas kernels for 4%

profile of v4, /device:TPU:80, one launch (start us, length us, event | category | flops | bytes accessed | tf_op | source)
XLA Modules:
  0.0 167.6 jit_solution(8744126667481687034)
XLA Ops:
  0.0 5.9 %collective-permute-start = (bf16[32,1024]{1,0:T(8,128)(2,1)}, bf16[32,1024]{1,0:T(8,128)(2,1)S(1)}, u32[]{:S(2)}, u32[]{:S(2)}) collective-permute-start(bf16[32,1024]{1,0:T(8,128)(2,1)} %bitcast.16), channel_id=1, source_target_pairs={{0,256},{256,0},{1,257},{257,1},{2,258},{258,2},{3,259},{259,3},{4... | collective-permute-start | bytes 196616 | tf_op jit(solution)/shard_map/ppermute | solution.py:229
  5.9 3.8 %collective-permute-start.1 = (bf16[64,1024]{1,0:T(8,128)(2,1)}, bf16[64,1024]{1,0:T(8,128)(2,1)S(1)}, u32[]{:S(2)}, u32[]{:S(2)}) collective-permute-start(bf16[64,1024]{1,0:T(8,128)(2,1)} %param.13), channel_id=1, source_target_pairs={{0,256},{256,0},{1,257},{257,1},{2,258},{258,2},{3,259},{259,3},{4... | collective-permute-start | bytes 393224 | tf_op jit(solution)/shard_map/ppermute | solution.py:229
  9.8 4.1 %fusion.2 = (bf16[32,256,128]{2,1,0:T(8,128)(2,1)}, bf16[32,256,128]{2,1,0:T(8,128)(2,1)S(1)}) fusion(bf16[32,512,128]{2,1,0:T(8,128)(2,1)} %param.8), kind=kLoop, calls=%fused_computation.7 | loop fusion | bytes 8388608 | tf_op jit(solution)/shard_map/slice | solution.py:243
  13.8 0.0 collective-permute-done
  13.8 5.9 %collective-permute-done.1 = bf16[64,1024]{1,0:T(8,128)(2,1)S(1)} collective-permute-done((bf16[64,1024]{1,0:T(8,128)(2,1)}, bf16[64,1024]{1,0:T(8,128)(2,1)S(1)}, u32[]{:S(2)}, u32[]{:S(2)}) %collective-permute-start.1) | collective-permute-done | bytes 131104 | tf_op jit(solution)/shard_map/ppermute | solution.py:229
  19.7 60.6 %all_to_all.15.kv_ref = bf16[32,256,128]{2,1,0:T(8,128)(2,1)} all-to-all(bf16[32,256,128]{2,1,0:T(8,128)(2,1)S(1)} %get-tuple-element.15), channel_id=1, replica_groups=mesh['yh'=2,'x'=4,'c'=2,'z'=8,'yl'=4] {'z','yl'}, dimensions={0} | all-to-all | bytes 4194304 | tf_op jit(solution)/shard_map/all_to_all | solution.py:225
  80.3 0.0 copy-start.2
  80.3 0.0 copy-start.6
  80.3 7.0 %all-to-all-start.1 = ((bf16[32,256,128]{2,1,0:T(8,128)(2,1)}), bf16[32,256,128]{2,1,0:T(8,128)(2,1)S(1)}, u32[]{:S(2)}, u32[]{:S(2)}) async-start(bf16[32,256,128]{2,1,0:T(8,128)(2,1)} %get-tuple-element.21), calls=%async_computation.1 | async-start | bytes 4194304 | tf_op jit(solution)/shard_map/all_to_all | solution.py:225
  87.3 0.0 copy-start.5
  87.3 0.0 copy-done.2
  87.4 1.9 %collective-permute-start.2 = (bf16[2,32,1024]{2,1,0:T(8,128)(2,1)S(1)}, bf16[2,32,1024]{2,1,0:T(8,128)(2,1)S(1)}, u32[]{:S(2)}, u32[]{:S(2)}) collective-permute-start(bf16[2,32,1024]{2,1,0:T(8,128)(2,1)S(1)} %get-tuple-element.30), channel_id=1, source_target_pairs={{0,32},{32,0},{1,33},{33,1},{2,34},{34,2},{3,35},{35,3},{4,36},{36... | collective-permute-start | bytes 393224 | tf_op jit(solution)/shard_map/ppermute | solution.py:229
  89.3 0.0 copy-done.6
  89.3 2.4 %collective-permute-start.6 = (bf16[2,64,1024]{2,1,0:T(8,128)(2,1)S(1)}, bf16[2,64,1024]{2,1,0:T(8,128)(2,1)S(1)}, u32[]{:S(2)}, u32[]{:S(2)}) collective-permute-start(bf16[2,64,1024]{2,1,0:T(8,128)(2,1)S(1)} %get-tuple-element.28), channel_id=1, source_target_pairs={{0,32},{32,0},{1,33},{33,1},{2,34},{34,2},{3,35},{35,3},{4,36},{36... | collective-permute-start | bytes 786440 | tf_op jit(solution)/shard_map/ppermute | solution.py:229
  91.7 0.0 collective-permute-done.2
  91.8 3.4 %collective-permute-start.3 = (bf16[2,2,32,1024]{3,2,1,0:T(8,128)(2,1)S(1)}, bf16[2,2,32,1024]{3,2,1,0:T(8,128)(2,1)}, u32[]{:S(2)}, u32[]{:S(2)}) collective-permute-start(bf16[2,2,32,1024]{3,2,1,0:T(8,128)(2,1)S(1)} %pad_maximum_fusion.1.refs_0_), channel_id=1, source_target_pairs={{0,64},{64,128},{128,192},{192,0},{1,65},{65,129},{129,193},{193,1... | collective-permute-start | bytes 786440 | tf_op jit(solution)/shard_map/ppermute | solution.py:234
  95.2 4.6 %collective-permute-start.4 = (bf16[2,2,32,1024]{3,2,1,0:T(8,128)(2,1)S(1)}, bf16[2,2,32,1024]{3,2,1,0:T(8,128)(2,1)}, u32[]{:S(2)}, u32[]{:S(2)}) collective-permute-start(bf16[2,2,32,1024]{3,2,1,0:T(8,128)(2,1)S(1)} %pad_maximum_fusion.1.refs_0_), channel_id=1, source_target_pairs={{0,128},{64,192},{128,0},{192,64},{1,129},{65,193},{129,1},{193,65... | collective-permute-start | bytes 786440 | tf_op jit(solution)/shard_map/ppermute | solution.py:234
  99.8 3.3 %collective-permute-start.5 = (bf16[2,2,32,1024]{3,2,1,0:T(8,128)(2,1)S(1)}, bf16[2,2,32,1024]{3,2,1,0:T(8,128)(2,1)}, u32[]{:S(2)}, u32[]{:S(2)}) collective-permute-start(bf16[2,2,32,1024]{3,2,1,0:T(8,128)(2,1)S(1)} %pad_maximum_fusion.1.refs_0_), channel_id=1, source_target_pairs={{0,192},{64,0},{128,64},{192,128},{1,193},{65,1},{129,65},{193,129... | collective-permute-start | bytes 786440 | tf_op jit(solution)/shard_map/ppermute | solution.py:234
  103.2 0.0 copy-start
  104.7 0.1 pad_add_fusion.place_ref
  104.7 0.0 collective-permute-done.6
  104.7 0.1 pad_maximum_fusion.refs_0_
  104.8 2.5 %collective-permute-start.7 = (bf16[2,2,64,1024]{3,2,1,0:T(8,128)(2,1)S(1)}, bf16[2,2,64,1024]{3,2,1,0:T(8,128)(2,1)S(1)}, u32[]{:S(2)}, u32[]{:S(2)}) collective-permute-start(bf16[2,2,64,1024]{3,2,1,0:T(8,128)(2,1)S(1)} %pad_maximum_fusion.refs_0_), channel_id=1, source_target_pairs={{0,64},{64,128},{128,192},{192,0},{1,65},{65,129},{129,193},{193,1... | collective-permute-start | bytes 1572872 | tf_op jit(solution)/shard_map/ppermute | solution.py:234
  107.3 2.8 %collective-permute-start.8 = (bf16[2,2,64,1024]{3,2,1,0:T(8,128)(2,1)S(1)}, bf16[2,2,64,1024]{3,2,1,0:T(8,128)(2,1)}, u32[]{:S(2)}, u32[]{:S(2)}) collective-permute-start(bf16[2,2,64,1024]{3,2,1,0:T(8,128)(2,1)S(1)} %pad_maximum_fusion.refs_0_), channel_id=1, source_target_pairs={{0,128},{64,192},{128,0},{192,64},{1,129},{65,193},{129,1},{193,65... | collective-permute-start | bytes 1572872 | tf_op jit(solution)/shard_map/ppermute | solution.py:234
  110.1 0.0 collective-permute-done.3.refs_1_
  110.1 3.7 %collective-permute-start.9 = (bf16[2,2,64,1024]{3,2,1,0:T(8,128)(2,1)S(1)}, bf16[2,2,64,1024]{3,2,1,0:T(8,128)(2,1)}, u32[]{:S(2)}, u32[]{:S(2)}) collective-permute-start(bf16[2,2,64,1024]{3,2,1,0:T(8,128)(2,1)S(1)} %pad_maximum_fusion.refs_0_), channel_id=1, source_target_pairs={{0,192},{64,0},{128,64},{192,128},{1,193},{65,1},{129,65},{193,129... | collective-permute-start | bytes 1572872 | tf_op jit(solution)/shard_map/ppermute | solution.py:234
  113.8 0.0 collective-permute-done.4.refs_2_
  113.8 0.0 collective-permute-done.5.refs_3_
  113.9 0.0 copy-start.1
  113.9 0.9 copy-done.1
  114.8 2.2 %project.1 = (bf16[512,128]{1,0:T(8,128)(2,1)S(1)}, bf16[16,16,128]{2,1,0:T(8,128)(2,1)S(1)}) custom-call(s32[3]{0:T(128)S(1)} %pad_add_fusion.place_ref, bf16[2,2,32,1024]{3,2,1,0:T(8,128)(2,1)S(1)} %pad_maximum_fusion.1.refs_0_, bf16[2,2,32,1024]{3,2,1,0:T(8,128)(2,1)} %collective-permute-done.3.refs_1_, ...), custom_call_target="tpu_custom_call" | custom-call | flops 134217728 | bytes 2097152 | tf_op jit(solution)/shard_map/project/pallas_call | solution.py:60
  117.0 0.0 copy-done.5
  117.0 0.0 copy-done
  117.0 2.2 %attend_first.1.before_ref = f32[512,128]{1,0:T(8,128)S(1)} custom-call(s32[1]{0:T(128)S(6)} %copy.8.length_ref, s32[1,128]{1,0:T(1,128)S(1)} %copy-done.5, s32[1]{0:T(128)S(6)} %copy.9.count_ref, bf16[512,128]{1,0:T(8,128)(2,1)S(1)} %get-tuple-element.20.query_ref, bf16[32,256,128]{2,1,0:T(8,128)(2,1)S(1)} %copy-done), custom_call_target="tpu_custom_call" | custom-call | flops 2147483648 | bytes 2097152 | tf_op jit(solution)/shard_map/attend_first/pallas_call | solution.py:160
  119.2 0.0 copy-start.3
  119.2 0.7 copy-done.3
  119.9 19.6 %all-to-all-done.1.kv_ref = bf16[32,256,128]{2,1,0:T(8,128)(2,1)S(1)} async-done(((bf16[32,256,128]{2,1,0:T(8,128)(2,1)}), bf16[32,256,128]{2,1,0:T(8,128)(2,1)S(1)}, u32[]{:S(2)}, u32[]{:S(2)}) %all-to-all-start.1) | async-done | bytes 2097184 | tf_op jit(solution)/shard_map/all_to_all | solution.py:225
  139.5 0.0 copy-start.4
  139.5 0.9 copy-done.4
  140.4 3.0 %attend_last.1 = bf16[16,48,128]{2,1,0:T(8,128)(2,1)} custom-call(s32[1]{0:T(128)S(6)} %copy.8.length_ref, s32[1,128]{1,0:T(1,128)S(1)} %copy-done.5, s32[1]{0:T(128)S(6)} %copy.9.count_ref, bf16[512,128]{1,0:T(8,128)(2,1)S(1)} %copy-done.4, bf16[32,256,128]{2,1,0:T(8,128)(2,1)S(1)} %all-to-all-done.1.kv_ref, f32[512,128]{1,0:T(8,128)S(1)} %attend_first.1.before_ref, ...), custom_call_target="tpu_custom_call" | custom-call | flops 2147483648 | bytes 2097152 | tf_op jit(solution)/shard_map/attend_last/pallas_call | solution.py:169
  143.5 8.2 %all-to-all-start.2 = ((bf16[16,48,128]{2,1,0:T(8,128)(2,1)}), bf16[16,48,128]{2,1,0:T(8,128)(2,1)S(1)}, u32[]{:S(2)}, u32[]{:S(2)}) async-start(bf16[16,48,128]{2,1,0:T(8,128)(2,1)} %attend_last.1), calls=%async_computation.2 | async-start | bytes 393216 | tf_op jit(solution)/shard_map/all_to_all | solution.py:225
  151.7 0.0 collective-permute-done.7.refs_1_
  151.7 0.0 collective-permute-done.8.refs_2_
  151.7 0.0 collective-permute-done.9.refs_3_
  151.7 13.3 %all-to-all-done.2.parts_ref = bf16[16,48,128]{2,1,0:T(8,128)(2,1)S(1)} async-done(((bf16[16,48,128]{2,1,0:T(8,128)(2,1)}), bf16[16,48,128]{2,1,0:T(8,128)(2,1)S(1)}, u32[]{:S(2)}, u32[]{:S(2)}) %all-to-all-start.2) | async-done | bytes 196640 | tf_op jit(solution)/shard_map/all_to_all | solution.py:225
  165.0 2.5 %output.1 = bf16[32,1024]{1,0:T(8,128)(2,1)} custom-call(s32[3]{0:T(128)S(1)} %pad_add_fusion.place_ref, s32[1]{0:T(128)S(6)} %sub.7.count_ref, bf16[16,48,128]{2,1,0:T(8,128)(2,1)S(1)} %all-to-all-done.2.parts_ref, bf16[2,2,64,1024]{3,2,1,0:T(8,128)(2,1)S(1)} %pad_maximum_fusion.refs_0_, bf16[2,2,64,1024]{3,2,1,0:T(8,128)(2,1)S(1)} %collective-permute-done.7.refs_1_, ...), custom_call_target="tpu_custom_call" | custom-call | flops 67108864 | bytes 3145728 | tf_op jit(solution)/shard_map/output/pallas_call | solution.py:213
  (3 shorter events, 0.1 us)
Async XLA Ops:
  0.0 13.8 %collective-permute-start = (bf16[32,1024]{1,0:T(8,128)(2,1)}, bf16[32,1024]{1,0:T(8,128)(2,1)S(1)}, u32[]{:S(2)}, u32[]{:S(2)}) collective-permute-start(bf16[32,1024]{1,0:T(8,128)(2,1)} %bitcast.16), channel_id=1, source_target_pairs={{0,256},{256,0},{1,257},{257,1},{2,258},{258,2},{3,259},{259,3},{4... | collective-permute-start | bytes 196616 | tf_op jit(solution)/shard_map/ppermute | solution.py:229
  5.9 13.8 %collective-permute-start.1 = (bf16[64,1024]{1,0:T(8,128)(2,1)}, bf16[64,1024]{1,0:T(8,128)(2,1)S(1)}, u32[]{:S(2)}, u32[]{:S(2)}) collective-permute-start(bf16[64,1024]{1,0:T(8,128)(2,1)} %param.13), channel_id=1, source_target_pairs={{0,256},{256,0},{1,257},{257,1},{2,258},{258,2},{3,259},{259,3},{4... | collective-permute-start | bytes 393224 | tf_op jit(solution)/shard_map/ppermute | solution.py:229
  80.3 7.0 %copy-start.2 = (bf16[32,1,1024]{2,0,1:T(8,128)(2,1)S(1)}, bf16[32,1,1024]{2,0,1:T(8,128)(2,1)}, u32[]{:S(2)}) copy-start(bf16[32,1,1024]{2,0,1:T(8,128)(2,1)} %param.7) | copy-start | bytes 196612
  80.3 8.9 %copy-start.6 = (bf16[64,1024]{1,0:T(8,128)(2,1)S(1)}, bf16[64,1024]{1,0:T(8,128)(2,1)}, u32[]{:S(2)}) copy-start(bf16[64,1024]{1,0:T(8,128)(2,1)} %param.13) | copy-start | bytes 393220
  80.3 59.2 %all-to-all-start.1 = ((bf16[32,256,128]{2,1,0:T(8,128)(2,1)}), bf16[32,256,128]{2,1,0:T(8,128)(2,1)S(1)}, u32[]{:S(2)}, u32[]{:S(2)}) async-start(bf16[32,256,128]{2,1,0:T(8,128)(2,1)} %get-tuple-element.21), calls=%async_computation.1 | async-start | bytes 4194304 | tf_op jit(solution)/shard_map/all_to_all | solution.py:225
  87.3 29.7 %copy-start.5 = (s32[1,128]{1,0:T(1,128)S(1)}, s32[1,128]{1,0:T(1,128)}, u32[]{:S(2)}) copy-start(s32[1,128]{1,0:T(1,128)} %mask_ref.3) | copy-start | bytes 1540
  87.4 4.4 %collective-permute-start.2 = (bf16[2,32,1024]{2,1,0:T(8,128)(2,1)S(1)}, bf16[2,32,1024]{2,1,0:T(8,128)(2,1)S(1)}, u32[]{:S(2)}, u32[]{:S(2)}) collective-permute-start(bf16[2,32,1024]{2,1,0:T(8,128)(2,1)S(1)} %get-tuple-element.30), channel_id=1, source_target_pairs={{0,32},{32,0},{1,33},{33,1},{2,34},{34,2},{3,35},{35,3},{4,36},{36... | collective-permute-start | bytes 393224 | tf_op jit(solution)/shard_map/ppermute | solution.py:229
  89.3 15.4 %collective-permute-start.6 = (bf16[2,64,1024]{2,1,0:T(8,128)(2,1)S(1)}, bf16[2,64,1024]{2,1,0:T(8,128)(2,1)S(1)}, u32[]{:S(2)}, u32[]{:S(2)}) collective-permute-start(bf16[2,64,1024]{2,1,0:T(8,128)(2,1)S(1)} %get-tuple-element.28), channel_id=1, source_target_pairs={{0,32},{32,0},{1,33},{33,1},{2,34},{34,2},{3,35},{35,3},{4,36},{36... | collective-permute-start | bytes 786440 | tf_op jit(solution)/shard_map/ppermute | solution.py:229
  91.8 18.3 %collective-permute-start.3 = (bf16[2,2,32,1024]{3,2,1,0:T(8,128)(2,1)S(1)}, bf16[2,2,32,1024]{3,2,1,0:T(8,128)(2,1)}, u32[]{:S(2)}, u32[]{:S(2)}) collective-permute-start(bf16[2,2,32,1024]{3,2,1,0:T(8,128)(2,1)S(1)} %pad_maximum_fusion.1.refs_0_), channel_id=1, source_target_pairs={{0,64},{64,128},{128,192},{192,0},{1,65},{65,129},{129,193},{193,1... | collective-permute-start | bytes 786440 | tf_op jit(solution)/shard_map/ppermute | solution.py:234
  95.2 18.6 %collective-permute-start.4 = (bf16[2,2,32,1024]{3,2,1,0:T(8,128)(2,1)S(1)}, bf16[2,2,32,1024]{3,2,1,0:T(8,128)(2,1)}, u32[]{:S(2)}, u32[]{:S(2)}) collective-permute-start(bf16[2,2,32,1024]{3,2,1,0:T(8,128)(2,1)S(1)} %pad_maximum_fusion.1.refs_0_), channel_id=1, source_target_pairs={{0,128},{64,192},{128,0},{192,64},{1,129},{65,193},{129,1},{193,65... | collective-permute-start | bytes 786440 | tf_op jit(solution)/shard_map/ppermute | solution.py:234
  99.8 14.0 %collective-permute-start.5 = (bf16[2,2,32,1024]{3,2,1,0:T(8,128)(2,1)S(1)}, bf16[2,2,32,1024]{3,2,1,0:T(8,128)(2,1)}, u32[]{:S(2)}, u32[]{:S(2)}) collective-permute-start(bf16[2,2,32,1024]{3,2,1,0:T(8,128)(2,1)S(1)} %pad_maximum_fusion.1.refs_0_), channel_id=1, source_target_pairs={{0,192},{64,0},{128,64},{192,128},{1,193},{65,1},{129,65},{193,129... | collective-permute-start | bytes 786440 | tf_op jit(solution)/shard_map/ppermute | solution.py:234
  103.2 13.8 %copy-start = (bf16[32,256,128]{2,1,0:T(8,128)(2,1)S(1)}, bf16[32,256,128]{2,1,0:T(8,128)(2,1)}, u32[]{:S(2)}) copy-start(bf16[32,256,128]{2,1,0:T(8,128)(2,1)} %all_to_all.15.kv_ref) | copy-start | bytes 6291460
  104.8 46.9 %collective-permute-start.7 = (bf16[2,2,64,1024]{3,2,1,0:T(8,128)(2,1)S(1)}, bf16[2,2,64,1024]{3,2,1,0:T(8,128)(2,1)S(1)}, u32[]{:S(2)}, u32[]{:S(2)}) collective-permute-start(bf16[2,2,64,1024]{3,2,1,0:T(8,128)(2,1)S(1)} %pad_maximum_fusion.refs_0_), channel_id=1, source_target_pairs={{0,64},{64,128},{128,192},{192,0},{1,65},{65,129},{129,193},{193,1... | collective-permute-start | bytes 1572872 | tf_op jit(solution)/shard_map/ppermute | solution.py:234
  107.3 44.4 %collective-permute-start.8 = (bf16[2,2,64,1024]{3,2,1,0:T(8,128)(2,1)S(1)}, bf16[2,2,64,1024]{3,2,1,0:T(8,128)(2,1)}, u32[]{:S(2)}, u32[]{:S(2)}) collective-permute-start(bf16[2,2,64,1024]{3,2,1,0:T(8,128)(2,1)S(1)} %pad_maximum_fusion.refs_0_), channel_id=1, source_target_pairs={{0,128},{64,192},{128,0},{192,64},{1,129},{65,193},{129,1},{193,65... | collective-permute-start | bytes 1572872 | tf_op jit(solution)/shard_map/ppermute | solution.py:234
  110.1 41.6 %collective-permute-start.9 = (bf16[2,2,64,1024]{3,2,1,0:T(8,128)(2,1)S(1)}, bf16[2,2,64,1024]{3,2,1,0:T(8,128)(2,1)}, u32[]{:S(2)}, u32[]{:S(2)}) collective-permute-start(bf16[2,2,64,1024]{3,2,1,0:T(8,128)(2,1)S(1)} %pad_maximum_fusion.refs_0_), channel_id=1, source_target_pairs={{0,192},{64,0},{128,64},{192,128},{1,193},{65,1},{129,65},{193,129... | collective-permute-start | bytes 1572872 | tf_op jit(solution)/shard_map/ppermute | solution.py:234
  113.9 1.0 copy-start.1
  119.2 0.7 copy-start.3
  139.5 0.9 copy-start.4
  143.5 21.6 %all-to-all-start.2 = ((bf16[16,48,128]{2,1,0:T(8,128)(2,1)}), bf16[16,48,128]{2,1,0:T(8,128)(2,1)S(1)}, u32[]{:S(2)}, u32[]{:S(2)}) async-start(bf16[16,48,128]{2,1,0:T(8,128)(2,1)} %attend_last.1), calls=%async_computation.2 | async-start | bytes 393216 | tf_op jit(solution)/shard_map/all_to_all | solution.py:225

commit v5 on v4

--- a/solution.py
+++ b/solution.py
@@ -10,8 +10,8 @@
 
 D = 1024
 BLK = 128
-FINE = 128
-FIRST = 256
+FINE = 64
+FIRST = 320
 GRP = ("yh", "x", "c")
 HALF = 64
 PARAMS = pltpu.CompilerParams(vmem_limit_bytes=24 * 1024 * 1024)
@@ -33,8 +33,11 @@
     return (yh ^ half) * 8 + lax.rem(x - turns + 4, 4) * 2 + (c ^ core)
 
 
-def project_kernel(place_ref, *refs):
-    quads, (w_ref, query_ref, gate_ref) = refs[:4], refs[4:]
+def project_kernel(place_ref, length_ref, mask_ref, *refs):
+    quads, (w_ref, query_ref, gate_ref, message_ref) = refs[:4], refs[4:]
+    block = lax.broadcasted_iota(jnp.int32, (16, 128), 1)
+    live = jnp.clip(length_ref[0] - block * BLK, 0, BLK) * mask_ref[...]
+    message_ref[256:272] = live.astype(jnp.float32).astype(jnp.bfloat16)
     for turns, quad in enumerate(quads):
         _, _, own, width = quad.shape
         rows = quad[...].reshape(4 * own, width).astype(jnp.float32)
@@ -46,15 +49,18 @@
         first, second = pairs[:, 0], pairs[:, 1]
         turned = pltpu.roll(first.reshape(-1, 128), HALF, 1).reshape(first.shape)
         gate = jnp.where(low_lanes(first.shape), turned, second).astype(jnp.bfloat16)
+        turned = pltpu.roll(second.reshape(-1, 128), HALF, 1).reshape(second.shape)
+        packed = (jnp.where(low_lanes(first.shape), first, turned) * (0.5 * HALF ** (-0.5))).astype(jnp.bfloat16)
         for core in range(2):
             for half in range(2):
                 at = member(place_ref, turns, core, half)
                 block = core * 2 + half
                 query_ref[pl.ds(pl.multiple_of(at * own, own), own)] = query[block * own : (block + 1) * own]
                 gate_ref[at] = gate[block]
-
-
-def project(place, quads, w_proj):
+                message_ref[pl.ds(pl.multiple_of(at * 16, 16), 16)] = packed[block]
+
+
+def project(place, length, mask, quads, w_proj):
     own = quads[0].shape[2]
     vmem = pl.BlockSpec(memory_space=pltpu.VMEM)
     return pl.pallas_call(
@@ -62,13 +68,14 @@
         out_shape=(
             jax.ShapeDtypeStruct((16 * own, 128), jnp.bfloat16),
             jax.ShapeDtypeStruct((16, own // 2, 128), jnp.bfloat16),
+            jax.ShapeDtypeStruct((272, 128), jnp.bfloat16),
         ),
-        in_specs=[pl.BlockSpec(memory_space=pltpu.SMEM)] + [vmem] * 5,
-        out_specs=(vmem, vmem),
+        in_specs=[pl.BlockSpec(memory_space=pltpu.SMEM)] * 2 + [vmem] * 6,
+        out_specs=(vmem, vmem, vmem),
         compiler_params=PARAMS,
         cost_estimate=pl.CostEstimate(flops=2 * 512 * D * 128, bytes_accessed=2 << 20, transcendentals=0),
         name="project",
-    )(place, *quads, w_proj)
+    )(place, length, mask, *quads, w_proj)
 
 
 def attend_tiles(offset, length_ref, mask_ref, count_ref, query_ref, kv_ref, total, masked):
@@ -106,20 +113,70 @@
         attend_rows(((0, 256), (256, 512)))
 
 
-def attend_first_kernel(offset, length_ref, mask_ref, count_ref, query_ref, kv_ref, total, masked):
-    @pl.when(pl.program_id(0) == 0)
-    def _():
-        total[...] = jnp.zeros_like(total)
-
-    attend_tiles(offset, length_ref, mask_ref, count_ref, query_ref, kv_ref, total, masked)
+def attend_plane_kernel(y_ref, live_ref, message_ref, kv_ref, out_ref, masked):
+    user = pl.program_id(0)
+    planes, _, rows, _ = kv_ref.shape
+    pieces = rows // FINE
+    blocks = -(-rows // BLK)
+    lives = []
+    for plane in range(planes):
+        for piece in range(pieces):
+            block, part = divmod(piece * FINE, BLK)
+            lives.append(jnp.clip(live_ref[(user * planes + plane) * blocks + block] - part, 0, FINE))
+    some = functools.reduce(jnp.add, lives) > 0
+
+    @pl.when(some)
+    def _():
+        row = lax.broadcasted_iota(jnp.int32, (FINE, 128), 0)
+        for i, live in enumerate(lives):
+            plane, piece = divmod(i, pieces)
+            values = kv_ref[plane, 0, piece * FINE : (piece + 1) * FINE]
+            masked[i * FINE : (i + 1) * FINE] = jnp.where(row < live, values, jnp.zeros_like(values))
+        packed = message_ref[0, 0:256].astype(jnp.float32)
+        low = low_lanes(packed.shape)
+        totals = []
+        for values in (packed, pltpu.roll(packed, HALF, 1)):
+            query = jnp.where(low, values, 0.0).astype(jnp.bfloat16)
+            scores = lax.dot_general(
+                query, masked[...], (((1,), (1,)), ((), ())), preferred_element_type=jnp.float32
+            )
+            weights = (scores + scores * jnp.tanh(scores)).astype(jnp.bfloat16)
+            totals.append(jnp.dot(weights, masked[...], preferred_element_type=jnp.float32))
+        out_ref[0] = jnp.where(low, pltpu.roll(totals[0], HALF, 1), totals[1])
+
+    @pl.when(jnp.logical_not(some))
+    def _():
+        out_ref[...] = jnp.zeros_like(out_ref)
+
+
+def attend_plane(y, live, messages, kv):
+    planes, users, rows, _ = kv.shape
+    return pl.pallas_call(
+        attend_plane_kernel,
+        out_shape=jax.ShapeDtypeStruct((users, 256, 128), jnp.float32),
+        grid_spec=pltpu.PrefetchScalarGridSpec(
+            num_scalar_prefetch=1,
+            grid=(users,),
+            in_specs=[
+                pl.BlockSpec(memory_space=pltpu.SMEM),
+                pl.BlockSpec((1, 272, 128), lambda i, y: (i, 0, 0)),
+                pl.BlockSpec((planes, 1, rows, 128), lambda i, y: (0, y[0] ^ i, 0, 0)),
+            ],
+            out_specs=pl.BlockSpec((1, 256, 128), lambda i, y: (i, 0, 0)),
+            scratch_shapes=[pltpu.VMEM((planes * rows, 128), jnp.bfloat16)],
+        ),
+        compiler_params=PARAMS,
+        cost_estimate=pl.CostEstimate(flops=1 << 30, bytes_accessed=3 << 20, transcendentals=1 << 22),
+        name="attend_plane",
+    )(y, live, messages, kv)
 
 
 def attend_last_kernel(
-    offset, length_ref, mask_ref, count_ref, query_ref, kv_ref, before_ref, gate_ref, out_ref, total, masked
+    offset, length_ref, mask_ref, count_ref, query_ref, kv_ref, gate_ref, a_ref, b_ref, c_ref, d_ref, out_ref, total, masked
 ):
     @pl.when(pl.program_id(0) == 0)
     def _():
-        total[...] = before_ref[...]
+        total[...] = jnp.zeros_like(total)
 
     attend_tiles(offset, length_ref, mask_ref, count_ref, query_ref, kv_ref, total, masked)
 
@@ -129,53 +186,40 @@
         first, second = slices[:, 0], slices[:, 1]
         turned = pltpu.roll(first.reshape(-1, 128), HALF, 1).reshape(first.shape)
         packed = jnp.where(low_lanes(first.shape), turned, second)
+        others = a_ref[...] + b_ref[...] + c_ref[...] + d_ref[...]
+        packed += others.reshape(packed.shape)
         high = packed.astype(jnp.bfloat16)
         out_ref[:, 0:16, :] = high
         out_ref[:, 16:32, :] = (packed - high.astype(jnp.float32)).astype(jnp.bfloat16)
         out_ref[:, 32:48, :] = gate_ref[...]
 
 
-def attend(offset, sources, length, mask, cand_count, query, kv, before=None, gate=None):
+def attend_last(offset, sources, length, mask, cand_count, query, kv, gate, sums):
     count = query.shape[0]
     devices, rows, _ = kv.shape
     smem = pl.BlockSpec(memory_space=pltpu.SMEM)
-    in_specs = [
-        smem,
-        smem,
-        smem,
-        pl.BlockSpec((count, 128), lambda i: (0, 0)),
-        pl.BlockSpec((sources, rows, 128), lambda i: (i, 0, 0)),
-    ]
-    masked = pltpu.VMEM((sources * rows, 128), jnp.bfloat16)
-    running = pltpu.VMEM((count, 128), jnp.float32)
     positions = devices * rows
-    common = dict(
+    return pl.pallas_call(
+        functools.partial(attend_last_kernel, offset),
+        out_shape=jax.ShapeDtypeStruct((count // 32, 48, 128), jnp.bfloat16),
         grid=(devices // sources,),
+        in_specs=[
+            smem,
+            smem,
+            smem,
+            pl.BlockSpec((count, 128), lambda i: (0, 0)),
+            pl.BlockSpec((sources, rows, 128), lambda i: (i, 0, 0)),
+            pl.BlockSpec((count // 32, 16, 128), lambda i: (0, 0, 0)),
+        ]
+        + [pl.BlockSpec((256, 128), lambda i: (0, 0))] * 4,
+        out_specs=pl.BlockSpec((count // 32, 48, 128), lambda i: (0, 0, 0)),
+        scratch_shapes=[pltpu.VMEM((count, 128), jnp.float32), pltpu.VMEM((sources * rows, 128), jnp.bfloat16)],
         compiler_params=PARAMS,
         cost_estimate=pl.CostEstimate(
             flops=4 * count * positions * 128, bytes_accessed=positions * 256, transcendentals=count * positions
         ),
-    )
-    if before is None:
-        return pl.pallas_call(
-            functools.partial(attend_first_kernel, offset),
-            out_shape=jax.ShapeDtypeStruct((count, 128), jnp.float32),
-            in_specs=in_specs,
-            out_specs=pl.BlockSpec((count, 128), lambda i: (0, 0)),
-            scratch_shapes=[masked],
-            name="attend_first",
-            **common,
-        )(length, mask, cand_count, query, kv)
-    return pl.pallas_call(
-        functools.partial(attend_last_kernel, offset),
-        out_shape=jax.ShapeDtypeStruct((count // 32, 48, 128), jnp.bfloat16),
-        in_specs=in_specs
-        + [pl.BlockSpec((count, 128), lambda i: (0, 0)), pl.BlockSpec((count // 32, 16, 128), lambda i: (0, 0, 0))],
-        out_specs=pl.BlockSpec((count // 32, 48, 128), lambda i: (0, 0, 0)),
-        scratch_shapes=[running, masked],
         name="attend_last",
-        **common,
-    )(length, mask, cand_count, query, kv, before, gate)
+    )(length, mask, cand_count, query, kv, gate, *sums)
 
 
 def spread_heads(packed):
@@ -238,20 +282,29 @@
     own_rows = cand_x.shape[0]
     rows = cand_x.reshape(own_rows, D)
     place = jnp.stack([lax.axis_index("yh"), lax.axis_index("x"), lax.axis_index("c")]).astype(jnp.int32)
+    y = lax.axis_index("yl").astype(jnp.int32)
+
+    def along_y(values, step):
+        return lax.ppermute(values, "yl", [(i, i ^ step) for i in range(4)])
+
+    second = hist_kv[:, FIRST:]
+    plane = exchange(hist_kv[:, :FIRST].reshape(8, 4, FIRST, 128), "z")
     other_rows, other_w = swap(rows, "yh"), swap(w_out, "yh")
-    first, second, other_rows, other_w = lax.optimization_barrier(
-        (hist_kv[:, :FIRST], hist_kv[:, FIRST:], other_rows, other_w)
+    quads = go_round(jnp.stack([rows, other_rows]))
+    other_w, *quads = lax.optimization_barrier((other_w, *quads))
+    query, gate, message = project(place, hist_len, block_mask, quads, w_proj)
+    messages = jnp.stack([message] + [along_y(message, step) for step in (1, 2, 3)])
+    plane, second, query, gate, messages, other_w = lax.optimization_barrier(
+        (plane, second, query, gate, messages, other_w)
     )
-    hist = ("z", "yl")
-    bulk = exchange(first, hist)
-    bulk, second, other_rows, other_w = lax.optimization_barrier((bulk, second, other_rows, other_w))
-    rest = exchange(second, hist)
-
-    limits = (hist_len, block_mask, cand_count)
-    query, gate = project(place, go_round(jnp.stack([rows, other_rows])), w_proj)
-    total = attend(0, 8, *limits, query, bulk)
+    rest = exchange(second, ("z", "yl"))
+
+    live = messages[:, 256].astype(jnp.int32).reshape(4, 8, 4, 4)
+    live = lax.dynamic_index_in_dim(live, y, 2, keepdims=False)[:, :, : -(-FIRST // BLK)]
+    part = attend_plane(y.reshape(1), live.reshape(-1), messages, plane)
+    sums = [part[0]] + [along_y(part[step], step) for step in (1, 2, 3)]
     w_quads = go_round(jnp.stack([w_out, other_w]))
-    attended = attend(FIRST, 8, *limits, query, rest, total, gate)
+    attended = attend_last(FIRST, 8, hist_len, block_mask, cand_count, query, rest, gate, sums)
     keep = cand_count - lax.axis_index(GRP) * own_rows
     parts = exchange(attended, GRP)
     return output(place, keep, parts, w_quads, rows).reshape(cand_x.shape)

time: 168 us -> 159 us (0.946)
  the two profiles are of different devices: /device:TPU:80 before, /device:TPU:16 now
where the time goes in v5:
time: 159 us; the launch traced here: 158 us
  starting transfers between devices  82.9 us (52%)
  waiting for transfers between devices  48.8 us (31%)
  Pallas kernels  16.5 us (10%)
  local copies, waits for them, and re-layouts  6.62 us (4%)
  between operations  1.64 us (1%)
    all_to_all x3, starting transfers between devices, exchange(): return lax.all_to_all(values, axes, split_axis=0, concat_axis=0, tiled=True)  24.9 us
    ppermute x6, starting transfers between devices, go_round(): lax.ppermute(quad, 'x', [(i, (i + turns) % 4) for i in range(4)])  24.1 us
    all_to_all x3, waiting for transfers between devices, exchange(): return lax.all_to_all(values, axes, split_axis=0, concat_axis=0, tiled=True)  22.3 us
    ppermute x6, starting transfers between devices, along_y(): return lax.ppermute(values, 'yl', [(i, i ^ step) for i in range(4)])  18.4 us
    ppermute x4, starting transfers between devices, swap(): return lax.ppermute(values, axis, [(0, 1), (1, 0)])  15.5 us
    ppermute x4, waiting for transfers between devices, swap(): return lax.ppermute(values, axis, [(0, 1), (1, 0)])  13.4 us
    ppermute x6, waiting for transfers between devices, along_y(): return lax.ppermute(values, 'yl', [(i, i ^ step) for i in range(4)])  13 us
    pallas_call x1, Pallas kernels, attend_plane(): pl.pallas_call(attend_plane_kernel, out_shape=jax.ShapeDtypeStruct((users...  7.54 us
  transfers between devices with their start and end apart: 19, of which 9 were waited for; matrix products, arithmetic and copies ran while one was open for 3% of the time, Pallas kernels for 9%

profile of v5, /device:TPU:16, one launch (start us, length us, event | category | flops | bytes accessed | tf_op | source)
XLA Modules:
  0.0 157.6 jit_solution(11225924293788216033)
XLA Ops:
  0.0 3.4 %slice.24 = bf16[32,320,128]{2,1,0:T(8,128)(2,1)} slice(bf16[32,512,128]{2,1,0:T(8,128)(2,1)} %param.8), slice={[0:32], [0:320], [0:128]} | slice | bytes 5242880 | tf_op jit(solution)/shard_map/slice | solution.py:291
  3.4 10.4 %all-to-all-start = ((bf16[8,4,320,128]{3,2,1,0:T(8,128)(2,1)}), bf16[8,4,320,128]{3,2,1,0:T(8,128)(2,1)S(1)}, u32[]{:S(2)}, u32[]{:S(2)}) async-start(bf16[8,4,320,128]{3,2,1,0:T(8,128)(2,1)} %bitcast.36), calls=%async_computation | async-start | bytes 5242880 | tf_op jit(solution)/shard_map/all_to_all | solution.py:269
  13.9 5.9 %collective-permute-start.1 = (bf16[32,1024]{1,0:T(8,128)(2,1)S(1)}, bf16[32,1024]{1,0:T(8,128)(2,1)S(1)}, u32[]{:S(2)}, u32[]{:S(2)}) collective-permute-start(bf16[32,1024]{1,0:T(8,128)(2,1)S(1)} %bitcast.32), channel_id=1, source_target_pairs={{0,256},{256,0},{1,257},{257,1},{2,258},{258,2},{3,259},{259,3},{4... | collective-permute-start | bytes 196616 | tf_op jit(solution)/shard_map/ppermute | solution.py:273
  19.8 4.9 %collective-permute-done.1 = bf16[32,1024]{1,0:T(8,128)(2,1)S(1)} collective-permute-done((bf16[32,1024]{1,0:T(8,128)(2,1)S(1)}, bf16[32,1024]{1,0:T(8,128)(2,1)S(1)}, u32[]{:S(2)}, u32[]{:S(2)}) %collective-permute-start.1) | collective-permute-done | bytes 65568 | tf_op jit(solution)/shard_map/ppermute | solution.py:273
  24.7 1.9 %collective-permute-start.2 = (bf16[2,32,1024]{2,1,0:T(8,128)(2,1)S(1)}, bf16[2,32,1024]{2,1,0:T(8,128)(2,1)S(1)}, u32[]{:S(2)}, u32[]{:S(2)}) collective-permute-start(bf16[2,32,1024]{2,1,0:T(8,128)(2,1)S(1)} %get-tuple-element.40), channel_id=1, source_target_pairs={{0,32},{32,0},{1,33},{33,1},{2,34},{34,2},{3,35},{35,3},{4,36},{36... | collective-permute-start | bytes 393224 | tf_op jit(solution)/shard_map/ppermute | solution.py:273
  26.7 1.3 collective-permute-done.2
  28.0 3.4 %collective-permute-start.3 = (bf16[2,2,32,1024]{3,2,1,0:T(8,128)(2,1)S(1)}, bf16[2,2,32,1024]{3,2,1,0:T(8,128)(2,1)S(1)}, u32[]{:S(2)}, u32[]{:S(2)}) collective-permute-start(bf16[2,2,32,1024]{3,2,1,0:T(8,128)(2,1)S(1)} %pad_maximum_fusion.2.refs_0_), channel_id=1, source_target_pairs={{0,64},{64,128},{128,192},{192,0},{1,65},{65,129},{129,193},{193,1... | collective-permute-start | bytes 786440 | tf_op jit(solution)/shard_map/ppermute | solution.py:278
  31.4 4.6 %collective-permute-start.4 = (bf16[2,2,32,1024]{3,2,1,0:T(8,128)(2,1)S(1)}, bf16[2,2,32,1024]{3,2,1,0:T(8,128)(2,1)}, u32[]{:S(2)}, u32[]{:S(2)}) collective-permute-start(bf16[2,2,32,1024]{3,2,1,0:T(8,128)(2,1)S(1)} %pad_maximum_fusion.2.refs_0_), channel_id=1, source_target_pairs={{0,128},{64,192},{128,0},{192,64},{1,129},{65,193},{129,1},{193,65... | collective-permute-start | bytes 786440 | tf_op jit(solution)/shard_map/ppermute | solution.py:278
  36.1 3.3 %collective-permute-start.5 = (bf16[2,2,32,1024]{3,2,1,0:T(8,128)(2,1)S(1)}, bf16[2,2,32,1024]{3,2,1,0:T(8,128)(2,1)}, u32[]{:S(2)}, u32[]{:S(2)}) collective-permute-start(bf16[2,2,32,1024]{3,2,1,0:T(8,128)(2,1)S(1)} %pad_maximum_fusion.2.refs_0_), channel_id=1, source_target_pairs={{0,192},{64,0},{128,64},{192,128},{1,193},{65,1},{129,65},{193,129... | collective-permute-start | bytes 786440 | tf_op jit(solution)/shard_map/ppermute | solution.py:278
  39.4 5.7 %collective-permute-start = (bf16[64,1024]{1,0:T(8,128)(2,1)}, bf16[64,1024]{1,0:T(8,128)(2,1)}, u32[]{:S(2)}, u32[]{:S(2)}) collective-permute-start(bf16[64,1024]{1,0:T(8,128)(2,1)} %param.13), channel_id=1, source_target_pairs={{0,256},{256,0},{1,257},{257,1},{2,258},{258,2},{3,259},{259,3},{4... | collective-permute-start | bytes 393224 | tf_op jit(solution)/shard_map/ppermute | solution.py:273
  45.8 0.1 pad_add_fusion.place_ref
  45.9 7.2 %collective-permute-done = bf16[64,1024]{1,0:T(8,128)(2,1)} collective-permute-done((bf16[64,1024]{1,0:T(8,128)(2,1)}, bf16[64,1024]{1,0:T(8,128)(2,1)}, u32[]{:S(2)}, u32[]{:S(2)}) %collective-permute-start) | collective-permute-done | bytes 131104 | tf_op jit(solution)/shard_map/ppermute | solution.py:273
  53.1 0.0 collective-permute-done.5.refs_3_
  53.2 2.1 %project.1 = (bf16[512,128]{1,0:T(8,128)(2,1)S(1)}, bf16[16,16,128]{2,1,0:T(8,128)(2,1)S(1)}, bf16[272,128]{1,0:T(8,128)(2,1)S(1)}) custom-call(s32[3]{0:T(128)S(1)} %pad_add_fusion.place_ref, s32[1]{0:T(128)S(6)} %copy.12.length_ref, s32[1,128]{1,0:T(1,128)S(1)} %copy-done.2, bf16[2,2,32,1024]{3,2,1,0:T(8,128)(2,1)S(1)} %pad_maximum_fusion.2.refs_0_, ...), custom_call_target="tpu_custom_call" | custom-call | flops 134217728 | bytes 2097152 | tf_op jit(solution)/shard_map/project/pallas_call | solution.py:66
  55.3 0.0 copy-start.5
  55.3 1.9 %collective-permute-start.8 = (bf16[272,128]{1,0:T(8,128)(2,1)S(1)}, bf16[272,128]{1,0:T(8,128)(2,1)S(1)}, u32[]{:S(2)}, u32[]{:S(2)}) collective-permute-start(bf16[272,128]{1,0:T(8,128)(2,1)S(1)} %get-tuple-element.25), channel_id=1, source_target_pairs={{0,3},{1,2},{2,1},{3,0},{4,7},{5,6},{6,5},{7,4},{8,11},{9,10},{10,... | collective-permute-start | bytes 208904 | tf_op jit(solution)/shard_map/ppermute | solution.py:288
  57.2 3.9 %collective-permute-start.7 = (bf16[272,128]{1,0:T(8,128)(2,1)S(1)}, bf16[272,128]{1,0:T(8,128)(2,1)S(1)}, u32[]{:S(2)}, u32[]{:S(2)}) collective-permute-start(bf16[272,128]{1,0:T(8,128)(2,1)S(1)} %get-tuple-element.25), channel_id=1, source_target_pairs={{0,2},{1,3},{2,0},{3,1},{4,6},{5,7},{6,4},{7,5},{8,10},{9,11},{10,... | collective-permute-start | bytes 208904 | tf_op jit(solution)/shard_map/ppermute | solution.py:288
  61.1 3.4 %collective-permute-start.6 = (bf16[272,128]{1,0:T(8,128)(2,1)S(1)}, bf16[272,128]{1,0:T(8,128)(2,1)S(1)}, u32[]{:S(2)}, u32[]{:S(2)}) collective-permute-start(bf16[272,128]{1,0:T(8,128)(2,1)S(1)} %get-tuple-element.25), channel_id=1, source_target_pairs={{0,1},{1,0},{2,3},{3,2},{4,5},{5,4},{6,7},{7,6},{8,9},{9,8},{10,11... | collective-permute-start | bytes 208904 | tf_op jit(solution)/shard_map/ppermute | solution.py:288
  64.5 2.7 %slice.25 = bf16[32,192,128]{2,1,0:T(8,128)(2,1)} slice(bf16[32,512,128]{2,1,0:T(8,128)(2,1)} %param.8), slice={[0:32], [320:512], [0:128]} | slice | bytes 3145728 | tf_op jit(solution)/shard_map/slice | solution.py:290
  67.2 0.1 collective-permute-done.6
  67.3 9.0 %all-to-all-done.kv_ref = bf16[8,4,320,128]{3,2,1,0:T(8,128)(2,1)S(1)} async-done(((bf16[8,4,320,128]{3,2,1,0:T(8,128)(2,1)}), bf16[8,4,320,128]{3,2,1,0:T(8,128)(2,1)S(1)}, u32[]{:S(2)}, u32[]{:S(2)}) %all-to-all-start) | async-done | bytes 2621472 | tf_op jit(solution)/shard_map/all_to_all | solution.py:269
  76.3 5.4 %all-to-all-start.1 = ((bf16[32,192,128]{2,1,0:T(8,128)(2,1)}), bf16[32,192,128]{2,1,0:T(8,128)(2,1)}, u32[]{:S(2)}, u32[]{:S(2)}) async-start(bf16[32,192,128]{2,1,0:T(8,128)(2,1)} %slice.25), calls=%async_computation.1 | async-start | bytes 3145728 | tf_op jit(solution)/shard_map/all_to_all | solution.py:269
  81.8 0.1 reshape.24
  82.0 0.1 copy.10
  82.1 0.1 copy.11
  82.2 0.1 reshape.22.live_ref
  82.3 0.9 fusion.1
  83.2 1.9 %collective-permute-start.12 = (bf16[2,64,1024]{2,1,0:T(8,128)(2,1)S(1)}, bf16[2,64,1024]{2,1,0:T(8,128)(2,1)S(1)}, u32[]{:S(2)}, u32[]{:S(2)}) collective-permute-start(bf16[2,64,1024]{2,1,0:T(8,128)(2,1)S(1)} %get-tuple-element.38), channel_id=1, source_target_pairs={{0,32},{32,0},{1,33},{33,1},{2,34},{34,2},{3,35},{35,3},{4,36},{36... | collective-permute-start | bytes 786440 | tf_op jit(solution)/shard_map/ppermute | solution.py:273
  85.2 0.0 copy-start.6
  85.2 7.5 %attend_plane.1 = f32[4,256,128]{2,1,0:T(8,128)S(1)} custom-call(s32[1]{0:T(128)} %bitcast.14.y_ref, s32[96]{0:T(128)S(1)} %reshape.22.live_ref, bf16[4,272,128]{2,1,0:T(8,128)(2,1)S(1)} %pad_maximum_fusion.1.message_ref, bf16[8,4,320,128]{3,2,1,0:T(8,128)(2,1)S(1)} %all-to-all-done.kv_ref), custom_call_target="tpu_custom_call" | custom-call | flops 1073741824 | bytes 3145728 | tf_op jit(solution)/shard_map/attend_plane/pallas_call | solution.py:154
  92.8 3.4 %collective-permute-start.9 = (f32[256,128]{1,0:T(8,128)S(1)}, f32[256,128]{1,0:T(8,128)S(1)}, u32[]{:S(2)}, u32[]{:S(2)}) collective-permute-start(f32[256,128]{1,0:T(8,128)S(1)} %get-tuple-element.35), channel_id=1, source_target_pairs={{0,1},{1,0},{2,3},{3,2},{4,5},{5,4},{6,7},{7,6},{8,9},{9,8},{10,11... | collective-permute-start | bytes 393224 | tf_op jit(solution)/shard_map/ppermute | solution.py:288
  96.1 2.5 %collective-permute-start.10 = (f32[256,128]{1,0:T(8,128)S(1)}, f32[256,128]{1,0:T(8,128)S(1)}, u32[]{:S(2)}, u32[]{:S(2)}) collective-permute-start(f32[256,128]{1,0:T(8,128)S(1)} %get-tuple-element.34), channel_id=1, source_target_pairs={{0,2},{1,3},{2,0},{3,1},{4,6},{5,7},{6,4},{7,5},{8,10},{9,11},{10,... | collective-permute-start | bytes 393224 | tf_op jit(solution)/shard_map/ppermute | solution.py:288
  98.6 3.4 %collective-permute-start.11 = (f32[256,128]{1,0:T(8,128)S(1)}, f32[256,128]{1,0:T(8,128)S(1)}, u32[]{:S(2)}, u32[]{:S(2)}) collective-permute-start(f32[256,128]{1,0:T(8,128)S(1)} %get-tuple-element.33), channel_id=1, source_target_pairs={{0,3},{1,2},{2,1},{3,0},{4,7},{5,6},{6,5},{7,4},{8,11},{9,10},{10,... | collective-permute-start | bytes 393224 | tf_op jit(solution)/shard_map/ppermute | solution.py:288
  102.0 0.0 collective-permute-done.12
  102.0 0.1 pad_maximum_fusion.refs_0_
  102.1 3.4 %collective-permute-start.13 = (bf16[2,2,64,1024]{3,2,1,0:T(8,128)(2,1)S(1)}, bf16[2,2,64,1024]{3,2,1,0:T(8,128)(2,1)S(1)}, u32[]{:S(2)}, u32[]{:S(2)}) collective-permute-start(bf16[2,2,64,1024]{3,2,1,0:T(8,128)(2,1)S(1)} %pad_maximum_fusion.refs_0_), channel_id=1, source_target_pairs={{0,64},{64,128},{128,192},{192,0},{1,65},{65,129},{129,193},{193,1... | collective-permute-start | bytes 1572872 | tf_op jit(solution)/shard_map/ppermute | solution.py:278
  105.5 4.6 %collective-permute-start.14 = (bf16[2,2,64,1024]{3,2,1,0:T(8,128)(2,1)S(1)}, bf16[2,2,64,1024]{3,2,1,0:T(8,128)(2,1)S(1)}, u32[]{:S(2)}, u32[]{:S(2)}) collective-permute-start(bf16[2,2,64,1024]{3,2,1,0:T(8,128)(2,1)S(1)} %pad_maximum_fusion.refs_0_), channel_id=1, source_target_pairs={{0,128},{64,192},{128,0},{192,64},{1,129},{65,193},{129,1},{193,65... | collective-permute-start | bytes 1572872 | tf_op jit(solution)/shard_map/ppermute | solution.py:278
  110.1 3.6 %collective-permute-done.9.b_ref = f32[256,128]{1,0:T(8,128)S(1)} collective-permute-done((f32[256,128]{1,0:T(8,128)S(1)}, f32[256,128]{1,0:T(8,128)S(1)}, u32[]{:S(2)}, u32[]{:S(2)}) %collective-permute-start.9) | collective-permute-done | bytes 131104 | tf_op jit(solution)/shard_map/ppermute | solution.py:288
  113.7 4.7 %collective-permute-start.15 = (bf16[2,2,64,1024]{3,2,1,0:T(8,128)(2,1)S(1)}, bf16[2,2,64,1024]{3,2,1,0:T(8,128)(2,1)S(1)}, u32[]{:S(2)}, u32[]{:S(2)}) collective-permute-start(bf16[2,2,64,1024]{3,2,1,0:T(8,128)(2,1)S(1)} %pad_maximum_fusion.refs_0_), channel_id=1, source_target_pairs={{0,192},{64,0},{128,64},{192,128},{1,193},{65,1},{129,65},{193,129... | collective-permute-start | bytes 1572872 | tf_op jit(solution)/shard_map/ppermute | solution.py:278
  119.0 6.8 %collective-permute-done.10.c_ref = f32[256,128]{1,0:T(8,128)S(1)} collective-permute-done((f32[256,128]{1,0:T(8,128)S(1)}, f32[256,128]{1,0:T(8,128)S(1)}, u32[]{:S(2)}, u32[]{:S(2)}) %collective-permute-start.10) | collective-permute-done | bytes 131104 | tf_op jit(solution)/shard_map/ppermute | solution.py:288
  125.9 2.5 %collective-permute-done.11.d_ref = f32[256,128]{1,0:T(8,128)S(1)} collective-permute-done((f32[256,128]{1,0:T(8,128)S(1)}, f32[256,128]{1,0:T(8,128)S(1)}, u32[]{:S(2)}, u32[]{:S(2)}) %collective-permute-start.11) | collective-permute-done | bytes 131104 | tf_op jit(solution)/shard_map/ppermute | solution.py:288
  128.4 0.0 all-to-all-done.1.kv_ref
  128.4 4.9 %attend_last.1 = bf16[16,48,128]{2,1,0:T(8,128)(2,1)} custom-call(s32[1]{0:T(128)S(6)} %copy.12.length_ref, s32[1,128]{1,0:T(1,128)S(1)} %copy-done.2, s32[1]{0:T(128)S(6)} %copy.13.count_ref, bf16[512,128]{1,0:T(8,128)(2,1)S(1)} %copy-done.4, bf16[32,192,128]{2,1,0:T(8,128)(2,1)} %all-to-all-done.1.kv_ref, bf16[16,16,128]{2,1,0:T(8,128)(2,1)S(1)} %copy-done.6, ...), custom_call_target="tpu_custom_call" | custom-call | flops 1610612736 | bytes 1572864 | tf_op jit(solution)/shard_map/attend_last/pallas_call | solution.py:202
  133.3 9.0 %all-to-all-start.2 = ((bf16[16,48,128]{2,1,0:T(8,128)(2,1)}), bf16[16,48,128]{2,1,0:T(8,128)(2,1)S(1)}, u32[]{:S(2)}, u32[]{:S(2)}) async-start(bf16[16,48,128]{2,1,0:T(8,128)(2,1)} %attend_last.1), calls=%async_computation.2 | async-start | bytes 393216 | tf_op jit(solution)/shard_map/all_to_all | solution.py:269
  142.4 0.0 collective-permute-done.14.refs_2_
  142.4 0.0 collective-permute-done.15.refs_3_
  142.4 13.3 %all-to-all-done.2.parts_ref = bf16[16,48,128]{2,1,0:T(8,128)(2,1)S(1)} async-done(((bf16[16,48,128]{2,1,0:T(8,128)(2,1)}), bf16[16,48,128]{2,1,0:T(8,128)(2,1)S(1)}, u32[]{:S(2)}, u32[]{:S(2)}) %all-to-all-start.2) | async-done | bytes 196640 | tf_op jit(solution)/shard_map/all_to_all | solution.py:269
  155.8 1.9 %output.1 = bf16[32,1024]{1,0:T(8,128)(2,1)} custom-call(s32[3]{0:T(128)S(1)} %pad_add_fusion.place_ref, s32[1]{0:T(128)S(6)} %sub.7.count_ref, bf16[16,48,128]{2,1,0:T(8,128)(2,1)S(1)} %all-to-all-done.2.parts_ref, bf16[2,2,64,1024]{3,2,1,0:T(8,128)(2,1)S(1)} %pad_maximum_fusion.refs_0_, bf16[2,2,64,1024]{3,2,1,0:T(8,128)(2,1)S(1)} %collective-permute-done.13.refs_1_, ...), custom_call_target="tpu_custom_call" | custom-call | flops 67108864 | bytes 3145728 | tf_op jit(solution)/shard_map/output/pallas_call | solution.py:257
  (25 shorter events, 0.2 us)
Async XLA Ops:
  3.4 10.5 %copy-start = (bf16[32,1,1024]{2,0,1:T(8,128)(2,1)S(1)}, bf16[32,1,1024]{2,0,1:T(8,128)(2,1)}, u32[]{:S(2)}) copy-start(bf16[32,1,1024]{2,0,1:T(8,128)(2,1)} %param.7) | copy-start | bytes 196612
  3.4 49.7 %copy-start.1 = (bf16[1024,128]{1,0:T(8,128)(2,1)S(1)}, bf16[1024,128]{1,0:T(8,128)(2,1)}, u32[]{:S(2)}) copy-start(bf16[1024,128]{1,0:T(8,128)(2,1)} %refs_4_.1) | copy-start | bytes 786436
  3.4 49.7 %copy-start.2 = (s32[1,128]{1,0:T(1,128)S(1)}, s32[1,128]{1,0:T(1,128)}, u32[]{:S(2)}) copy-start(s32[1,128]{1,0:T(1,128)} %mask_ref.3) | copy-start | bytes 1540
  3.4 72.9 %all-to-all-start = ((bf16[8,4,320,128]{3,2,1,0:T(8,128)(2,1)}), bf16[8,4,320,128]{3,2,1,0:T(8,128)(2,1)S(1)}, u32[]{:S(2)}, u32[]{:S(2)}) async-start(bf16[8,4,320,128]{3,2,1,0:T(8,128)(2,1)} %bitcast.36), calls=%async_computation | async-start | bytes 5242880 | tf_op jit(solution)/shard_map/all_to_all | solution.py:269
  13.9 10.8 %collective-permute-start.1 = (bf16[32,1024]{1,0:T(8,128)(2,1)S(1)}, bf16[32,1024]{1,0:T(8,128)(2,1)S(1)}, u32[]{:S(2)}, u32[]{:S(2)}) collective-permute-start(bf16[32,1024]{1,0:T(8,128)(2,1)S(1)} %bitcast.32), channel_id=1, source_target_pairs={{0,256},{256,0},{1,257},{257,1},{2,258},{258,2},{3,259},{259,3},{4... | collective-permute-start | bytes 196616 | tf_op jit(solution)/shard_map/ppermute | solution.py:273
  24.7 3.2 %collective-permute-start.2 = (bf16[2,32,1024]{2,1,0:T(8,128)(2,1)S(1)}, bf16[2,32,1024]{2,1,0:T(8,128)(2,1)S(1)}, u32[]{:S(2)}, u32[]{:S(2)}) collective-permute-start(bf16[2,32,1024]{2,1,0:T(8,128)(2,1)S(1)} %get-tuple-element.40), channel_id=1, source_target_pairs={{0,32},{32,0},{1,33},{33,1},{2,34},{34,2},{3,35},{35,3},{4,36},{36... | collective-permute-start | bytes 393224 | tf_op jit(solution)/shard_map/ppermute | solution.py:273
  28.0 25.1 %collective-permute-start.3 = (bf16[2,2,32,1024]{3,2,1,0:T(8,128)(2,1)S(1)}, bf16[2,2,32,1024]{3,2,1,0:T(8,128)(2,1)S(1)}, u32[]{:S(2)}, u32[]{:S(2)}) collective-permute-start(bf16[2,2,32,1024]{3,2,1,0:T(8,128)(2,1)S(1)} %pad_maximum_fusion.2.refs_0_), channel_id=1, source_target_pairs={{0,64},{64,128},{128,192},{192,0},{1,65},{65,129},{129,193},{193,1... | collective-permute-start | bytes 786440 | tf_op jit(solution)/shard_map/ppermute | solution.py:278
  31.4 21.7 %collective-permute-start.4 = (bf16[2,2,32,1024]{3,2,1,0:T(8,128)(2,1)S(1)}, bf16[2,2,32,1024]{3,2,1,0:T(8,128)(2,1)}, u32[]{:S(2)}, u32[]{:S(2)}) collective-permute-start(bf16[2,2,32,1024]{3,2,1,0:T(8,128)(2,1)S(1)} %pad_maximum_fusion.2.refs_0_), channel_id=1, source_target_pairs={{0,128},{64,192},{128,0},{192,64},{1,129},{65,193},{129,1},{193,65... | collective-permute-start | bytes 786440 | tf_op jit(solution)/shard_map/ppermute | solution.py:278
  36.1 17.1 %collective-permute-start.5 = (bf16[2,2,32,1024]{3,2,1,0:T(8,128)(2,1)S(1)}, bf16[2,2,32,1024]{3,2,1,0:T(8,128)(2,1)}, u32[]{:S(2)}, u32[]{:S(2)}) collective-permute-start(bf16[2,2,32,1024]{3,2,1,0:T(8,128)(2,1)S(1)} %pad_maximum_fusion.2.refs_0_), channel_id=1, source_target_pairs={{0,192},{64,0},{128,64},{192,128},{1,193},{65,1},{129,65},{193,129... | collective-permute-start | bytes 786440 | tf_op jit(solution)/shard_map/ppermute | solution.py:278
  39.4 13.7 %collective-permute-start = (bf16[64,1024]{1,0:T(8,128)(2,1)}, bf16[64,1024]{1,0:T(8,128)(2,1)}, u32[]{:S(2)}, u32[]{:S(2)}) collective-permute-start(bf16[64,1024]{1,0:T(8,128)(2,1)} %param.13), channel_id=1, source_target_pairs={{0,256},{256,0},{1,257},{257,1},{2,258},{258,2},{3,259},{259,3},{4... | collective-permute-start | bytes 393224 | tf_op jit(solution)/shard_map/ppermute | solution.py:273
  55.3 12.0 %copy-start.3 = (bf16[512,128]{1,0:T(8,128)(2,1)}, bf16[512,128]{1,0:T(8,128)(2,1)S(1)}, u32[]{:S(2)}) copy-start(bf16[512,128]{1,0:T(8,128)(2,1)S(1)} %get-tuple-element.27.query_ref) | copy-start | bytes 393220
  55.3 12.0 %copy-start.5 = (bf16[16,16,128]{2,1,0:T(8,128)(2,1)}, bf16[16,16,128]{2,1,0:T(8,128)(2,1)S(1)}, u32[]{:S(2)}) copy-start(bf16[16,16,128]{2,1,0:T(8,128)(2,1)S(1)} %get-tuple-element.29.gate_ref) | copy-start | bytes 196612
  55.3 11.9 %collective-permute-start.8 = (bf16[272,128]{1,0:T(8,128)(2,1)S(1)}, bf16[272,128]{1,0:T(8,128)(2,1)S(1)}, u32[]{:S(2)}, u32[]{:S(2)}) collective-permute-start(bf16[272,128]{1,0:T(8,128)(2,1)S(1)} %get-tuple-element.25), channel_id=1, source_target_pairs={{0,3},{1,2},{2,1},{3,0},{4,7},{5,6},{6,5},{7,4},{8,11},{9,10},{10,... | collective-permute-start | bytes 208904 | tf_op jit(solution)/shard_map/ppermute | solution.py:288
  57.2 10.0 %collective-permute-start.7 = (bf16[272,128]{1,0:T(8,128)(2,1)S(1)}, bf16[272,128]{1,0:T(8,128)(2,1)S(1)}, u32[]{:S(2)}, u32[]{:S(2)}) collective-permute-start(bf16[272,128]{1,0:T(8,128)(2,1)S(1)} %get-tuple-element.25), channel_id=1, source_target_pairs={{0,2},{1,3},{2,0},{3,1},{4,6},{5,7},{6,4},{7,5},{8,10},{9,11},{10,... | collective-permute-start | bytes 208904 | tf_op jit(solution)/shard_map/ppermute | solution.py:288
  61.1 6.2 %collective-permute-start.6 = (bf16[272,128]{1,0:T(8,128)(2,1)S(1)}, bf16[272,128]{1,0:T(8,128)(2,1)S(1)}, u32[]{:S(2)}, u32[]{:S(2)}) collective-permute-start(bf16[272,128]{1,0:T(8,128)(2,1)S(1)} %get-tuple-element.25), channel_id=1, source_target_pairs={{0,1},{1,0},{2,3},{3,2},{4,5},{5,4},{6,7},{7,6},{8,9},{9,8},{10,11... | collective-permute-start | bytes 208904 | tf_op jit(solution)/shard_map/ppermute | solution.py:288
  67.2 15.1 %copy-start.7 = (bf16[64,1024]{1,0:T(8,128)(2,1)S(1)}, bf16[64,1024]{1,0:T(8,128)(2,1)}, u32[]{:S(2)}) copy-start(bf16[64,1024]{1,0:T(8,128)(2,1)} %param.13) | copy-start | bytes 393220
  76.3 52.0 %all-to-all-start.1 = ((bf16[32,192,128]{2,1,0:T(8,128)(2,1)}), bf16[32,192,128]{2,1,0:T(8,128)(2,1)}, u32[]{:S(2)}, u32[]{:S(2)}) async-start(bf16[32,192,128]{2,1,0:T(8,128)(2,1)} %slice.25), calls=%async_computation.1 | async-start | bytes 3145728 | tf_op jit(solution)/shard_map/all_to_all | solution.py:269
  83.2 18.8 %collective-permute-start.12 = (bf16[2,64,1024]{2,1,0:T(8,128)(2,1)S(1)}, bf16[2,64,1024]{2,1,0:T(8,128)(2,1)S(1)}, u32[]{:S(2)}, u32[]{:S(2)}) collective-permute-start(bf16[2,64,1024]{2,1,0:T(8,128)(2,1)S(1)} %get-tuple-element.38), channel_id=1, source_target_pairs={{0,32},{32,0},{1,33},{33,1},{2,34},{34,2},{3,35},{35,3},{4,36},{36... | collective-permute-start | bytes 786440 | tf_op jit(solution)/shard_map/ppermute | solution.py:273
  85.2 43.2 %copy-start.4 = (bf16[512,128]{1,0:T(8,128)(2,1)S(1)}, bf16[512,128]{1,0:T(8,128)(2,1)}, u32[]{:S(2)}) copy-start(bf16[512,128]{1,0:T(8,128)(2,1)} %copy-done.3) | copy-start | bytes 393220
  85.2 43.2 %copy-start.6 = (bf16[16,16,128]{2,1,0:T(8,128)(2,1)S(1)}, bf16[16,16,128]{2,1,0:T(8,128)(2,1)}, u32[]{:S(2)}) copy-start(bf16[16,16,128]{2,1,0:T(8,128)(2,1)} %copy-done.5) | copy-start | bytes 196612
  92.8 20.9 %collective-permute-start.9 = (f32[256,128]{1,0:T(8,128)S(1)}, f32[256,128]{1,0:T(8,128)S(1)}, u32[]{:S(2)}, u32[]{:S(2)}) collective-permute-start(f32[256,128]{1,0:T(8,128)S(1)} %get-tuple-element.35), channel_id=1, source_target_pairs={{0,1},{1,0},{2,3},{3,2},{4,5},{5,4},{6,7},{7,6},{8,9},{9,8},{10,11... | collective-permute-start | bytes 393224 | tf_op jit(solution)/shard_map/ppermute | solution.py:288
  96.1 29.7 %collective-permute-start.10 = (f32[256,128]{1,0:T(8,128)S(1)}, f32[256,128]{1,0:T(8,128)S(1)}, u32[]{:S(2)}, u32[]{:S(2)}) collective-permute-start(f32[256,128]{1,0:T(8,128)S(1)} %get-tuple-element.34), channel_id=1, source_target_pairs={{0,2},{1,3},{2,0},{3,1},{4,6},{5,7},{6,4},{7,5},{8,10},{9,11},{10,... | collective-permute-start | bytes 393224 | tf_op jit(solution)/shard_map/ppermute | solution.py:288
  98.6 29.8 %collective-permute-start.11 = (f32[256,128]{1,0:T(8,128)S(1)}, f32[256,128]{1,0:T(8,128)S(1)}, u32[]{:S(2)}, u32[]{:S(2)}) collective-permute-start(f32[256,128]{1,0:T(8,128)S(1)} %get-tuple-element.33), channel_id=1, source_target_pairs={{0,3},{1,2},{2,1},{3,0},{4,7},{5,6},{6,5},{7,4},{8,11},{9,10},{10,... | collective-permute-start | bytes 393224 | tf_op jit(solution)/shard_map/ppermute | solution.py:288
  102.1 40.3 %collective-permute-start.13 = (bf16[2,2,64,1024]{3,2,1,0:T(8,128)(2,1)S(1)}, bf16[2,2,64,1024]{3,2,1,0:T(8,128)(2,1)S(1)}, u32[]{:S(2)}, u32[]{:S(2)}) collective-permute-start(bf16[2,2,64,1024]{3,2,1,0:T(8,128)(2,1)S(1)} %pad_maximum_fusion.refs_0_), channel_id=1, source_target_pairs={{0,64},{64,128},{128,192},{192,0},{1,65},{65,129},{129,193},{193,1... | collective-permute-start | bytes 1572872 | tf_op jit(solution)/shard_map/ppermute | solution.py:278
  105.5 36.9 %collective-permute-start.14 = (bf16[2,2,64,1024]{3,2,1,0:T(8,128)(2,1)S(1)}, bf16[2,2,64,1024]{3,2,1,0:T(8,128)(2,1)S(1)}, u32[]{:S(2)}, u32[]{:S(2)}) collective-permute-start(bf16[2,2,64,1024]{3,2,1,0:T(8,128)(2,1)S(1)} %pad_maximum_fusion.refs_0_), channel_id=1, source_target_pairs={{0,128},{64,192},{128,0},{192,64},{1,129},{65,193},{129,1},{193,65... | collective-permute-start | bytes 1572872 | tf_op jit(solution)/shard_map/ppermute | solution.py:278
  113.7 28.7 %collective-permute-start.15 = (bf16[2,2,64,1024]{3,2,1,0:T(8,128)(2,1)S(1)}, bf16[2,2,64,1024]{3,2,1,0:T(8,128)(2,1)S(1)}, u32[]{:S(2)}, u32[]{:S(2)}) collective-permute-start(bf16[2,2,64,1024]{3,2,1,0:T(8,128)(2,1)S(1)} %pad_maximum_fusion.refs_0_), channel_id=1, source_target_pairs={{0,192},{64,0},{128,64},{192,128},{1,193},{65,1},{129,65},{193,129... | collective-permute-start | bytes 1572872 | tf_op jit(solution)/shard_map/ppermute | solution.py:278
  133.3 22.4 %all-to-all-start.2 = ((bf16[16,48,128]{2,1,0:T(8,128)(2,1)}), bf16[16,48,128]{2,1,0:T(8,128)(2,1)S(1)}, u32[]{:S(2)}, u32[]{:S(2)}) async-start(bf16[16,48,128]{2,1,0:T(8,128)(2,1)} %attend_last.1), calls=%async_computation.2 | async-start | bytes 393216 | tf_op jit(solution)/shard_map/all_to_all | solution.py:269

commit v6 on v5

--- a/solution.py
+++ b/solution.py
@@ -11,7 +11,7 @@
 D = 1024
 BLK = 128
 FINE = 64
-FIRST = 320
+FIRST = 384
 GRP = ("yh", "x", "c")
 HALF = 64
 PARAMS = pltpu.CompilerParams(vmem_limit_bytes=24 * 1024 * 1024)
@@ -78,15 +78,16 @@
     )(place, length, mask, *quads, w_proj)
 
 
-def attend_tiles(offset, length_ref, mask_ref, count_ref, query_ref, kv_ref, total, masked):
+def attend_tiles(offset, y_ref, length_ref, mask_ref, count_ref, query_ref, kv_ref, total, masked):
     step = pl.program_id(0)
     sources, rows, _ = kv_ref.shape
     lives = []
     for source in range(sources):
+        device = (step * (sources // 4) + source // 4) * 4 + (y_ref[0] ^ (source % 4))
         for block in range(rows // FINE):
-            position = (step * sources + source) * 512 + offset + block * FINE
+            position = device * 512 + offset + block * FINE
             count = jnp.clip(length_ref[0] - position, 0, FINE)
-            lives.append(count * mask_ref[0, (step * sources + source) * 4 + (offset + block * FINE) // BLK])
+            lives.append(count * mask_ref[0, device * 4 + (offset + block * FINE) // BLK])
 
     def attend_rows(chunks):
         row = lax.broadcasted_iota(jnp.int32, (FINE, 128), 0)
@@ -172,13 +173,13 @@
 
 
 def attend_last_kernel(
-    offset, length_ref, mask_ref, count_ref, query_ref, kv_ref, gate_ref, a_ref, b_ref, c_ref, d_ref, out_ref, total, masked
+    offset, y_ref, length_ref, mask_ref, count_ref, query_ref, kv_ref, gate_ref, a_ref, b_ref, c_ref, d_ref, out_ref, total, masked
 ):
     @pl.when(pl.program_id(0) == 0)
     def _():
         total[...] = jnp.zeros_like(total)
 
-    attend_tiles(offset, length_ref, mask_ref, count_ref, query_ref, kv_ref, total, masked)
+    attend_tiles(offset, y_ref, length_ref, mask_ref, count_ref, query_ref, kv_ref, total, masked)
 
     @pl.when(pl.program_id(0) == pl.num_programs(0) - 1)
     def _():
@@ -194,7 +195,7 @@
         out_ref[:, 32:48, :] = gate_ref[...]
 
 
-def attend_last(offset, sources, length, mask, cand_count, query, kv, gate, sums):
+def attend_last(offset, sources, y, length, mask, cand_count, query, kv, gate, sums):
     count = query.shape[0]
     devices, rows, _ = kv.shape
     smem = pl.BlockSpec(memory_space=pltpu.SMEM)
@@ -204,6 +205,7 @@
         out_shape=jax.ShapeDtypeStruct((count // 32, 48, 128), jnp.bfloat16),
         grid=(devices // sources,),
         in_specs=[
+            smem,
             smem,
             smem,
             smem,
@@ -219,7 +221,7 @@
             flops=4 * count * positions * 128, bytes_accessed=positions * 256, transcendentals=count * positions
         ),
         name="attend_last",
-    )(length, mask, cand_count, query, kv, gate, *sums)
+    )(y, length, mask, cand_count, query, kv, gate, *sums)
 
 
 def spread_heads(packed):
@@ -273,8 +275,12 @@
     return lax.ppermute(values, axis, [(0, 1), (1, 0)])
 
 
-def go_round(pair):
-    quad = jnp.stack([pair, swap(pair, "c")])
+def both_cores(own, other):
+    pair = jnp.stack([own, other])
+    return jnp.stack([pair, swap(pair, "c")])
+
+
+def go_round(quad):
     return [quad] + [lax.ppermute(quad, "x", [(i, (i + turns) % 4) for i in range(4)]) for turns in (1, 2, 3)]
 
 
@@ -287,24 +293,30 @@
     def along_y(values, step):
         return lax.ppermute(values, "yl", [(i, i ^ step) for i in range(4)])
 
-    second = hist_kv[:, FIRST:]
+    second = hist_kv.reshape(8, 4, 512, 128)[:, :, FIRST:]
     plane = exchange(hist_kv[:, :FIRST].reshape(8, 4, FIRST, 128), "z")
     other_rows, other_w = swap(rows, "yh"), swap(w_out, "yh")
-    quads = go_round(jnp.stack([rows, other_rows]))
-    other_w, *quads = lax.optimization_barrier((other_w, *quads))
+    quads = go_round(both_cores(rows, other_rows))
+    second, _ = lax.optimization_barrier((second, other_rows))
+    staged = [lax.dynamic_index_in_dim(second, y ^ step, 1, keepdims=False) for step in range(4)]
+    staged = jnp.stack([staged[0]] + [along_y(staged[step], step) for step in (1, 2, 3)], axis=1)
+    other_w, staged, *quads = lax.optimization_barrier((other_w, staged, *quads))
     query, gate, message = project(place, hist_len, block_mask, quads, w_proj)
     messages = jnp.stack([message] + [along_y(message, step) for step in (1, 2, 3)])
-    plane, second, query, gate, messages, other_w = lax.optimization_barrier(
-        (plane, second, query, gate, messages, other_w)
+    live = messages[:, 256].astype(jnp.int32).reshape(4, 8, 4, 4)
+    live = lax.dynamic_index_in_dim(live, y, 2, keepdims=False)[:, :, : -(-FIRST // BLK)].reshape(-1)
+    message, other_w = lax.optimization_barrier((message, other_w))
+    w_quad = both_cores(w_out, other_w)
+    plane, staged, query, gate, messages, live, w_quad = lax.optimization_barrier(
+        (plane, staged, query, gate, messages, live, w_quad)
     )
-    rest = exchange(second, ("z", "yl"))
-
-    live = messages[:, 256].astype(jnp.int32).reshape(4, 8, 4, 4)
-    live = lax.dynamic_index_in_dim(live, y, 2, keepdims=False)[:, :, : -(-FIRST // BLK)]
-    part = attend_plane(y.reshape(1), live.reshape(-1), messages, plane)
+    rest = exchange(staged, "z").reshape(32, 512 - FIRST, 128)
+
+    part = attend_plane(y.reshape(1), live, messages, plane)
     sums = [part[0]] + [along_y(part[step], step) for step in (1, 2, 3)]
-    w_quads = go_round(jnp.stack([w_out, other_w]))
-    attended = attend_last(FIRST, 8, hist_len, block_mask, cand_count, query, rest, gate, sums)
+    part, w_quad = lax.optimization_barrier((part, w_quad))
+    w_quads = go_round(w_quad)
+    attended = attend_last(FIRST, 16, y.reshape(1), hist_len, block_mask, cand_count, query, rest, gate, sums)
     keep = cand_count - lax.axis_index(GRP) * own_rows
     parts = exchange(attended, GRP)
     return output(place, keep, parts, w_quads, rows).reshape(cand_x.shape)

time: 159 us -> 153 us (0.962)
  the two profiles are of different devices: /device:TPU:16 before, /device:TPU:8 now
where the time goes in v6:
time: 153 us; the launch traced here: 151 us
  starting transfers between devices  93.5 us (61%)
  waiting for transfers between devices  20.2 us (13%)
  Pallas kernels  16.8 us (11%)
  local copies, waits for them, and re-layouts  13.7 us (9%)
  other arithmetic  5.27 us (3%)
  between operations  1.75 us (1%)
    ppermute x9, starting transfers between devices, along_y(): return lax.ppermute(values, 'yl', [(i, i ^ step) for i in range(4)])  28.8 us
    ppermute x6, starting transfers between devices, go_round(): lax.ppermute(quad, 'x', [(i, (i + turns) % 4) for i in range(4)])  23.5 us
    all_to_all x3, starting transfers between devices, exchange(): return lax.all_to_all(values, axes, split_axis=0, concat_axis=0, tiled=True)  23.1 us
    ppermute x4, starting transfers between devices, swap(): return lax.ppermute(values, axis, [(0, 1), (1, 0)])  18.2 us
    pallas_call x1, Pallas kernels, attend_plane(): pl.pallas_call(attend_plane_kernel, out_shape=jax.ShapeDtypeStruct((users...  8.84 us
    all_to_all x3, waiting for transfers between devices, exchange(): return lax.all_to_all(values, axes, split_axis=0, concat_axis=0, tiled=True)  8.22 us
    ppermute x6, waiting for transfers between devices, go_round(): lax.ppermute(quad, 'x', [(i, (i + turns) % 4) for i in range(4)])  5.99 us
    slice x1, local copies, waits for them, and re-layouts, per_device(): plane = exchange(hist_kv[:, :FIRST].reshape(8, 4, FIRST, 128), 'z')  3.87 us
  transfers between devices with their start and end apart: 22, of which 8 were waited for; matrix products, arithmetic and copies ran while one was open for 8% of the time, Pallas kernels for 10%

profile of v6, /device:TPU:8, one launch (start us, length us, event | category | flops | bytes accessed | tf_op | source)
XLA Modules:
  0.0 151.3 jit_solution(11184468690256458266)
XLA Ops:
  0.0 3.9 %slice.24 = bf16[32,384,128]{2,1,0:T(8,128)(2,1)} slice(bf16[32,512,128]{2,1,0:T(8,128)(2,1)} %param.8), slice={[0:32], [0:384], [0:128]} | slice | bytes 6291456 | tf_op jit(solution)/shard_map/slice | solution.py:297
  3.9 10.4 %all-to-all-start = ((bf16[8,4,384,128]{3,2,1,0:T(8,128)(2,1)}), bf16[8,4,384,128]{3,2,1,0:T(8,128)(2,1)S(1)}, u32[]{:S(2)}, u32[]{:S(2)}) async-start(bf16[8,4,384,128]{3,2,1,0:T(8,128)(2,1)} %bitcast.47), calls=%async_computation | async-start | bytes 6291456 | tf_op jit(solution)/shard_map/all_to_all | solution.py:271
  14.3 6.8 %collective-permute-start.1 = (bf16[32,1024]{1,0:T(8,128)(2,1)S(1)}, bf16[32,1024]{1,0:T(8,128)(2,1)S(1)}, u32[]{:S(2)}, u32[]{:S(2)}) collective-permute-start(bf16[32,1024]{1,0:T(8,128)(2,1)S(1)} %bitcast.43), channel_id=1, source_target_pairs={{0,256},{256,0},{1,257},{257,1},{2,258},{258,2},{3,259},{259,3},{4... | collective-permute-start | bytes 196616 | tf_op jit(solution)/shard_map/ppermute | solution.py:275
  21.2 2.3 %slice.32 = bf16[8,4,128,128]{3,2,1,0:T(8,128)(2,1)} slice(bf16[8,4,512,128]{3,2,1,0:T(8,128)(2,1)} %bitcast.48), slice={[0:8], [0:4], [384:512], [0:128]} | slice | bytes 2097152 | tf_op jit(solution)/shard_map/slice | solution.py:296
  23.5 1.0 collective-permute-done.1
  24.5 2.1 %constant_dynamic-slice_fusion.1 = (bf16[8,1,128,128]{3,2,1,0:T(8,128)(2,1)}, bf16[8,128,128]{2,1,0:T(8,128)(2,1)S(1)}, bf16[8,128,128]{2,1,0:T(8,128)(2,1)}, bf16[8,128,128]{2,1,0:T(8,128)(2,1)}) fusion(bf16[8,4,128,128]{3,2,1,0:T(8,128)(2,1)} %slice.32, s32[]{:T(128)S(6)} %select_n.15, s32[]{:T(128)S(6)} %select_n.18, s32[]{:T(128)S(6)} %select_n.17, ...), kind=kLoop, calls=%fused_computation.16 | loop fusion | bytes 2097168 | tf_op jit(solution)/shard_map/jit(dynamic_index_in_dim)/dynamic_slice | solution.py:301
  26.6 4.1 %collective-permute-start.4 = (bf16[8,128,128]{2,1,0:T(8,128)(2,1)S(1)}, bf16[8,128,128]{2,1,0:T(8,128)(2,1)S(1)}, u32[]{:S(2)}, u32[]{:S(2)}) collective-permute-start(bf16[8,128,128]{2,1,0:T(8,128)(2,1)S(1)} %get-tuple-element.44), channel_id=1, source_target_pairs={{0,3},{1,2},{2,1},{3,0},{4,7},{5,6},{6,5},{7,4},{8,11},{9,10},{10,... | collective-permute-start | bytes 786440 | tf_op jit(solution)/shard_map/ppermute | solution.py:294
  30.8 1.9 %collective-permute-start.5 = (bf16[2,32,1024]{2,1,0:T(8,128)(2,1)S(1)}, bf16[2,32,1024]{2,1,0:T(8,128)(2,1)S(1)}, u32[]{:S(2)}, u32[]{:S(2)}) collective-permute-start(bf16[2,32,1024]{2,1,0:T(8,128)(2,1)S(1)} %get-tuple-element.54), channel_id=1, source_target_pairs={{0,32},{32,0},{1,33},{33,1},{2,34},{34,2},{3,35},{35,3},{4,36},{36... | collective-permute-start | bytes 393224 | tf_op jit(solution)/shard_map/ppermute | solution.py:275
  32.7 2.6 %collective-permute-start.3 = (bf16[8,128,128]{2,1,0:T(8,128)(2,1)}, bf16[8,128,128]{2,1,0:T(8,128)(2,1)}, u32[]{:S(2)}, u32[]{:S(2)}) collective-permute-start(bf16[8,128,128]{2,1,0:T(8,128)(2,1)} %get-tuple-element.45), channel_id=1, source_target_pairs={{0,2},{1,3},{2,0},{3,1},{4,6},{5,7},{6,4},{7,5},{8,10},{9,11},{10,... | collective-permute-start | bytes 786440 | tf_op jit(solution)/shard_map/ppermute | solution.py:294
  35.4 2.9 %collective-permute-start.2 = (bf16[8,128,128]{2,1,0:T(8,128)(2,1)}, bf16[8,128,128]{2,1,0:T(8,128)(2,1)}, u32[]{:S(2)}, u32[]{:S(2)}) collective-permute-start(bf16[8,128,128]{2,1,0:T(8,128)(2,1)} %get-tuple-element.46), channel_id=1, source_target_pairs={{0,1},{1,0},{2,3},{3,2},{4,5},{5,4},{6,7},{7,6},{8,9},{9,8},{10,11... | collective-permute-start | bytes 786440 | tf_op jit(solution)/shard_map/ppermute | solution.py:294
  38.3 3.4 %collective-permute-start.6 = (bf16[2,2,32,1024]{3,2,1,0:T(8,128)(2,1)S(1)}, bf16[2,2,32,1024]{3,2,1,0:T(8,128)(2,1)}, u32[]{:S(2)}, u32[]{:S(2)}) collective-permute-start(bf16[2,2,32,1024]{3,2,1,0:T(8,128)(2,1)S(1)} %pad_maximum_fusion.3.refs_0_), channel_id=1, source_target_pairs={{0,64},{64,128},{128,192},{192,0},{1,65},{65,129},{129,193},{193,1... | collective-permute-start | bytes 786440 | tf_op jit(solution)/shard_map/ppermute | solution.py:284
  41.7 4.6 %collective-permute-start.7 = (bf16[2,2,32,1024]{3,2,1,0:T(8,128)(2,1)S(1)}, bf16[2,2,32,1024]{3,2,1,0:T(8,128)(2,1)}, u32[]{:S(2)}, u32[]{:S(2)}) collective-permute-start(bf16[2,2,32,1024]{3,2,1,0:T(8,128)(2,1)S(1)} %pad_maximum_fusion.3.refs_0_), channel_id=1, source_target_pairs={{0,128},{64,192},{128,0},{192,64},{1,129},{65,193},{129,1},{193,65... | collective-permute-start | bytes 786440 | tf_op jit(solution)/shard_map/ppermute | solution.py:284
  46.4 1.6 %collective-permute-done.4 = bf16[8,128,128]{2,1,0:T(8,128)(2,1)S(1)} collective-permute-done((bf16[8,128,128]{2,1,0:T(8,128)(2,1)S(1)}, bf16[8,128,128]{2,1,0:T(8,128)(2,1)S(1)}, u32[]{:S(2)}, u32[]{:S(2)}) %collective-permute-start.4) | collective-permute-done | bytes 262176 | tf_op jit(solution)/shard_map/ppermute | solution.py:294
  48.0 0.7 copy-done.7
  48.7 4.7 %collective-permute-start.8 = (bf16[2,2,32,1024]{3,2,1,0:T(8,128)(2,1)S(1)}, bf16[2,2,32,1024]{3,2,1,0:T(8,128)(2,1)}, u32[]{:S(2)}, u32[]{:S(2)}) collective-permute-start(bf16[2,2,32,1024]{3,2,1,0:T(8,128)(2,1)S(1)} %pad_maximum_fusion.3.refs_0_), channel_id=1, source_target_pairs={{0,192},{64,0},{128,64},{192,128},{1,193},{65,1},{129,65},{193,129... | collective-permute-start | bytes 786440 | tf_op jit(solution)/shard_map/ppermute | solution.py:284
  54.2 7.5 %collective-permute-start = (bf16[64,1024]{1,0:T(8,128)(2,1)}, bf16[64,1024]{1,0:T(8,128)(2,1)S(1)}, u32[]{:S(2)}, u32[]{:S(2)}) collective-permute-start(bf16[64,1024]{1,0:T(8,128)(2,1)} %param.13), channel_id=1, source_target_pairs={{0,256},{256,0},{1,257},{257,1},{2,258},{258,2},{3,259},{259,3},{4... | collective-permute-start | bytes 393224 | tf_op jit(solution)/shard_map/ppermute | solution.py:275
  61.7 2.3 %pad_maximum_fusion = bf16[8,4,128,128]{3,2,1,0:T(8,128)(2,1)} fusion(bf16[8,1,128,128]{3,2,1,0:T(8,128)(2,1)} %bitcast.49, bf16[8,1,128,128]{3,2,1,0:T(8,128)(2,1)} %bitcast.11, bf16[8,1,128,128]{3,2,1,0:T(8,128)(2,1)} %bitcast.9, bf16[8,1,128,128]{3,2,1,0:T(8,128)(2,1)} %get-tuple-element.43), kind=kLoop, calls=%fused_computation | loop fusion | flops 1572864 | bytes 2097152 | tf_op jit(solution)/shard_map/stack | solution.py:302
  64.0 2.8 %collective-permute-done = bf16[64,1024]{1,0:T(8,128)(2,1)S(1)} collective-permute-done((bf16[64,1024]{1,0:T(8,128)(2,1)}, bf16[64,1024]{1,0:T(8,128)(2,1)S(1)}, u32[]{:S(2)}, u32[]{:S(2)}) %collective-permute-start) | collective-permute-done | bytes 131104 | tf_op jit(solution)/shard_map/ppermute | solution.py:275
  66.9 0.9 copy-done.1
  67.8 2.2 %project.1 = (bf16[512,128]{1,0:T(8,128)(2,1)S(1)}, bf16[16,16,128]{2,1,0:T(8,128)(2,1)S(1)}, bf16[272,128]{1,0:T(8,128)(2,1)S(1)}) custom-call(s32[3]{0:T(128)S(1)} %pad_add_fusion.place_ref, s32[1]{0:T(128)S(6)} %copy.12.length_ref, s32[1,128]{1,0:T(1,128)S(1)} %copy-done.2, bf16[2,2,32,1024]{3,2,1,0:T(8,128)(2,1)S(1)} %pad_maximum_fusion.3.refs_0_, ...), custom_call_target="tpu_custom_call" | custom-call | flops 134217728 | bytes 2097152 | tf_op jit(solution)/shard_map/project/pallas_call | solution.py:66
  70.1 4.6 %collective-permute-start.11 = (bf16[272,128]{1,0:T(8,128)(2,1)S(1)}, bf16[272,128]{1,0:T(8,128)(2,1)S(1)}, u32[]{:S(2)}, u32[]{:S(2)}) collective-permute-start(bf16[272,128]{1,0:T(8,128)(2,1)S(1)} %get-tuple-element.32), channel_id=1, source_target_pairs={{0,3},{1,2},{2,1},{3,0},{4,7},{5,6},{6,5},{7,4},{8,11},{9,10},{10,... | collective-permute-start | bytes 208904 | tf_op jit(solution)/shard_map/ppermute | solution.py:294
  74.7 2.4 %collective-permute-start.10 = (bf16[272,128]{1,0:T(8,128)(2,1)S(1)}, bf16[272,128]{1,0:T(8,128)(2,1)S(1)}, u32[]{:S(2)}, u32[]{:S(2)}) collective-permute-start(bf16[272,128]{1,0:T(8,128)(2,1)S(1)} %get-tuple-element.32), channel_id=1, source_target_pairs={{0,2},{1,3},{2,0},{3,1},{4,6},{5,7},{6,4},{7,5},{8,10},{9,11},{10,... | collective-permute-start | bytes 208904 | tf_op jit(solution)/shard_map/ppermute | solution.py:294
  77.1 2.9 %collective-permute-start.9 = (bf16[272,128]{1,0:T(8,128)(2,1)S(1)}, bf16[272,128]{1,0:T(8,128)(2,1)S(1)}, u32[]{:S(2)}, u32[]{:S(2)}) collective-permute-start(bf16[272,128]{1,0:T(8,128)(2,1)S(1)} %get-tuple-element.32), channel_id=1, source_target_pairs={{0,1},{1,0},{2,3},{3,2},{4,5},{5,4},{6,7},{7,6},{8,9},{9,8},{10,11... | collective-permute-start | bytes 208904 | tf_op jit(solution)/shard_map/ppermute | solution.py:294
  80.0 0.9 fusion.2
  80.9 1.9 %collective-permute-start.12 = (bf16[2,64,1024]{2,1,0:T(8,128)(2,1)}, bf16[2,64,1024]{2,1,0:T(8,128)(2,1)}, u32[]{:S(2)}, u32[]{:S(2)}) collective-permute-start(bf16[2,64,1024]{2,1,0:T(8,128)(2,1)} %get-tuple-element.52), channel_id=1, source_target_pairs={{0,32},{32,0},{1,33},{33,1},{2,34},{34,2},{3,35},{35,3},{4,36},{36... | collective-permute-start | bytes 786440 | tf_op jit(solution)/shard_map/ppermute | solution.py:275
  82.8 0.5 collective-permute-done.9
  83.4 0.8 reshape.33
  84.2 0.9 constant_dynamic-slice_fusion
  85.1 0.1 copy.11
  85.2 0.1 reshape.30.live_ref
  85.4 1.9 %pad_maximum_fusion.1.refs_0_ = bf16[2,2,64,1024]{3,2,1,0:T(8,128)(2,1)} fusion(bf16[1,2,64,1024]{3,2,1,0:T(8,128)(2,1)} %bitcast.26, bf16[1,2,64,1024]{3,2,1,0:T(8,128)(2,1)} %get-tuple-element.51), kind=kLoop, calls=%fused_computation.1 | loop fusion | flops 262144 | bytes 1048576 | tf_op jit(solution)/shard_map/stack | solution.py:280
  87.2 0.9 all-to-all-done.kv_ref
  88.1 4.8 %all-to-all-start.1 = ((bf16[8,4,128,128]{3,2,1,0:T(8,128)(2,1)}), bf16[8,4,128,128]{3,2,1,0:T(8,128)(2,1)}, u32[]{:S(2)}, u32[]{:S(2)}) async-start(bf16[8,4,128,128]{3,2,1,0:T(8,128)(2,1)} %pad_maximum_fusion), calls=%async_computation.1 | async-start | bytes 2097152 | tf_op jit(solution)/shard_map/all_to_all | solution.py:271
  93.0 8.8 %attend_plane.1 = f32[4,256,128]{2,1,0:T(8,128)S(1)} custom-call(s32[1]{0:T(128)} %bitcast.4.y_ref, s32[96]{0:T(128)S(1)} %reshape.30.live_ref, bf16[4,272,128]{2,1,0:T(8,128)(2,1)S(1)} %pad_maximum_fusion.2.message_ref, bf16[8,4,384,128]{3,2,1,0:T(8,128)(2,1)S(1)} %all-to-all-done.kv_ref), custom_call_target="tpu_custom_call" | custom-call | flops 1073741824 | bytes 3145728 | tf_op jit(solution)/shard_map/attend_plane/pallas_call | solution.py:155
  101.8 2.7 %collective-permute-start.13 = (f32[256,128]{1,0:T(8,128)S(1)}, f32[256,128]{1,0:T(8,128)S(1)}, u32[]{:S(2)}, u32[]{:S(2)}) collective-permute-start(f32[256,128]{1,0:T(8,128)S(1)} %get-tuple-element.49), channel_id=1, source_target_pairs={{0,1},{1,0},{2,3},{3,2},{4,5},{5,4},{6,7},{7,6},{8,9},{9,8},{10,11... | collective-permute-start | bytes 393224 | tf_op jit(solution)/shard_map/ppermute | solution.py:294
  104.6 4.2 %collective-permute-start.14 = (f32[256,128]{1,0:T(8,128)S(1)}, f32[256,128]{1,0:T(8,128)S(1)}, u32[]{:S(2)}, u32[]{:S(2)}) collective-permute-start(f32[256,128]{1,0:T(8,128)S(1)} %get-tuple-element.48), channel_id=1, source_target_pairs={{0,2},{1,3},{2,0},{3,1},{4,6},{5,7},{6,4},{7,5},{8,10},{9,11},{10,... | collective-permute-start | bytes 393224 | tf_op jit(solution)/shard_map/ppermute | solution.py:294
  108.7 2.3 %collective-permute-start.15 = (f32[256,128]{1,0:T(8,128)S(1)}, f32[256,128]{1,0:T(8,128)S(1)}, u32[]{:S(2)}, u32[]{:S(2)}) collective-permute-start(f32[256,128]{1,0:T(8,128)S(1)} %get-tuple-element.47), channel_id=1, source_target_pairs={{0,3},{1,2},{2,1},{3,0},{4,7},{5,6},{6,5},{7,4},{8,11},{9,10},{10,... | collective-permute-start | bytes 393224 | tf_op jit(solution)/shard_map/ppermute | solution.py:294
  111.1 2.8 %collective-permute-start.16 = (bf16[2,2,64,1024]{3,2,1,0:T(8,128)(2,1)}, bf16[2,2,64,1024]{3,2,1,0:T(8,128)(2,1)S(1)}, u32[]{:S(2)}, u32[]{:S(2)}) collective-permute-start(bf16[2,2,64,1024]{3,2,1,0:T(8,128)(2,1)} %pad_maximum_fusion.1.refs_0_), channel_id=1, source_target_pairs={{0,64},{64,128},{128,192},{192,0},{1,65},{65,129},{129,193},{193,1... | collective-permute-start | bytes 1572872 | tf_op jit(solution)/shard_map/ppermute | solution.py:284
  113.9 4.6 %collective-permute-start.17 = (bf16[2,2,64,1024]{3,2,1,0:T(8,128)(2,1)}, bf16[2,2,64,1024]{3,2,1,0:T(8,128)(2,1)S(1)}, u32[]{:S(2)}, u32[]{:S(2)}) collective-permute-start(bf16[2,2,64,1024]{3,2,1,0:T(8,128)(2,1)} %pad_maximum_fusion.1.refs_0_), channel_id=1, source_target_pairs={{0,128},{64,192},{128,0},{192,64},{1,129},{65,193},{129,1},{193,65... | collective-permute-start | bytes 1572872 | tf_op jit(solution)/shard_map/ppermute | solution.py:284
  118.6 3.3 %collective-permute-start.18 = (bf16[2,2,64,1024]{3,2,1,0:T(8,128)(2,1)}, bf16[2,2,64,1024]{3,2,1,0:T(8,128)(2,1)S(1)}, u32[]{:S(2)}, u32[]{:S(2)}) collective-permute-start(bf16[2,2,64,1024]{3,2,1,0:T(8,128)(2,1)} %pad_maximum_fusion.1.refs_0_), channel_id=1, source_target_pairs={{0,192},{64,0},{128,64},{192,128},{1,193},{65,1},{129,65},{193,129... | collective-permute-start | bytes 1572872 | tf_op jit(solution)/shard_map/ppermute | solution.py:284
  122.6 0.9 copy-done.4
  123.5 0.8 copy-done.6
  124.3 3.4 %attend_last.1 = bf16[16,48,128]{2,1,0:T(8,128)(2,1)} custom-call(s32[1]{0:T(128)} %bitcast.4.y_ref, s32[1]{0:T(128)S(6)} %copy.12.length_ref, s32[1,128]{1,0:T(1,128)S(1)} %copy-done.2, s32[1]{0:T(128)S(6)} %copy.13.count_ref, bf16[512,128]{1,0:T(8,128)(2,1)S(1)} %copy-done.4, bf16[32,128,128]{2,1,0:T(8,128)(2,1)} %bitcast.27.kv_ref, ...), custom_call_target="tpu_custom_call" | custom-call | flops 1073741824 | bytes 1048576 | tf_op jit(solution)/shard_map/attend_last/pallas_call | solution.py:203
  127.8 7.8 %all-to-all-start.2 = ((bf16[16,48,128]{2,1,0:T(8,128)(2,1)}), bf16[16,48,128]{2,1,0:T(8,128)(2,1)S(1)}, u32[]{:S(2)}, u32[]{:S(2)}) async-start(bf16[16,48,128]{2,1,0:T(8,128)(2,1)} %attend_last.1), calls=%async_computation.2 | async-start | bytes 393216 | tf_op jit(solution)/shard_map/all_to_all | solution.py:271
  135.6 3.5 %collective-permute-done.17.refs_2_ = bf16[2,2,64,1024]{3,2,1,0:T(8,128)(2,1)S(1)} collective-permute-done((bf16[2,2,64,1024]{3,2,1,0:T(8,128)(2,1)}, bf16[2,2,64,1024]{3,2,1,0:T(8,128)(2,1)S(1)}, u32[]{:S(2)}, u32[]{:S(2)}) %collective-permute-start.17) | collective-permute-done | bytes 524320 | tf_op jit(solution)/shard_map/ppermute | solution.py:284
  139.1 2.5 %collective-permute-done.18.refs_3_ = bf16[2,2,64,1024]{3,2,1,0:T(8,128)(2,1)S(1)} collective-permute-done((bf16[2,2,64,1024]{3,2,1,0:T(8,128)(2,1)}, bf16[2,2,64,1024]{3,2,1,0:T(8,128)(2,1)S(1)}, u32[]{:S(2)}, u32[]{:S(2)}) %collective-permute-start.18) | collective-permute-done | bytes 524320 | tf_op jit(solution)/shard_map/ppermute | solution.py:284
  141.5 7.4 %all-to-all-done.2.parts_ref = bf16[16,48,128]{2,1,0:T(8,128)(2,1)S(1)} async-done(((bf16[16,48,128]{2,1,0:T(8,128)(2,1)}), bf16[16,48,128]{2,1,0:T(8,128)(2,1)S(1)}, u32[]{:S(2)}, u32[]{:S(2)}) %all-to-all-start.2) | async-done | bytes 196640 | tf_op jit(solution)/shard_map/all_to_all | solution.py:271
  148.9 2.4 %output.1 = bf16[32,1024]{1,0:T(8,128)(2,1)} custom-call(s32[3]{0:T(128)S(1)} %pad_add_fusion.place_ref, s32[1]{0:T(128)S(6)} %sub.7.count_ref, bf16[16,48,128]{2,1,0:T(8,128)(2,1)S(1)} %all-to-all-done.2.parts_ref, bf16[2,2,64,1024]{3,2,1,0:T(8,128)(2,1)} %pad_maximum_fusion.1.refs_0_, bf16[2,2,64,1024]{3,2,1,0:T(8,128)(2,1)S(1)} %collective-permute-done.16.refs_1_, ...), custom_call_target="tpu_custom_call" | custom-call | flops 67108864 | bytes 3145728 | tf_op jit(solution)/shard_map/output/pallas_call | solution.py:259
  (35 shorter events, 0.4 us)
Async XLA Ops:
  3.9 10.5 %copy-start = (bf16[32,1,1024]{2,0,1:T(8,128)(2,1)S(1)}, bf16[32,1,1024]{2,0,1:T(8,128)(2,1)}, u32[]{:S(2)}) copy-start(bf16[32,1,1024]{2,0,1:T(8,128)(2,1)} %param.7) | copy-start | bytes 196612
  3.9 84.2 %all-to-all-start = ((bf16[8,4,384,128]{3,2,1,0:T(8,128)(2,1)}), bf16[8,4,384,128]{3,2,1,0:T(8,128)(2,1)S(1)}, u32[]{:S(2)}, u32[]{:S(2)}) async-start(bf16[8,4,384,128]{3,2,1,0:T(8,128)(2,1)} %bitcast.47), calls=%async_computation | async-start | bytes 6291456 | tf_op jit(solution)/shard_map/all_to_all | solution.py:271
  14.3 10.2 %collective-permute-start.1 = (bf16[32,1024]{1,0:T(8,128)(2,1)S(1)}, bf16[32,1024]{1,0:T(8,128)(2,1)S(1)}, u32[]{:S(2)}, u32[]{:S(2)}) collective-permute-start(bf16[32,1024]{1,0:T(8,128)(2,1)S(1)} %bitcast.43), channel_id=1, source_target_pairs={{0,256},{256,0},{1,257},{257,1},{2,258},{258,2},{3,259},{259,3},{4... | collective-permute-start | bytes 196616 | tf_op jit(solution)/shard_map/ppermute | solution.py:275
  21.2 45.7 %copy-start.2 = (s32[1,128]{1,0:T(1,128)S(1)}, s32[1,128]{1,0:T(1,128)}, u32[]{:S(2)}) copy-start(s32[1,128]{1,0:T(1,128)} %mask_ref.3) | copy-start | bytes 1540
  26.6 21.4 %collective-permute-start.4 = (bf16[8,128,128]{2,1,0:T(8,128)(2,1)S(1)}, bf16[8,128,128]{2,1,0:T(8,128)(2,1)S(1)}, u32[]{:S(2)}, u32[]{:S(2)}) collective-permute-start(bf16[8,128,128]{2,1,0:T(8,128)(2,1)S(1)} %get-tuple-element.44), channel_id=1, source_target_pairs={{0,3},{1,2},{2,1},{3,0},{4,7},{5,6},{6,5},{7,4},{8,11},{9,10},{10,... | collective-permute-start | bytes 786440 | tf_op jit(solution)/shard_map/ppermute | solution.py:294
  30.8 7.5 %collective-permute-start.5 = (bf16[2,32,1024]{2,1,0:T(8,128)(2,1)S(1)}, bf16[2,32,1024]{2,1,0:T(8,128)(2,1)S(1)}, u32[]{:S(2)}, u32[]{:S(2)}) collective-permute-start(bf16[2,32,1024]{2,1,0:T(8,128)(2,1)S(1)} %get-tuple-element.54), channel_id=1, source_target_pairs={{0,32},{32,0},{1,33},{33,1},{2,34},{34,2},{3,35},{35,3},{4,36},{36... | collective-permute-start | bytes 393224 | tf_op jit(solution)/shard_map/ppermute | solution.py:275
  32.7 21.5 %collective-permute-start.3 = (bf16[8,128,128]{2,1,0:T(8,128)(2,1)}, bf16[8,128,128]{2,1,0:T(8,128)(2,1)}, u32[]{:S(2)}, u32[]{:S(2)}) collective-permute-start(bf16[8,128,128]{2,1,0:T(8,128)(2,1)} %get-tuple-element.45), channel_id=1, source_target_pairs={{0,2},{1,3},{2,0},{3,1},{4,6},{5,7},{6,4},{7,5},{8,10},{9,11},{10,... | collective-permute-start | bytes 786440 | tf_op jit(solution)/shard_map/ppermute | solution.py:294
  35.4 26.3 %collective-permute-start.2 = (bf16[8,128,128]{2,1,0:T(8,128)(2,1)}, bf16[8,128,128]{2,1,0:T(8,128)(2,1)}, u32[]{:S(2)}, u32[]{:S(2)}) collective-permute-start(bf16[8,128,128]{2,1,0:T(8,128)(2,1)} %get-tuple-element.46), channel_id=1, source_target_pairs={{0,1},{1,0},{2,3},{3,2},{4,5},{5,4},{6,7},{7,6},{8,9},{9,8},{10,11... | collective-permute-start | bytes 786440 | tf_op jit(solution)/shard_map/ppermute | solution.py:294
  38.3 28.5 %collective-permute-start.6 = (bf16[2,2,32,1024]{3,2,1,0:T(8,128)(2,1)S(1)}, bf16[2,2,32,1024]{3,2,1,0:T(8,128)(2,1)}, u32[]{:S(2)}, u32[]{:S(2)}) collective-permute-start(bf16[2,2,32,1024]{3,2,1,0:T(8,128)(2,1)S(1)} %pad_maximum_fusion.3.refs_0_), channel_id=1, source_target_pairs={{0,64},{64,128},{128,192},{192,0},{1,65},{65,129},{129,193},{193,1... | collective-permute-start | bytes 786440 | tf_op jit(solution)/shard_map/ppermute | solution.py:284
  41.7 25.1 %collective-permute-start.7 = (bf16[2,2,32,1024]{3,2,1,0:T(8,128)(2,1)S(1)}, bf16[2,2,32,1024]{3,2,1,0:T(8,128)(2,1)}, u32[]{:S(2)}, u32[]{:S(2)}) collective-permute-start(bf16[2,2,32,1024]{3,2,1,0:T(8,128)(2,1)S(1)} %pad_maximum_fusion.3.refs_0_), channel_id=1, source_target_pairs={{0,128},{64,192},{128,0},{192,64},{1,129},{65,193},{129,1},{193,65... | collective-permute-start | bytes 786440 | tf_op jit(solution)/shard_map/ppermute | solution.py:284
  48.0 0.7 copy-start.7
  48.7 18.1 %collective-permute-start.8 = (bf16[2,2,32,1024]{3,2,1,0:T(8,128)(2,1)S(1)}, bf16[2,2,32,1024]{3,2,1,0:T(8,128)(2,1)}, u32[]{:S(2)}, u32[]{:S(2)}) collective-permute-start(bf16[2,2,32,1024]{3,2,1,0:T(8,128)(2,1)S(1)} %pad_maximum_fusion.3.refs_0_), channel_id=1, source_target_pairs={{0,192},{64,0},{128,64},{192,128},{1,193},{65,1},{129,65},{193,129... | collective-permute-start | bytes 786440 | tf_op jit(solution)/shard_map/ppermute | solution.py:284
  53.4 26.6 %copy-start.8 = (bf16[64,1024]{1,0:T(8,128)(2,1)S(1)}, bf16[64,1024]{1,0:T(8,128)(2,1)}, u32[]{:S(2)}) copy-start(bf16[64,1024]{1,0:T(8,128)(2,1)} %param.13) | copy-start | bytes 393220
  54.2 12.7 %collective-permute-start = (bf16[64,1024]{1,0:T(8,128)(2,1)}, bf16[64,1024]{1,0:T(8,128)(2,1)S(1)}, u32[]{:S(2)}, u32[]{:S(2)}) collective-permute-start(bf16[64,1024]{1,0:T(8,128)(2,1)} %param.13), channel_id=1, source_target_pairs={{0,256},{256,0},{1,257},{257,1},{2,258},{258,2},{3,259},{259,3},{4... | collective-permute-start | bytes 393224 | tf_op jit(solution)/shard_map/ppermute | solution.py:275
  66.9 1.0 copy-start.1
  70.0 13.3 %copy-start.3 = (bf16[512,128]{1,0:T(8,128)(2,1)}, bf16[512,128]{1,0:T(8,128)(2,1)S(1)}, u32[]{:S(2)}) copy-start(bf16[512,128]{1,0:T(8,128)(2,1)S(1)} %get-tuple-element.35.query_ref) | copy-start | bytes 393220
  70.0 13.3 %copy-start.5 = (bf16[16,16,128]{2,1,0:T(8,128)(2,1)}, bf16[16,16,128]{2,1,0:T(8,128)(2,1)S(1)}, u32[]{:S(2)}) copy-start(bf16[16,16,128]{2,1,0:T(8,128)(2,1)S(1)} %get-tuple-element.37.gate_ref) | copy-start | bytes 196612
  70.1 12.8 %collective-permute-start.11 = (bf16[272,128]{1,0:T(8,128)(2,1)S(1)}, bf16[272,128]{1,0:T(8,128)(2,1)S(1)}, u32[]{:S(2)}, u32[]{:S(2)}) collective-permute-start(bf16[272,128]{1,0:T(8,128)(2,1)S(1)} %get-tuple-element.32), channel_id=1, source_target_pairs={{0,3},{1,2},{2,1},{3,0},{4,7},{5,6},{6,5},{7,4},{8,11},{9,10},{10,... | collective-permute-start | bytes 208904 | tf_op jit(solution)/shard_map/ppermute | solution.py:294
  74.7 8.1 %collective-permute-start.10 = (bf16[272,128]{1,0:T(8,128)(2,1)S(1)}, bf16[272,128]{1,0:T(8,128)(2,1)S(1)}, u32[]{:S(2)}, u32[]{:S(2)}) collective-permute-start(bf16[272,128]{1,0:T(8,128)(2,1)S(1)} %get-tuple-element.32), channel_id=1, source_target_pairs={{0,2},{1,3},{2,0},{3,1},{4,6},{5,7},{6,4},{7,5},{8,10},{9,11},{10,... | collective-permute-start | bytes 208904 | tf_op jit(solution)/shard_map/ppermute | solution.py:294
  77.1 6.2 %collective-permute-start.9 = (bf16[272,128]{1,0:T(8,128)(2,1)S(1)}, bf16[272,128]{1,0:T(8,128)(2,1)S(1)}, u32[]{:S(2)}, u32[]{:S(2)}) collective-permute-start(bf16[272,128]{1,0:T(8,128)(2,1)S(1)} %get-tuple-element.32), channel_id=1, source_target_pairs={{0,1},{1,0},{2,3},{3,2},{4,5},{5,4},{6,7},{7,6},{8,9},{9,8},{10,11... | collective-permute-start | bytes 208904 | tf_op jit(solution)/shard_map/ppermute | solution.py:294
  80.9 4.5 %collective-permute-start.12 = (bf16[2,64,1024]{2,1,0:T(8,128)(2,1)}, bf16[2,64,1024]{2,1,0:T(8,128)(2,1)}, u32[]{:S(2)}, u32[]{:S(2)}) collective-permute-start(bf16[2,64,1024]{2,1,0:T(8,128)(2,1)} %get-tuple-element.52), channel_id=1, source_target_pairs={{0,32},{32,0},{1,33},{33,1},{2,34},{34,2},{3,35},{35,3},{4,36},{36... | collective-permute-start | bytes 786440 | tf_op jit(solution)/shard_map/ppermute | solution.py:275
  88.1 34.5 %all-to-all-start.1 = ((bf16[8,4,128,128]{3,2,1,0:T(8,128)(2,1)}), bf16[8,4,128,128]{3,2,1,0:T(8,128)(2,1)}, u32[]{:S(2)}, u32[]{:S(2)}) async-start(bf16[8,4,128,128]{3,2,1,0:T(8,128)(2,1)} %pad_maximum_fusion), calls=%async_computation.1 | async-start | bytes 2097152 | tf_op jit(solution)/shard_map/all_to_all | solution.py:271
  101.8 16.7 %collective-permute-start.13 = (f32[256,128]{1,0:T(8,128)S(1)}, f32[256,128]{1,0:T(8,128)S(1)}, u32[]{:S(2)}, u32[]{:S(2)}) collective-permute-start(f32[256,128]{1,0:T(8,128)S(1)} %get-tuple-element.49), channel_id=1, source_target_pairs={{0,1},{1,0},{2,3},{3,2},{4,5},{5,4},{6,7},{7,6},{8,9},{9,8},{10,11... | collective-permute-start | bytes 393224 | tf_op jit(solution)/shard_map/ppermute | solution.py:294
  104.6 18.0 %collective-permute-start.14 = (f32[256,128]{1,0:T(8,128)S(1)}, f32[256,128]{1,0:T(8,128)S(1)}, u32[]{:S(2)}, u32[]{:S(2)}) collective-permute-start(f32[256,128]{1,0:T(8,128)S(1)} %get-tuple-element.48), channel_id=1, source_target_pairs={{0,2},{1,3},{2,0},{3,1},{4,6},{5,7},{6,4},{7,5},{8,10},{9,11},{10,... | collective-permute-start | bytes 393224 | tf_op jit(solution)/shard_map/ppermute | solution.py:294
  108.7 13.9 %collective-permute-start.15 = (f32[256,128]{1,0:T(8,128)S(1)}, f32[256,128]{1,0:T(8,128)S(1)}, u32[]{:S(2)}, u32[]{:S(2)}) collective-permute-start(f32[256,128]{1,0:T(8,128)S(1)} %get-tuple-element.47), channel_id=1, source_target_pairs={{0,3},{1,2},{2,1},{3,0},{4,7},{5,6},{6,5},{7,4},{8,11},{9,10},{10,... | collective-permute-start | bytes 393224 | tf_op jit(solution)/shard_map/ppermute | solution.py:294
  111.1 24.5 %collective-permute-start.16 = (bf16[2,2,64,1024]{3,2,1,0:T(8,128)(2,1)}, bf16[2,2,64,1024]{3,2,1,0:T(8,128)(2,1)S(1)}, u32[]{:S(2)}, u32[]{:S(2)}) collective-permute-start(bf16[2,2,64,1024]{3,2,1,0:T(8,128)(2,1)} %pad_maximum_fusion.1.refs_0_), channel_id=1, source_target_pairs={{0,64},{64,128},{128,192},{192,0},{1,65},{65,129},{129,193},{193,1... | collective-permute-start | bytes 1572872 | tf_op jit(solution)/shard_map/ppermute | solution.py:284
  113.9 25.2 %collective-permute-start.17 = (bf16[2,2,64,1024]{3,2,1,0:T(8,128)(2,1)}, bf16[2,2,64,1024]{3,2,1,0:T(8,128)(2,1)S(1)}, u32[]{:S(2)}, u32[]{:S(2)}) collective-permute-start(bf16[2,2,64,1024]{3,2,1,0:T(8,128)(2,1)} %pad_maximum_fusion.1.refs_0_), channel_id=1, source_target_pairs={{0,128},{64,192},{128,0},{192,64},{1,129},{65,193},{129,1},{193,65... | collective-permute-start | bytes 1572872 | tf_op jit(solution)/shard_map/ppermute | solution.py:284
  118.6 23.0 %collective-permute-start.18 = (bf16[2,2,64,1024]{3,2,1,0:T(8,128)(2,1)}, bf16[2,2,64,1024]{3,2,1,0:T(8,128)(2,1)S(1)}, u32[]{:S(2)}, u32[]{:S(2)}) collective-permute-start(bf16[2,2,64,1024]{3,2,1,0:T(8,128)(2,1)} %pad_maximum_fusion.1.refs_0_), channel_id=1, source_target_pairs={{0,192},{64,0},{128,64},{192,128},{1,193},{65,1},{129,65},{193,129... | collective-permute-start | bytes 1572872 | tf_op jit(solution)/shard_map/ppermute | solution.py:284
  122.6 0.9 copy-start.4
  123.5 0.8 copy-start.6
  127.8 21.1 %all-to-all-start.2 = ((bf16[16,48,128]{2,1,0:T(8,128)(2,1)}), bf16[16,48,128]{2,1,0:T(8,128)(2,1)S(1)}, u32[]{:S(2)}, u32[]{:S(2)}) async-start(bf16[16,48,128]{2,1,0:T(8,128)(2,1)} %attend_last.1), calls=%async_computation.2 | async-start | bytes 393216 | tf_op jit(solution)/shard_map/all_to_all | solution.py:271

commit v7 on v6

--- a/solution.py
+++ b/solution.py
@@ -295,9 +295,10 @@
 
     second = hist_kv.reshape(8, 4, 512, 128)[:, :, FIRST:]
     plane = exchange(hist_kv[:, :FIRST].reshape(8, 4, FIRST, 128), "z")
-    other_rows, other_w = swap(rows, "yh"), swap(w_out, "yh")
+    other = swap(jnp.concatenate([rows, w_out]), "yh")
+    other_rows, other_w = other[:own_rows], other[own_rows:]
     quads = go_round(both_cores(rows, other_rows))
-    second, _ = lax.optimization_barrier((second, other_rows))
+    second, _ = lax.optimization_barrier((second, other))
     staged = [lax.dynamic_index_in_dim(second, y ^ step, 1, keepdims=False) for step in range(4)]
     staged = jnp.stack([staged[0]] + [along_y(staged[step], step) for step in (1, 2, 3)], axis=1)
     other_w, staged, *quads = lax.optimization_barrier((other_w, staged, *quads))

time: 153 us -> 151 us (0.987)
  starting transfers between devices: 93.5 us -> 85.5 us
  waiting for transfers between devices: 20.2 us -> 27.3 us
    ppermute x4 -> x3, starting transfers between devices: 18.2 us -> 10.7 us  [swap(): return lax.ppermute(values, axis, [(0, 1), (1, 0)])]
    ppermute x6, waiting for transfers between devices: 5.99 us -> 11.6 us  [go_round(): lax.ppermute(quad, 'x', [(i, (i + turns) % 4) for i in range(4)])]
    ppermute x4 -> x3, waiting for transfers between devices: 3.81 us -> 5.89 us  [swap(): return lax.ppermute(values, axis, [(0, 1), (1, 0)])]
    all_to_all x3, starting transfers between devices: 23.1 us -> 21.5 us  [exchange(): return lax.all_to_all(values, axes, split_axis=0, concat_axis=0, tiled=True)]
    unnamed x18 -> x22, local copies, waits for them, and re-layouts: 3.41 us -> 3.36 us
  transfers between devices with their start and end apart: 22 -> 21, of which waited for: 8 -> 9; matrix products, arithmetic and copies ran while one was open for 8% -> 7% of each run, Pallas kernels for 10% -> 10%
where the time goes in v7:
time: 151 us; the launch traced here: 149 us
  starting transfers between devices  85.5 us (57%)
  waiting for transfers between devices  27.3 us (18%)
  Pallas kernels  16.6 us (11%)
  local copies, waits for them, and re-layouts  12.2 us (8%)
  other arithmetic  5.86 us (4%)
  between operations  1.78 us (1%)
    ppermute x9, starting transfers between devices, along_y(): return lax.ppermute(values, 'yl', [(i, i ^ step) for i in range(4)])  29.3 us
    ppermute x6, starting transfers between devices, go_round(): lax.ppermute(quad, 'x', [(i, (i + turns) % 4) for i in range(4)])  24.1 us
    all_to_all x3, starting transfers between devices, exchange(): return lax.all_to_all(values, axes, split_axis=0, concat_axis=0, tiled=True)  21.5 us
    ppermute x6, waiting for transfers between devices, go_round(): lax.ppermute(quad, 'x', [(i, (i + turns) % 4) for i in range(4)])  11.6 us
    ppermute x3, starting transfers between devices, swap(): return lax.ppermute(values, axis, [(0, 1), (1, 0)])  10.7 us
    pallas_call x1, Pallas kernels, attend_plane(): pl.pallas_call(attend_plane_kernel, out_shape=jax.ShapeDtypeStruct((users...  8.84 us
    all_to_all x3, waiting for transfers between devices, exchange(): return lax.all_to_all(values, axes, split_axis=0, concat_axis=0, tiled=True)  8.75 us
    ppermute x3, waiting for transfers between devices, swap(): return lax.ppermute(values, axis, [(0, 1), (1, 0)])  5.89 us
  transfers between devices with their start and end apart: 21, of which 9 were waited for; matrix products, arithmetic and copies ran while one was open for 7% of the time, Pallas kernels for 10%

profile of v7, /device:TPU:8, one launch (start us, length us, event | category | flops | bytes accessed | tf_op | source)
XLA Modules:
  0.0 149.3 jit_solution(567271390225381297)
XLA Ops:
  0.0 3.9 %slice.30 = bf16[32,384,128]{2,1,0:T(8,128)(2,1)} slice(bf16[32,512,128]{2,1,0:T(8,128)(2,1)} %param.8), slice={[0:32], [0:384], [0:128]} | slice | bytes 6291456 | tf_op jit(solution)/shard_map/slice | solution.py:297
  3.9 10.4 %all-to-all-start = ((bf16[8,4,384,128]{3,2,1,0:T(8,128)(2,1)}), bf16[8,4,384,128]{3,2,1,0:T(8,128)(2,1)S(1)}, u32[]{:S(2)}, u32[]{:S(2)}) async-start(bf16[8,4,384,128]{3,2,1,0:T(8,128)(2,1)} %bitcast.48), calls=%async_computation | async-start | bytes 6291456 | tf_op jit(solution)/shard_map/all_to_all | solution.py:271
  14.3 0.7 pad_maximum_fusion.5
  15.0 6.8 %collective-permute-start = (bf16[96,1024]{1,0:T(8,128)(2,1)}, bf16[96,1024]{1,0:T(8,128)(2,1)S(1)}, u32[]{:S(2)}, u32[]{:S(2)}) collective-permute-start(bf16[96,1024]{1,0:T(8,128)(2,1)} %pad_maximum_fusion.5), channel_id=1, source_target_pairs={{0,256},{256,0},{1,257},{257,1},{2,258},{258,2},{3,259},{259,3},{4... | collective-permute-start | bytes 589832 | tf_op jit(solution)/shard_map/ppermute | solution.py:275
  21.9 2.3 %slice.41 = bf16[8,4,128,128]{3,2,1,0:T(8,128)(2,1)} slice(bf16[8,4,512,128]{3,2,1,0:T(8,128)(2,1)} %bitcast.49), slice={[0:8], [0:4], [384:512], [0:128]} | slice | bytes 2097152 | tf_op jit(solution)/shard_map/slice | solution.py:296
  24.2 5.9 %collective-permute-done = bf16[96,1024]{1,0:T(8,128)(2,1)S(1)} collective-permute-done((bf16[96,1024]{1,0:T(8,128)(2,1)}, bf16[96,1024]{1,0:T(8,128)(2,1)S(1)}, u32[]{:S(2)}, u32[]{:S(2)}) %collective-permute-start) | collective-permute-done | bytes 196640 | tf_op jit(solution)/shard_map/ppermute | solution.py:275
  30.1 2.2 %constant_dynamic-slice_fusion.1 = (bf16[8,1,128,128]{3,2,1,0:T(8,128)(2,1)}, bf16[8,128,128]{2,1,0:T(8,128)(2,1)S(1)}, bf16[8,128,128]{2,1,0:T(8,128)(2,1)}, bf16[8,128,128]{2,1,0:T(8,128)(2,1)}) fusion(bf16[8,4,128,128]{3,2,1,0:T(8,128)(2,1)} %slice.41, s32[]{:T(128)S(6)} %select_n.15, s32[]{:T(128)S(6)} %select_n.18, s32[]{:T(128)S(6)} %select_n.17, ...), kind=kLoop, calls=%fused_computation.18 | loop fusion | bytes 2097168 | tf_op jit(solution)/shard_map/jit(dynamic_index_in_dim)/dynamic_slice | solution.py:302
  32.2 5.0 %collective-permute-start.3 = (bf16[8,128,128]{2,1,0:T(8,128)(2,1)S(1)}, bf16[8,128,128]{2,1,0:T(8,128)(2,1)S(1)}, u32[]{:S(2)}, u32[]{:S(2)}) collective-permute-start(bf16[8,128,128]{2,1,0:T(8,128)(2,1)S(1)} %get-tuple-element.44), channel_id=1, source_target_pairs={{0,3},{1,2},{2,1},{3,0},{4,7},{5,6},{6,5},{7,4},{8,11},{9,10},{10,... | collective-permute-start | bytes 786440 | tf_op jit(solution)/shard_map/ppermute | solution.py:294
  37.3 1.9 %collective-permute-start.4 = (bf16[2,32,1024]{2,1,0:T(8,128)(2,1)S(1)}, bf16[2,32,1024]{2,1,0:T(8,128)(2,1)S(1)}, u32[]{:S(2)}, u32[]{:S(2)}) collective-permute-start(bf16[2,32,1024]{2,1,0:T(8,128)(2,1)S(1)} %get-tuple-element.54), channel_id=1, source_target_pairs={{0,32},{32,0},{1,33},{33,1},{2,34},{34,2},{3,35},{35,3},{4,36},{36... | collective-permute-start | bytes 393224 | tf_op jit(solution)/shard_map/ppermute | solution.py:275
  39.3 1.9 %collective-permute-start.2 = (bf16[8,128,128]{2,1,0:T(8,128)(2,1)}, bf16[8,128,128]{2,1,0:T(8,128)(2,1)}, u32[]{:S(2)}, u32[]{:S(2)}) collective-permute-start(bf16[8,128,128]{2,1,0:T(8,128)(2,1)} %get-tuple-element.45), channel_id=1, source_target_pairs={{0,2},{1,3},{2,0},{3,1},{4,6},{5,7},{6,4},{7,5},{8,10},{9,11},{10,... | collective-permute-start | bytes 786440 | tf_op jit(solution)/shard_map/ppermute | solution.py:294
  41.2 3.4 %collective-permute-start.1 = (bf16[8,128,128]{2,1,0:T(8,128)(2,1)}, bf16[8,128,128]{2,1,0:T(8,128)(2,1)}, u32[]{:S(2)}, u32[]{:S(2)}) collective-permute-start(bf16[8,128,128]{2,1,0:T(8,128)(2,1)} %get-tuple-element.46), channel_id=1, source_target_pairs={{0,1},{1,0},{2,3},{3,2},{4,5},{5,4},{6,7},{7,6},{8,9},{9,8},{10,11... | collective-permute-start | bytes 786440 | tf_op jit(solution)/shard_map/ppermute | solution.py:294
  44.6 3.4 %collective-permute-start.5 = (bf16[2,2,32,1024]{3,2,1,0:T(8,128)(2,1)S(1)}, bf16[2,2,32,1024]{3,2,1,0:T(8,128)(2,1)}, u32[]{:S(2)}, u32[]{:S(2)}) collective-permute-start(bf16[2,2,32,1024]{3,2,1,0:T(8,128)(2,1)S(1)} %pad_maximum_fusion.3.refs_0_), channel_id=1, source_target_pairs={{0,64},{64,128},{128,192},{192,0},{1,65},{65,129},{129,193},{193,1... | collective-permute-start | bytes 786440 | tf_op jit(solution)/shard_map/ppermute | solution.py:284
  48.0 4.6 %collective-permute-start.6 = (bf16[2,2,32,1024]{3,2,1,0:T(8,128)(2,1)S(1)}, bf16[2,2,32,1024]{3,2,1,0:T(8,128)(2,1)}, u32[]{:S(2)}, u32[]{:S(2)}) collective-permute-start(bf16[2,2,32,1024]{3,2,1,0:T(8,128)(2,1)S(1)} %pad_maximum_fusion.3.refs_0_), channel_id=1, source_target_pairs={{0,128},{64,192},{128,0},{192,64},{1,129},{65,193},{129,1},{193,65... | collective-permute-start | bytes 786440 | tf_op jit(solution)/shard_map/ppermute | solution.py:284
  52.7 0.4 collective-permute-done.3
  53.1 0.7 copy-done.10
  53.8 4.7 %collective-permute-start.7 = (bf16[2,2,32,1024]{3,2,1,0:T(8,128)(2,1)S(1)}, bf16[2,2,32,1024]{3,2,1,0:T(8,128)(2,1)}, u32[]{:S(2)}, u32[]{:S(2)}) collective-permute-start(bf16[2,2,32,1024]{3,2,1,0:T(8,128)(2,1)S(1)} %pad_maximum_fusion.3.refs_0_), channel_id=1, source_target_pairs={{0,192},{64,0},{128,64},{192,128},{1,193},{65,1},{129,65},{193,129... | collective-permute-start | bytes 786440 | tf_op jit(solution)/shard_map/ppermute | solution.py:284
  59.3 2.3 %pad_maximum_fusion = bf16[8,4,128,128]{3,2,1,0:T(8,128)(2,1)} fusion(bf16[8,1,128,128]{3,2,1,0:T(8,128)(2,1)} %bitcast.52, bf16[8,1,128,128]{3,2,1,0:T(8,128)(2,1)} %bitcast.11, bf16[8,1,128,128]{3,2,1,0:T(8,128)(2,1)} %bitcast.9, bf16[8,1,128,128]{3,2,1,0:T(8,128)(2,1)} %get-tuple-element.43), kind=kLoop, calls=%fused_computation | loop fusion | flops 1572864 | bytes 2097152 | tf_op jit(solution)/shard_map/stack | solution.py:303
  61.6 1.0 collective-permute-done.6.refs_2_
  62.6 1.5 %collective-permute-done.7.refs_3_ = bf16[2,2,32,1024]{3,2,1,0:T(8,128)(2,1)} collective-permute-done((bf16[2,2,32,1024]{3,2,1,0:T(8,128)(2,1)S(1)}, bf16[2,2,32,1024]{3,2,1,0:T(8,128)(2,1)}, u32[]{:S(2)}, u32[]{:S(2)}) %collective-permute-start.7) | collective-permute-done | bytes 262176 | tf_op jit(solution)/shard_map/ppermute | solution.py:284
  64.1 0.9 copy-done.3
  65.0 2.2 %project.1 = (bf16[512,128]{1,0:T(8,128)(2,1)S(1)}, bf16[16,16,128]{2,1,0:T(8,128)(2,1)S(1)}, bf16[272,128]{1,0:T(8,128)(2,1)S(1)}) custom-call(s32[3]{0:T(128)S(1)} %pad_add_fusion.place_ref, s32[1]{0:T(128)S(6)} %copy.12.length_ref, s32[1,128]{1,0:T(1,128)S(1)} %copy-done.4, bf16[2,2,32,1024]{3,2,1,0:T(8,128)(2,1)S(1)} %pad_maximum_fusion.3.refs_0_, ...), custom_call_target="tpu_custom_call" | custom-call | flops 134217728 | bytes 2097152 | tf_op jit(solution)/shard_map/project/pallas_call | solution.py:66
  67.3 4.5 %collective-permute-start.10 = (bf16[272,128]{1,0:T(8,128)(2,1)S(1)}, bf16[272,128]{1,0:T(8,128)(2,1)S(1)}, u32[]{:S(2)}, u32[]{:S(2)}) collective-permute-start(bf16[272,128]{1,0:T(8,128)(2,1)S(1)} %get-tuple-element.32), channel_id=1, source_target_pairs={{0,3},{1,2},{2,1},{3,0},{4,7},{5,6},{6,5},{7,4},{8,11},{9,10},{10,... | collective-permute-start | bytes 208904 | tf_op jit(solution)/shard_map/ppermute | solution.py:294
  71.8 2.5 %collective-permute-start.9 = (bf16[272,128]{1,0:T(8,128)(2,1)S(1)}, bf16[272,128]{1,0:T(8,128)(2,1)S(1)}, u32[]{:S(2)}, u32[]{:S(2)}) collective-permute-start(bf16[272,128]{1,0:T(8,128)(2,1)S(1)} %get-tuple-element.32), channel_id=1, source_target_pairs={{0,2},{1,3},{2,0},{3,1},{4,6},{5,7},{6,4},{7,5},{8,10},{9,11},{10,... | collective-permute-start | bytes 208904 | tf_op jit(solution)/shard_map/ppermute | solution.py:294
  74.3 2.8 %collective-permute-start.8 = (bf16[272,128]{1,0:T(8,128)(2,1)S(1)}, bf16[272,128]{1,0:T(8,128)(2,1)S(1)}, u32[]{:S(2)}, u32[]{:S(2)}) collective-permute-start(bf16[272,128]{1,0:T(8,128)(2,1)S(1)} %get-tuple-element.32), channel_id=1, source_target_pairs={{0,1},{1,0},{2,3},{3,2},{4,5},{5,4},{6,7},{7,6},{8,9},{9,8},{10,11... | collective-permute-start | bytes 208904 | tf_op jit(solution)/shard_map/ppermute | solution.py:294
  77.1 0.8 fusion.2
  77.9 1.9 %collective-permute-start.11 = (bf16[2,64,1024]{2,1,0:T(8,128)(2,1)}, bf16[2,64,1024]{2,1,0:T(8,128)(2,1)}, u32[]{:S(2)}, u32[]{:S(2)}) collective-permute-start(bf16[2,64,1024]{2,1,0:T(8,128)(2,1)} %get-tuple-element.52), channel_id=1, source_target_pairs={{0,32},{32,0},{1,33},{33,1},{2,34},{34,2},{3,35},{35,3},{4,36},{36... | collective-permute-start | bytes 786440 | tf_op jit(solution)/shard_map/ppermute | solution.py:275
  79.9 0.6 collective-permute-done.8
  80.6 0.7 copy-done.1
  81.3 0.1 reshape.33
  81.6 0.1 copy.11
  81.7 0.1 reshape.30.live_ref
  81.8 1.9 %pad_maximum_fusion.1.refs_0_ = bf16[2,2,64,1024]{3,2,1,0:T(8,128)(2,1)} fusion(bf16[1,2,64,1024]{3,2,1,0:T(8,128)(2,1)} %bitcast.26, bf16[1,2,64,1024]{3,2,1,0:T(8,128)(2,1)} %get-tuple-element.51), kind=kLoop, calls=%fused_computation.1 | loop fusion | flops 262144 | bytes 1048576 | tf_op jit(solution)/shard_map/stack | solution.py:280
  83.6 4.5 %all-to-all-done.kv_ref = bf16[8,4,384,128]{3,2,1,0:T(8,128)(2,1)S(1)} async-done(((bf16[8,4,384,128]{3,2,1,0:T(8,128)(2,1)}), bf16[8,4,384,128]{3,2,1,0:T(8,128)(2,1)S(1)}, u32[]{:S(2)}, u32[]{:S(2)}) %all-to-all-start) | async-done | bytes 3145760 | tf_op jit(solution)/shard_map/all_to_all | solution.py:271
  88.1 4.2 %all-to-all-start.1 = ((bf16[8,4,128,128]{3,2,1,0:T(8,128)(2,1)}), bf16[8,4,128,128]{3,2,1,0:T(8,128)(2,1)}, u32[]{:S(2)}, u32[]{:S(2)}) async-start(bf16[8,4,128,128]{3,2,1,0:T(8,128)(2,1)} %pad_maximum_fusion), calls=%async_computation.1 | async-start | bytes 2097152 | tf_op jit(solution)/shard_map/all_to_all | solution.py:271
  92.4 0.9 copy-done.2
  93.3 8.8 %attend_plane.1 = f32[4,256,128]{2,1,0:T(8,128)S(1)} custom-call(s32[1]{0:T(128)} %bitcast.4.y_ref, s32[96]{0:T(128)S(1)} %reshape.30.live_ref, bf16[4,272,128]{2,1,0:T(8,128)(2,1)S(1)} %copy-done.2, bf16[8,4,384,128]{3,2,1,0:T(8,128)(2,1)S(1)} %all-to-all-done.kv_ref), custom_call_target="tpu_custom_call" | custom-call | flops 1073741824 | bytes 3145728 | tf_op jit(solution)/shard_map/attend_plane/pallas_call | solution.py:155
  102.2 2.4 %collective-permute-start.12 = (f32[256,128]{1,0:T(8,128)S(1)}, f32[256,128]{1,0:T(8,128)S(1)}, u32[]{:S(2)}, u32[]{:S(2)}) collective-permute-start(f32[256,128]{1,0:T(8,128)S(1)} %get-tuple-element.49), channel_id=1, source_target_pairs={{0,1},{1,0},{2,3},{3,2},{4,5},{5,4},{6,7},{7,6},{8,9},{9,8},{10,11... | collective-permute-start | bytes 393224 | tf_op jit(solution)/shard_map/ppermute | solution.py:294
  104.6 4.5 %collective-permute-start.13 = (f32[256,128]{1,0:T(8,128)S(1)}, f32[256,128]{1,0:T(8,128)S(1)}, u32[]{:S(2)}, u32[]{:S(2)}) collective-permute-start(f32[256,128]{1,0:T(8,128)S(1)} %get-tuple-element.48), channel_id=1, source_target_pairs={{0,2},{1,3},{2,0},{3,1},{4,6},{5,7},{6,4},{7,5},{8,10},{9,11},{10,... | collective-permute-start | bytes 393224 | tf_op jit(solution)/shard_map/ppermute | solution.py:294
  109.1 2.4 %collective-permute-start.14 = (f32[256,128]{1,0:T(8,128)S(1)}, f32[256,128]{1,0:T(8,128)S(1)}, u32[]{:S(2)}, u32[]{:S(2)}) collective-permute-start(f32[256,128]{1,0:T(8,128)S(1)} %get-tuple-element.47), channel_id=1, source_target_pairs={{0,3},{1,2},{2,1},{3,0},{4,7},{5,6},{6,5},{7,4},{8,11},{9,10},{10,... | collective-permute-start | bytes 393224 | tf_op jit(solution)/shard_map/ppermute | solution.py:294
  111.4 3.4 %collective-permute-start.15 = (bf16[2,2,64,1024]{3,2,1,0:T(8,128)(2,1)}, bf16[2,2,64,1024]{3,2,1,0:T(8,128)(2,1)S(1)}, u32[]{:S(2)}, u32[]{:S(2)}) collective-permute-start(bf16[2,2,64,1024]{3,2,1,0:T(8,128)(2,1)} %pad_maximum_fusion.1.refs_0_), channel_id=1, source_target_pairs={{0,64},{64,128},{128,192},{192,0},{1,65},{65,129},{129,193},{193,1... | collective-permute-start | bytes 1572872 | tf_op jit(solution)/shard_map/ppermute | solution.py:284
  114.8 4.6 %collective-permute-start.16 = (bf16[2,2,64,1024]{3,2,1,0:T(8,128)(2,1)}, bf16[2,2,64,1024]{3,2,1,0:T(8,128)(2,1)S(1)}, u32[]{:S(2)}, u32[]{:S(2)}) collective-permute-start(bf16[2,2,64,1024]{3,2,1,0:T(8,128)(2,1)} %pad_maximum_fusion.1.refs_0_), channel_id=1, source_target_pairs={{0,128},{64,192},{128,0},{192,64},{1,129},{65,193},{129,1},{193,65... | collective-permute-start | bytes 1572872 | tf_op jit(solution)/shard_map/ppermute | solution.py:284
  119.5 3.3 %collective-permute-start.17 = (bf16[2,2,64,1024]{3,2,1,0:T(8,128)(2,1)}, bf16[2,2,64,1024]{3,2,1,0:T(8,128)(2,1)S(1)}, u32[]{:S(2)}, u32[]{:S(2)}) collective-permute-start(bf16[2,2,64,1024]{3,2,1,0:T(8,128)(2,1)} %pad_maximum_fusion.1.refs_0_), channel_id=1, source_target_pairs={{0,192},{64,0},{128,64},{192,128},{1,193},{65,1},{129,65},{193,129... | collective-permute-start | bytes 1572872 | tf_op jit(solution)/shard_map/ppermute | solution.py:284
  123.5 3.2 %attend_last.1 = bf16[16,48,128]{2,1,0:T(8,128)(2,1)} custom-call(s32[1]{0:T(128)} %bitcast.4.y_ref, s32[1]{0:T(128)S(6)} %copy.12.length_ref, s32[1,128]{1,0:T(1,128)S(1)} %copy-done.4, s32[1]{0:T(128)S(6)} %copy.13.count_ref, bf16[512,128]{1,0:T(8,128)(2,1)S(1)} %copy-done.6, bf16[32,128,128]{2,1,0:T(8,128)(2,1)} %bitcast.27.kv_ref, ...), custom_call_target="tpu_custom_call" | custom-call | flops 1073741824 | bytes 1048576 | tf_op jit(solution)/shard_map/attend_last/pallas_call | solution.py:203
  126.7 6.8 %all-to-all-start.2 = ((bf16[16,48,128]{2,1,0:T(8,128)(2,1)}), bf16[16,48,128]{2,1,0:T(8,128)(2,1)S(1)}, u32[]{:S(2)}, u32[]{:S(2)}) async-start(bf16[16,48,128]{2,1,0:T(8,128)(2,1)} %attend_last.1), calls=%async_computation.2 | async-start | bytes 393216 | tf_op jit(solution)/shard_map/all_to_all | solution.py:271
  133.5 7.0 %collective-permute-done.16.refs_2_ = bf16[2,2,64,1024]{3,2,1,0:T(8,128)(2,1)S(1)} collective-permute-done((bf16[2,2,64,1024]{3,2,1,0:T(8,128)(2,1)}, bf16[2,2,64,1024]{3,2,1,0:T(8,128)(2,1)S(1)}, u32[]{:S(2)}, u32[]{:S(2)}) %collective-permute-start.16) | collective-permute-done | bytes 524320 | tf_op jit(solution)/shard_map/ppermute | solution.py:284
  140.6 2.0 %collective-permute-done.17.refs_3_ = bf16[2,2,64,1024]{3,2,1,0:T(8,128)(2,1)S(1)} collective-permute-done((bf16[2,2,64,1024]{3,2,1,0:T(8,128)(2,1)}, bf16[2,2,64,1024]{3,2,1,0:T(8,128)(2,1)S(1)}, u32[]{:S(2)}, u32[]{:S(2)}) %collective-permute-start.17) | collective-permute-done | bytes 524320 | tf_op jit(solution)/shard_map/ppermute | solution.py:284
  142.6 4.3 %all-to-all-done.2.parts_ref = bf16[16,48,128]{2,1,0:T(8,128)(2,1)S(1)} async-done(((bf16[16,48,128]{2,1,0:T(8,128)(2,1)}), bf16[16,48,128]{2,1,0:T(8,128)(2,1)S(1)}, u32[]{:S(2)}, u32[]{:S(2)}) %all-to-all-start.2) | async-done | bytes 196640 | tf_op jit(solution)/shard_map/all_to_all | solution.py:271
  146.9 2.4 %output.1 = bf16[32,1024]{1,0:T(8,128)(2,1)} custom-call(s32[3]{0:T(128)S(1)} %pad_add_fusion.place_ref, s32[1]{0:T(128)S(6)} %sub.7.count_ref, bf16[16,48,128]{2,1,0:T(8,128)(2,1)S(1)} %all-to-all-done.2.parts_ref, bf16[2,2,64,1024]{3,2,1,0:T(8,128)(2,1)} %pad_maximum_fusion.1.refs_0_, bf16[2,2,64,1024]{3,2,1,0:T(8,128)(2,1)S(1)} %collective-permute-done.15.refs_1_, ...), custom_call_target="tpu_custom_call" | custom-call | flops 67108864 | bytes 3145728 | tf_op jit(solution)/shard_map/output/pallas_call | solution.py:259
  (41 shorter events, 0.4 us)
Async XLA Ops:
  3.9 10.5 %copy-start = (bf16[32,1,1024]{2,0,1:T(8,128)(2,1)S(1)}, bf16[32,1,1024]{2,0,1:T(8,128)(2,1)}, u32[]{:S(2)}) copy-start(bf16[32,1,1024]{2,0,1:T(8,128)(2,1)} %param.7) | copy-start | bytes 196612
  3.9 10.5 %copy-start.7 = (bf16[64,1024]{1,0:T(8,128)(2,1)S(1)}, bf16[64,1024]{1,0:T(8,128)(2,1)}, u32[]{:S(2)}) copy-start(bf16[64,1024]{1,0:T(8,128)(2,1)} %param.13) | copy-start | bytes 393220
  3.9 84.2 %all-to-all-start = ((bf16[8,4,384,128]{3,2,1,0:T(8,128)(2,1)}), bf16[8,4,384,128]{3,2,1,0:T(8,128)(2,1)S(1)}, u32[]{:S(2)}, u32[]{:S(2)}) async-start(bf16[8,4,384,128]{3,2,1,0:T(8,128)(2,1)} %bitcast.48), calls=%async_computation | async-start | bytes 6291456 | tf_op jit(solution)/shard_map/all_to_all | solution.py:271
  15.0 15.1 %collective-permute-start = (bf16[96,1024]{1,0:T(8,128)(2,1)}, bf16[96,1024]{1,0:T(8,128)(2,1)S(1)}, u32[]{:S(2)}, u32[]{:S(2)}) collective-permute-start(bf16[96,1024]{1,0:T(8,128)(2,1)} %pad_maximum_fusion.5), channel_id=1, source_target_pairs={{0,256},{256,0},{1,257},{257,1},{2,258},{258,2},{3,259},{259,3},{4... | collective-permute-start | bytes 589832 | tf_op jit(solution)/shard_map/ppermute | solution.py:275
  24.2 39.9 %copy-start.4 = (s32[1,128]{1,0:T(1,128)S(1)}, s32[1,128]{1,0:T(1,128)}, u32[]{:S(2)}) copy-start(s32[1,128]{1,0:T(1,128)} %mask_ref.3) | copy-start | bytes 1540
  30.1 14.5 %copy-start.9 = (bf16[96,1024]{1,0:T(8,128)(2,1)}, bf16[96,1024]{1,0:T(8,128)(2,1)S(1)}, u32[]{:S(2)}) copy-start(bf16[96,1024]{1,0:T(8,128)(2,1)S(1)} %collective-permute-done) | copy-start | bytes 589828
  32.2 20.8 %collective-permute-start.3 = (bf16[8,128,128]{2,1,0:T(8,128)(2,1)S(1)}, bf16[8,128,128]{2,1,0:T(8,128)(2,1)S(1)}, u32[]{:S(2)}, u32[]{:S(2)}) collective-permute-start(bf16[8,128,128]{2,1,0:T(8,128)(2,1)S(1)} %get-tuple-element.44), channel_id=1, source_target_pairs={{0,3},{1,2},{2,1},{3,0},{4,7},{5,6},{6,5},{7,4},{8,11},{9,10},{10,... | collective-permute-start | bytes 786440 | tf_op jit(solution)/shard_map/ppermute | solution.py:294
  37.3 7.2 %collective-permute-start.4 = (bf16[2,32,1024]{2,1,0:T(8,128)(2,1)S(1)}, bf16[2,32,1024]{2,1,0:T(8,128)(2,1)S(1)}, u32[]{:S(2)}, u32[]{:S(2)}) collective-permute-start(bf16[2,32,1024]{2,1,0:T(8,128)(2,1)S(1)} %get-tuple-element.54), channel_id=1, source_target_pairs={{0,32},{32,0},{1,33},{33,1},{2,34},{34,2},{3,35},{35,3},{4,36},{36... | collective-permute-start | bytes 393224 | tf_op jit(solution)/shard_map/ppermute | solution.py:275
  39.3 20.0 %collective-permute-start.2 = (bf16[8,128,128]{2,1,0:T(8,128)(2,1)}, bf16[8,128,128]{2,1,0:T(8,128)(2,1)}, u32[]{:S(2)}, u32[]{:S(2)}) collective-permute-start(bf16[8,128,128]{2,1,0:T(8,128)(2,1)} %get-tuple-element.45), channel_id=1, source_target_pairs={{0,2},{1,3},{2,0},{3,1},{4,6},{5,7},{6,4},{7,5},{8,10},{9,11},{10,... | collective-permute-start | bytes 786440 | tf_op jit(solution)/shard_map/ppermute | solution.py:294
  41.2 18.1 %collective-permute-start.1 = (bf16[8,128,128]{2,1,0:T(8,128)(2,1)}, bf16[8,128,128]{2,1,0:T(8,128)(2,1)}, u32[]{:S(2)}, u32[]{:S(2)}) collective-permute-start(bf16[8,128,128]{2,1,0:T(8,128)(2,1)} %get-tuple-element.46), channel_id=1, source_target_pairs={{0,1},{1,0},{2,3},{3,2},{4,5},{5,4},{6,7},{7,6},{8,9},{9,8},{10,11... | collective-permute-start | bytes 786440 | tf_op jit(solution)/shard_map/ppermute | solution.py:294
  44.6 16.9 %collective-permute-start.5 = (bf16[2,2,32,1024]{3,2,1,0:T(8,128)(2,1)S(1)}, bf16[2,2,32,1024]{3,2,1,0:T(8,128)(2,1)}, u32[]{:S(2)}, u32[]{:S(2)}) collective-permute-start(bf16[2,2,32,1024]{3,2,1,0:T(8,128)(2,1)S(1)} %pad_maximum_fusion.3.refs_0_), channel_id=1, source_target_pairs={{0,64},{64,128},{128,192},{192,0},{1,65},{65,129},{129,193},{193,1... | collective-permute-start | bytes 786440 | tf_op jit(solution)/shard_map/ppermute | solution.py:284
  48.0 14.6 %collective-permute-start.6 = (bf16[2,2,32,1024]{3,2,1,0:T(8,128)(2,1)S(1)}, bf16[2,2,32,1024]{3,2,1,0:T(8,128)(2,1)}, u32[]{:S(2)}, u32[]{:S(2)}) collective-permute-start(bf16[2,2,32,1024]{3,2,1,0:T(8,128)(2,1)S(1)} %pad_maximum_fusion.3.refs_0_), channel_id=1, source_target_pairs={{0,128},{64,192},{128,0},{192,64},{1,129},{65,193},{129,1},{193,65... | collective-permute-start | bytes 786440 | tf_op jit(solution)/shard_map/ppermute | solution.py:284
  53.1 0.7 copy-start.10
  53.8 10.3 %collective-permute-start.7 = (bf16[2,2,32,1024]{3,2,1,0:T(8,128)(2,1)S(1)}, bf16[2,2,32,1024]{3,2,1,0:T(8,128)(2,1)}, u32[]{:S(2)}, u32[]{:S(2)}) collective-permute-start(bf16[2,2,32,1024]{3,2,1,0:T(8,128)(2,1)S(1)} %pad_maximum_fusion.3.refs_0_), channel_id=1, source_target_pairs={{0,192},{64,0},{128,64},{192,128},{1,193},{65,1},{129,65},{193,129... | collective-permute-start | bytes 786440 | tf_op jit(solution)/shard_map/ppermute | solution.py:284
  58.5 18.6 %copy-start.8 = (bf16[64,1024]{1,0:T(8,128)(2,1)S(1)}, bf16[64,1024]{1,0:T(8,128)(2,1)}, u32[]{:S(2)}) copy-start(bf16[64,1024]{1,0:T(8,128)(2,1)} %param.13) | copy-start | bytes 393220
  58.5 18.6 %slice-start = ((bf16[96,1024]{1,0:T(8,128)(2,1)}), bf16[64,1024]{1,0:T(8,128)(2,1)S(1)}, s32[]{:S(2)}) async-start(bf16[96,1024]{1,0:T(8,128)(2,1)} %copy-done.9), calls=%async_computation.3 | async-start | bytes 262144 | tf_op jit(solution)/shard_map/slice | solution.py:299
  64.1 1.0 copy-start.3
  67.3 13.3 %copy-start.5 = (bf16[512,128]{1,0:T(8,128)(2,1)}, bf16[512,128]{1,0:T(8,128)(2,1)S(1)}, u32[]{:S(2)}) copy-start(bf16[512,128]{1,0:T(8,128)(2,1)S(1)} %get-tuple-element.35.query_ref) | copy-start | bytes 393220
  67.3 12.6 %collective-permute-start.10 = (bf16[272,128]{1,0:T(8,128)(2,1)S(1)}, bf16[272,128]{1,0:T(8,128)(2,1)S(1)}, u32[]{:S(2)}, u32[]{:S(2)}) collective-permute-start(bf16[272,128]{1,0:T(8,128)(2,1)S(1)} %get-tuple-element.32), channel_id=1, source_target_pairs={{0,3},{1,2},{2,1},{3,0},{4,7},{5,6},{6,5},{7,4},{8,11},{9,10},{10,... | collective-permute-start | bytes 208904 | tf_op jit(solution)/shard_map/ppermute | solution.py:294
  71.8 8.1 %collective-permute-start.9 = (bf16[272,128]{1,0:T(8,128)(2,1)S(1)}, bf16[272,128]{1,0:T(8,128)(2,1)S(1)}, u32[]{:S(2)}, u32[]{:S(2)}) collective-permute-start(bf16[272,128]{1,0:T(8,128)(2,1)S(1)} %get-tuple-element.32), channel_id=1, source_target_pairs={{0,2},{1,3},{2,0},{3,1},{4,6},{5,7},{6,4},{7,5},{8,10},{9,11},{10,... | collective-permute-start | bytes 208904 | tf_op jit(solution)/shard_map/ppermute | solution.py:294
  74.3 6.2 %collective-permute-start.8 = (bf16[272,128]{1,0:T(8,128)(2,1)S(1)}, bf16[272,128]{1,0:T(8,128)(2,1)S(1)}, u32[]{:S(2)}, u32[]{:S(2)}) collective-permute-start(bf16[272,128]{1,0:T(8,128)(2,1)S(1)} %get-tuple-element.32), channel_id=1, source_target_pairs={{0,1},{1,0},{2,3},{3,2},{4,5},{5,4},{6,7},{7,6},{8,9},{9,8},{10,11... | collective-permute-start | bytes 208904 | tf_op jit(solution)/shard_map/ppermute | solution.py:294
  77.9 3.9 %collective-permute-start.11 = (bf16[2,64,1024]{2,1,0:T(8,128)(2,1)}, bf16[2,64,1024]{2,1,0:T(8,128)(2,1)}, u32[]{:S(2)}, u32[]{:S(2)}) collective-permute-start(bf16[2,64,1024]{2,1,0:T(8,128)(2,1)} %get-tuple-element.52), channel_id=1, source_target_pairs={{0,32},{32,0},{1,33},{33,1},{2,34},{34,2},{3,35},{35,3},{4,36},{36... | collective-permute-start | bytes 786440 | tf_op jit(solution)/shard_map/ppermute | solution.py:275
  80.6 0.7 copy-start.1
  88.1 35.4 %all-to-all-start.1 = ((bf16[8,4,128,128]{3,2,1,0:T(8,128)(2,1)}), bf16[8,4,128,128]{3,2,1,0:T(8,128)(2,1)}, u32[]{:S(2)}, u32[]{:S(2)}) async-start(bf16[8,4,128,128]{3,2,1,0:T(8,128)(2,1)} %pad_maximum_fusion), calls=%async_computation.1 | async-start | bytes 2097152 | tf_op jit(solution)/shard_map/all_to_all | solution.py:271
  92.4 1.0 copy-start.2
  93.3 30.2 %copy-start.6 = (bf16[512,128]{1,0:T(8,128)(2,1)S(1)}, bf16[512,128]{1,0:T(8,128)(2,1)}, u32[]{:S(2)}) copy-start(bf16[512,128]{1,0:T(8,128)(2,1)} %copy-done.5) | copy-start | bytes 393220
  102.2 17.3 %collective-permute-start.12 = (f32[256,128]{1,0:T(8,128)S(1)}, f32[256,128]{1,0:T(8,128)S(1)}, u32[]{:S(2)}, u32[]{:S(2)}) collective-permute-start(f32[256,128]{1,0:T(8,128)S(1)} %get-tuple-element.49), channel_id=1, source_target_pairs={{0,1},{1,0},{2,3},{3,2},{4,5},{5,4},{6,7},{7,6},{8,9},{9,8},{10,11... | collective-permute-start | bytes 393224 | tf_op jit(solution)/shard_map/ppermute | solution.py:294
  104.6 18.9 %collective-permute-start.13 = (f32[256,128]{1,0:T(8,128)S(1)}, f32[256,128]{1,0:T(8,128)S(1)}, u32[]{:S(2)}, u32[]{:S(2)}) collective-permute-start(f32[256,128]{1,0:T(8,128)S(1)} %get-tuple-element.48), channel_id=1, source_target_pairs={{0,2},{1,3},{2,0},{3,1},{4,6},{5,7},{6,4},{7,5},{8,10},{9,11},{10,... | collective-permute-start | bytes 393224 | tf_op jit(solution)/shard_map/ppermute | solution.py:294
  109.1 14.4 %collective-permute-start.14 = (f32[256,128]{1,0:T(8,128)S(1)}, f32[256,128]{1,0:T(8,128)S(1)}, u32[]{:S(2)}, u32[]{:S(2)}) collective-permute-start(f32[256,128]{1,0:T(8,128)S(1)} %get-tuple-element.47), channel_id=1, source_target_pairs={{0,3},{1,2},{2,1},{3,0},{4,7},{5,6},{6,5},{7,4},{8,11},{9,10},{10,... | collective-permute-start | bytes 393224 | tf_op jit(solution)/shard_map/ppermute | solution.py:294
  111.4 22.1 %collective-permute-start.15 = (bf16[2,2,64,1024]{3,2,1,0:T(8,128)(2,1)}, bf16[2,2,64,1024]{3,2,1,0:T(8,128)(2,1)S(1)}, u32[]{:S(2)}, u32[]{:S(2)}) collective-permute-start(bf16[2,2,64,1024]{3,2,1,0:T(8,128)(2,1)} %pad_maximum_fusion.1.refs_0_), channel_id=1, source_target_pairs={{0,64},{64,128},{128,192},{192,0},{1,65},{65,129},{129,193},{193,1... | collective-permute-start | bytes 1572872 | tf_op jit(solution)/shard_map/ppermute | solution.py:284
  114.8 25.7 %collective-permute-start.16 = (bf16[2,2,64,1024]{3,2,1,0:T(8,128)(2,1)}, bf16[2,2,64,1024]{3,2,1,0:T(8,128)(2,1)S(1)}, u32[]{:S(2)}, u32[]{:S(2)}) collective-permute-start(bf16[2,2,64,1024]{3,2,1,0:T(8,128)(2,1)} %pad_maximum_fusion.1.refs_0_), channel_id=1, source_target_pairs={{0,128},{64,192},{128,0},{192,64},{1,129},{65,193},{129,1},{193,65... | collective-permute-start | bytes 1572872 | tf_op jit(solution)/shard_map/ppermute | solution.py:284
  119.5 23.1 %collective-permute-start.17 = (bf16[2,2,64,1024]{3,2,1,0:T(8,128)(2,1)}, bf16[2,2,64,1024]{3,2,1,0:T(8,128)(2,1)S(1)}, u32[]{:S(2)}, u32[]{:S(2)}) collective-permute-start(bf16[2,2,64,1024]{3,2,1,0:T(8,128)(2,1)} %pad_maximum_fusion.1.refs_0_), channel_id=1, source_target_pairs={{0,192},{64,0},{128,64},{192,128},{1,193},{65,1},{129,65},{193,129... | collective-permute-start | bytes 1572872 | tf_op jit(solution)/shard_map/ppermute | solution.py:284
  126.7 20.2 %all-to-all-start.2 = ((bf16[16,48,128]{2,1,0:T(8,128)(2,1)}), bf16[16,48,128]{2,1,0:T(8,128)(2,1)S(1)}, u32[]{:S(2)}, u32[]{:S(2)}) async-start(bf16[16,48,128]{2,1,0:T(8,128)(2,1)} %attend_last.1), calls=%async_computation.2 | async-start | bytes 393216 | tf_op jit(solution)/shard_map/all_to_all | solution.py:271
